TPU v7x, 256 devices: a whole 4x4x8 slice. The times are simulated.
256 devices in a mesh: dom: 128 (over x, z, y), edge: 2 (over core).
Axes of the slice: x: 4, y: 4, z: 8, core: 2. Of those that a mesh axis runs over, the one named last changes fastest.
Arguments:
- node_feats: bfloat16 [131072, 128], P('dom'), may hold values from -6 to 6
- hub_feats: bfloat16 [4096, 128], P('dom'), may hold values from -6 to 6
- w_self: bfloat16 [128, 128], replicated, may hold values from -0.5 to 0.5
- w_neigh: bfloat16 [128, 128], replicated, may hold values from -0.75 to 0.75
- bias: float32 [128], replicated, may hold values from -4 to 4
- cotangent: bfloat16 [131072, 128], P('dom'), may hold values from -6 to 6
- send_count: int32 [128, 128], P('dom'), may hold values from 0 to 128, as said below
- send_rows: int32 [128, 128, 128], P('dom'), may hold values from 0 to 1023, as said below
- edge_src: int32 [128, 2, 8192], P('dom', 'edge'), may hold values from 0 to 21503, as said below
- edge_dst: int32 [128, 2, 8192], P('dom', 'edge'), may hold values from 0 to 1023
- edge_count: int32 [128, 2], P('dom', 'edge'), may hold values from 2048 to 8192, as said below
Outputs:
- layer_out: bfloat16 [131072, 128], P('dom')
- grad_feats: float32 [131072, 128], P('dom')
- grad_hubs: float32 [4096, 128], P('dom')
- grad_self: float32 [128, 128], replicated
- grad_neigh: float32 [128, 128], replicated
- grad_bias: float32 [128], replicated
Inputs may be any that keep to these rules, and one draw needn't show every extreme that they name: send_count[p, p] is 0; otherwise at least 32; every partition p sends exactly 128 rows to partition (p + 1) mod 128. `send_rows`: rows of the sending partition; rows may repeat within a block. `edge_src`: every slot names a row of the source table: an own node, a live slot of a block from another partition, or a hub; slots at or beyond edge_count are ignored. `edge_count`: in every partition one of the two halves is full with 8192 live slots.
All inputs are finite; a program needn't handle non-finite values.
Results may differ from a plain program's by a relative error of at most 0.008.
Values may be sent and summed in bfloat16 or wider, within the bound.
No kernel may reach another device: no remote copies, remote signals or barrier semaphores. Data moves between devices by JAX's collectives and lax.ppermute only.
A program may use at most 128 MiB of HBM per device.

v0:
```python
import jax
import jax.numpy as jnp
from jax import lax
from jax.sharding import PartitionSpec as P


def silu_slope(value):
    sig = jax.nn.sigmoid(value)
    return sig * (1.0 + value * (1.0 - sig))


def dense_part(feat_rows, neigh_sum, degree, grad_out, w_self, w_neigh, bias):
    divisor = jnp.maximum(degree, 1.0)[:, None]
    aggregate = (neigh_sum / divisor).astype(jnp.bfloat16)
    preact = (
        jnp.dot(feat_rows, w_self, preferred_element_type=jnp.float32)
        + jnp.dot(aggregate, w_neigh, preferred_element_type=jnp.float32)
        + bias
    )
    layer_out = jax.nn.silu(preact).astype(jnp.bfloat16)
    grad_pre = (grad_out.astype(jnp.float32) * silu_slope(preact)).astype(jnp.bfloat16)
    dims = (((0,), (0,)), ((), ()))
    grad_self = lax.dot_general(feat_rows, grad_pre, dims, preferred_element_type=jnp.float32)
    grad_neigh = lax.dot_general(aggregate, grad_pre, dims, preferred_element_type=jnp.float32)
    grad_bias = jnp.sum(grad_pre.astype(jnp.float32), axis=0)
    grad_sum = (jnp.dot(grad_pre, w_neigh.T, preferred_element_type=jnp.float32) / divisor).astype(
        jnp.bfloat16
    )
    return (layer_out, grad_pre, grad_sum, grad_self, grad_neigh, grad_bias)


def body(
    node_feats,
    hub_feats,
    w_self,
    w_neigh,
    bias,
    cotangent,
    send_count,
    send_rows,
    edge_src,
    edge_dst,
    edge_count,
):
    num_dom = lax.axis_size("dom")
    local_rows, width = node_feats.shape
    block_rows = send_rows.shape[2]
    hub_all = lax.all_gather(hub_feats, "dom", axis=0, tiled=True)
    send_idx = send_rows[0]
    slot_mask = jnp.arange(block_rows, dtype=jnp.int32)[None, :] < send_count[0][:, None]
    outgoing = jnp.where(slot_mask[:, :, None], node_feats[send_idx], jnp.zeros((), jnp.bfloat16))
    received = lax.all_to_all(outgoing, "dom", split_axis=0, concat_axis=0, tiled=True)
    source_table = jnp.concatenate(
        [node_feats, received.reshape(num_dom * block_rows, width), hub_all], axis=0
    )
    table_len = source_table.shape[0]
    edge_from = edge_src.reshape(-1)
    edge_to = edge_dst.reshape(-1)
    edge_total = edge_from.shape[0]
    live_mask = (jnp.arange(edge_total, dtype=jnp.int32) < edge_count.reshape(())).astype(
        jnp.float32
    )
    block_len = min(4096, edge_total)
    blocks = edge_total // block_len
    from_blocks = edge_from.reshape(blocks, block_len)
    to_blocks = edge_to.reshape(blocks, block_len)
    mask_blocks = live_mask.reshape(blocks, block_len)

    def gather_block(carry, inputs):
        from_part, to_part, mask_part = inputs
        values = source_table[from_part].astype(jnp.float32) * mask_part[:, None]
        return (carry.at[to_part].add(values), None)

    neigh_part, _ = lax.scan(
        gather_block,
        jnp.zeros((local_rows, width), jnp.float32),
        (from_blocks, to_blocks, mask_blocks),
    )
    degree_part = jax.ops.segment_sum(live_mask, edge_to, local_rows)
    neigh_sum, degree = lax.psum((neigh_part, degree_part), "edge")
    layer_out, grad_pre, grad_sum, grad_self, grad_neigh, grad_bias = dense_part(
        node_feats, neigh_sum, degree, cotangent, w_self, w_neigh, bias
    )
    grad_self, grad_neigh, grad_bias = lax.psum((grad_self, grad_neigh, grad_bias), "dom")
    grad_input = jnp.dot(grad_pre, w_self.T, preferred_element_type=jnp.float32)

    def spread_block(carry, inputs):
        from_part, to_part, mask_part = inputs
        values = grad_sum[to_part].astype(jnp.float32) * mask_part[:, None]
        return (carry.at[from_part].add(values), None)

    table_grad, _ = lax.scan(
        spread_block,
        jnp.zeros((table_len, width), jnp.float32),
        (from_blocks, to_blocks, mask_blocks),
    )
    hub_start = local_rows + num_dom * block_rows
    bound_grad = table_grad[local_rows:hub_start].reshape(num_dom, block_rows, width)
    hub_grad = table_grad[hub_start:]
    bound_share = lax.psum_scatter(
        bound_grad.astype(jnp.bfloat16), "edge", scatter_dimension=1, tiled=True
    )
    bound_full = lax.all_gather(bound_share, "edge", axis=1, tiled=True)
    returned = lax.all_to_all(bound_full, "dom", split_axis=0, concat_axis=0, tiled=True)
    returned = returned.astype(jnp.float32) * slot_mask[:, :, None].astype(jnp.float32)
    extra = jax.ops.segment_sum(returned.reshape(-1, width), send_idx.reshape(-1), local_rows)
    node_part = table_grad[:local_rows]
    hub_rows = hub_feats.shape[0]
    node_total = lax.psum(node_part.astype(jnp.bfloat16), "edge").astype(jnp.float32)
    hub_total = lax.psum(hub_grad, ("dom", "edge"))
    grad_hubs = lax.dynamic_slice_in_dim(hub_total, lax.axis_index("dom") * hub_rows, hub_rows, 0)
    grad_feats = grad_input + node_total + extra
    return (layer_out, grad_feats, grad_hubs, grad_self, grad_neigh, grad_bias)


def solution(mesh):
    placed = (
        P("dom", None),
        P("dom", None),
        P(),
        P(),
        P(),
        P("dom", None),
        P("dom", None),
        P("dom", None, None),
        P("dom", "edge", None),
        P("dom", "edge", None),
        P("dom", "edge"),
    )
    return jax.shard_map(
        body,
        mesh=mesh,
        in_specs=placed,
        out_specs=(P("dom", None), P("dom", None), P("dom", None), P(), P(), P()),
        check_vma=False,
    )
```

profile of v0, /device:TPU:1, one launch (start us, length us, event | category | flops | bytes accessed | tf_op | source)
XLA Modules:
  0.0 1162.9 jit_solution(18082536915977000689)
XLA Ops:
  8.8 56.3 %gather_fusion = bf16[16384,128]{1,0:T(8,128)(2,1)} fusion(bf16[1024,128]{1,0:T(8,128)(2,1)} %param.15, s32[16384]{0:T(1024)S(1)} %fusion.13), kind=kCustom, calls=%fused_computation.2 | custom fusion | bytes 8454144 | tf_op jit(solution)/shard_map/gather | solution.py:51
  65.1 7.7 broadcast_select_fusion
  72.8 17.0 %all-to-all-start = ((bf16[128,128,128]{2,1,0:T(8,128)(2,1)}), bf16[128,128,128]{2,1,0:T(8,128)(2,1)}, u32[]{:S(2)}, u32[]{:S(2)}) async-start(bf16[128,128,128]{2,1,0:T(8,128)(2,1)} %broadcast_select_fusion), calls=%async_computation | async-start | bytes 8388608 | tf_op jit(solution)/shard_map/all_to_all | solution.py:52
  93.3 109.8 %all-gather.3.cloned.1.call-done = bf16[4096,128]{1,0:T(8,128)(2,1)} async-done(((bf16[32,128]{1,0:T(8,128)(2,1)}), bf16[4096,128]{1,0:T(8,128)(2,1)}) %all-gather.3.cloned.1.call-update) | async-done | bytes 1048592 | tf_op jit(solution)/shard_map/all_gather | solution.py:48
  203.1 7.8 pad_maximum_fusion
  211.0 99.0 %while.20 = (s32[]{:T(128)}, f32[1024,128]{1,0:T(8,128)S(1)}, s32[2,4096]{1,0:T(2,128)S(1)}, s32[2,4096]{1,0:T(2,128)S(1)}, bf16[21504,128]{1,0:T(8,128)(2,1)}, /*index=5*/f32[2,4096]{1,0:T(2,128)S(1)}, s32[]{:T(128)}) while((s32[]{:T(128)}, f32[1024,128]{1,0:T(8,128)S(1)}, s32[2,4096]{1,0:T(2,128)S(1)}, s32[2,4096]{1,0:T(2,128)S(1)}, ...), condition=%wide.region_2.3_spmd, body=%wide.region_0.2_spmd.sunk | while | flops 1601538 | bytes 6193245 | solution.py:74
  211.1 49.4 %scatter_custom_fusion.12 = f32[1024,128]{1,0:T(8,128)S(1)} fusion(f32[1024,128]{1,0:T(8,128)S(1)} %get-tuple-element.209, s32[4096]{0:T(1024)S(1)} %bitcast.67, f32[4096]{0:T(1024)S(1)} %bitcast.63, bf16[21504,128]{1,0:T(8,128)(2,1)} %get-tuple-element.219, s32[4096]{0:T(1024)S(1)} %broadcast_clamp_fusion.4), kind=kCustom, calls=%fused_computation.7.clone.1 | custom fusion | flops 1572864 | bytes 6062080 | tf_op jit(solution)/shard_map/while/body/eval_jaxpr/scatter-add | solution.py:72
  260.6 49.4 %scatter_custom_fusion.12 = f32[1024,128]{1,0:T(8,128)S(1)} fusion(f32[1024,128]{1,0:T(8,128)S(1)} %get-tuple-element.209, s32[4096]{0:T(1024)S(1)} %bitcast.67, f32[4096]{0:T(1024)S(1)} %bitcast.63, bf16[21504,128]{1,0:T(8,128)(2,1)} %get-tuple-element.219, s32[4096]{0:T(1024)S(1)} %broadcast_clamp_fusion.4), kind=kCustom, calls=%fused_computation.7.clone.1 | custom fusion | flops 1572864 | bytes 6062080 | tf_op jit(solution)/shard_map/while/body/eval_jaxpr/scatter-add | solution.py:72
  310.9 57.0 %scatter_custom_fusion.2 = f32[1024]{0:T(1024)S(1)} fusion(s32[8192]{0:T(1024)S(1)} %bitcast.70, f32[8192]{0:T(1024)S(1)} %fusion.14, f32[]{:T(128)} %constant.30.clone.1), kind=kCustom, calls=%fused_computation.47 | custom fusion | flops 8192 | bytes 4100 | tf_op jit(solution)/shard_map/scatter-add | solution.py:79
  367.9 6.7 psum.50
  377.6 4.4 broadcast_in_dim.22
  382.0 90.1 %while.21 = (s32[]{:T(128)}, f32[21504,128]{1,0:T(8,128)}, s32[2,4096]{1,0:T(2,128)S(1)}, s32[2,4096]{1,0:T(2,128)S(1)}, bf16[1024,128]{1,0:T(8,128)(2,1)S(1)}, /*index=5*/f32[2,4096]{1,0:T(2,128)S(1)}, s32[]{:T(128)}) while((s32[]{:T(128)}, f32[21504,128]{1,0:T(8,128)}, s32[2,4096]{1,0:T(2,128)S(1)}, s32[2,4096]{1,0:T(2,128)S(1)}, ...), condition=%wide.region_8.9_spmd, body=%wide.region_6.8_spmd.sunk | while | flops 1601538 | bytes 11436125 | solution.py:92
  382.1 45.0 %scatter_custom_fusion.14 = f32[21504,128]{1,0:T(8,128)} fusion(f32[21504,128]{1,0:T(8,128)} %get-tuple-element.230, s32[4096]{0:T(1024)S(1)} %bitcast.68, f32[4096]{0:T(1024)S(1)} %bitcast.64, bf16[1024,128]{1,0:T(8,128)(2,1)S(1)} %get-tuple-element.240, s32[4096]{0:T(1024)S(1)} %broadcast_clamp_fusion.5), kind=kCustom, calls=%fused_computation.16.clone.1 | custom fusion | flops 1572864 | bytes 11304960 | tf_op jit(solution)/shard_map/while/body/eval_jaxpr/scatter-add | solution.py:90
  427.2 45.0 %scatter_custom_fusion.14 = f32[21504,128]{1,0:T(8,128)} fusion(f32[21504,128]{1,0:T(8,128)} %get-tuple-element.230, s32[4096]{0:T(1024)S(1)} %bitcast.68, f32[4096]{0:T(1024)S(1)} %bitcast.64, bf16[1024,128]{1,0:T(8,128)(2,1)S(1)} %get-tuple-element.240, s32[4096]{0:T(1024)S(1)} %broadcast_clamp_fusion.5), kind=kCustom, calls=%fused_computation.16.clone.1 | custom fusion | flops 1572864 | bytes 11304960 | tf_op jit(solution)/shard_map/while/body/eval_jaxpr/scatter-add | solution.py:90
  472.2 4.7 convert.4
  476.9 2.2 slice.21
  480.5 16.8 %reduce-scatter.2.cloned.1.call-done = bf16[128,64,128]{2,1,0:T(8,128)(2,1)} async-done(((bf16[128,128,128]{2,1,0:T(8,128)(2,1)}), bf16[128,64,128]{2,1,0:T(8,128)(2,1)}) %reduce-scatter.2.cloned.1.call-update) | async-done | bytes 2097168 | tf_op jit(solution)/shard_map/reduce_scatter | solution.py:100
  497.3 22.2 %all-gather.5.cloned.1.call-done = bf16[128,128,128]{2,1,0:T(8,128)(2,1)} async-done(((bf16[128,64,128]{2,1,0:T(8,128)(2,1)}), bf16[128,128,128]{2,1,0:T(8,128)(2,1)}) %all-gather.5.cloned.1.call-update) | async-done | bytes 4194320 | tf_op jit(solution)/shard_map/all_gather | solution.py:103
  519.6 14.1 %all-to-all-start.1 = ((bf16[128,128,128]{2,1,0:T(8,128)(2,1)}), bf16[128,128,128]{2,1,0:T(8,128)(2,1)}, u32[]{:S(2)}, u32[]{:S(2)}) async-start(bf16[128,128,128]{2,1,0:T(8,128)(2,1)} %all-gather.5.cloned.1.call-done), calls=%async_computation.2 | async-start | bytes 8388608 | tf_op jit(solution)/shard_map/all_to_all | solution.py:104
  537.4 3.1 slice.13
  540.5 366.6 %psum.55 = f32[128]{0:T(128)} all-reduce(f32[128]{0:T(128)S(1)} %get-tuple-element.110), channel_id=1, replica_groups=mesh['dom'=128,'edge'=2] {'dom'}, use_global_device_ids=true, to_apply=%region_16.17 | all-reduce | flops 128 | bytes 1024 | tf_op jit(solution)/shard_map/psum | solution.py:84
  909.8 148.6 %all-reduce.10.cloned.1.call-done = f32[4096,128]{1,0:T(8,128)} async-done(((f32[4096,128]{1,0:T(8,128)}), f32[4096,128]{1,0:T(8,128)}) %all-reduce.10.cloned.1.call-update) | async-done | bytes 2097168 | tf_op jit(solution)/shard_map/psum | solution.py:110
  1059.8 7.6 convert_multiply_fusion
  1067.4 87.8 %scatter_fusion = f32[1024,128]{1,0:T(8,128)S(1)} fusion(f32[1024,128]{1,0:T(8,128)S(1)} %convolution_add_fusion, s32[16384]{0:T(1024)S(1)} %bitcast.69, f32[16384,128]{1,0:T(8,128)} %bitcast.60), kind=kCustom, calls=%fused_computation.6 | custom fusion | flops 2097152 | bytes 25231360 | tf_op jit(solution)/shard_map/scatter-add | solution.py:106
  (79 shorter events, 18.5 us)
Async XLA Ops:
  7.2 369.0 %copy-start = (bf16[128,128]{1,0:T(8,128)(2,1)S(1)}, bf16[128,128]{1,0:T(8,128)(2,1)}, u32[]{:S(2)}) copy-start(bf16[128,128]{1,0:T(8,128)(2,1)} %param.18) | copy-start | bytes 98308
  72.8 19.0 %copy-start.9 = (s32[1,1,8192]{2,1,0:T(1,128)S(1)}, s32[1,1,8192]{2,1,0:T(1,128)}, u32[]{:S(2)}) copy-start(s32[1,1,8192]{2,1,0:T(1,128)} %param.23) | copy-start | bytes 98308
  72.8 19.7 %copy-start.10 = (s32[1,1,8192]{2,1,0:T(1,128)S(1)}, s32[1,1,8192]{2,1,0:T(1,128)}, u32[]{:S(2)}) copy-start(s32[1,1,8192]{2,1,0:T(1,128)} %param.24) | copy-start | bytes 98308
  72.8 130.3 %copy-start.3 = (bf16[1024,128]{1,0:T(8,128)(2,1)S(1)}, bf16[1024,128]{1,0:T(8,128)(2,1)}, u32[]{:S(2)}) copy-start(bf16[1024,128]{1,0:T(8,128)(2,1)} %param.15) | copy-start | bytes 786436
  72.8 130.3 %all-to-all-start = ((bf16[128,128,128]{2,1,0:T(8,128)(2,1)}), bf16[128,128,128]{2,1,0:T(8,128)(2,1)}, u32[]{:S(2)}, u32[]{:S(2)}) async-start(bf16[128,128,128]{2,1,0:T(8,128)(2,1)} %broadcast_select_fusion), calls=%async_computation | async-start | bytes 8388608 | tf_op jit(solution)/shard_map/all_to_all | solution.py:52
  89.8 113.3 %all-gather.3.cloned.1.call-start = ((), (), s32[]{:S(2)}) async-start(), calls=%async_computation.3 | async-start | bytes 1056768 | tf_op jit(solution)/shard_map/all_gather | solution.py:48
  90.6 284.3 %all-reduce.6.cloned.1.call-start = ((), (), s32[]{:S(2)}) async-start(), calls=%async_computation.4 | async-start | bytes 1048576 | tf_op jit(solution)/shard_map/psum | solution.py:80
  211.0 163.7 %copy-start.7 = (bf16[128,128]{1,0:T(8,128)(2,1)S(1)}, bf16[128,128]{1,0:T(8,128)(2,1)}, u32[]{:S(2)}) copy-start(bf16[128,128]{1,0:T(8,128)(2,1)} %param.17) | copy-start | bytes 98308
  211.0 165.2 %copy-start.11 = (bf16[1024,128]{1,0:T(8,128)(2,1)S(1)}, bf16[1024,128]{1,0:T(8,128)(2,1)}, u32[]{:S(2)}) copy-start(bf16[1024,128]{1,0:T(8,128)(2,1)} %param.20) | copy-start | bytes 786436
  211.0 165.2 %copy-start.12 = (f32[128]{0:T(128)S(1)}, f32[128]{0:T(128)}, u32[]{:S(2)}) copy-start(f32[128]{0:T(128)} %param.19) | copy-start | bytes 1540
  310.1 0.8 copy-start.5
  310.9 186.4 %reduce-scatter.2.cloned.1.call-start = ((), (), s32[]{:S(2)}) async-start(), calls=%async_computation.6 | async-start | bytes 6291456 | tf_op jit(solution)/shard_map/reduce_scatter | solution.py:100
  476.9 3.6 copy-start.4
  480.5 39.1 %all-gather.5.cloned.1.call-start = ((), (), s32[]{:S(2)}) async-start(), calls=%async_computation.7 | async-start | bytes 6291456 | tf_op jit(solution)/shard_map/all_gather | solution.py:103
  519.6 540.2 %all-to-all-start.1 = ((bf16[128,128,128]{2,1,0:T(8,128)(2,1)}), bf16[128,128,128]{2,1,0:T(8,128)(2,1)}, u32[]{:S(2)}, u32[]{:S(2)}) async-start(bf16[128,128,128]{2,1,0:T(8,128)(2,1)} %all-gather.5.cloned.1.call-done), calls=%async_computation.2 | async-start | bytes 8388608 | tf_op jit(solution)/shard_map/all_to_all | solution.py:104
  533.7 373.4 %all-reduce.12.cloned.1.call-start = ((), (), s32[]{:S(2)}) async-start(), calls=%async_computation.9 | async-start | bytes 262144 | tf_op jit(solution)/shard_map/psum | solution.py:84
  535.6 373.1 %all-reduce.8.cloned.1.call-start = ((), (), s32[]{:S(2)}) async-start(), calls=%async_computation.5 | async-start | bytes 524288 | tf_op jit(solution)/shard_map/psum | solution.py:109
  537.3 521.2 %all-reduce.10.cloned.1.call-start = ((), (), s32[]{:S(2)}) async-start(), calls=%async_computation.8 | async-start | bytes 4194304 | tf_op jit(solution)/shard_map/psum | solution.py:110
  1059.8 7.6 copy-start.6
  1067.4 87.9 %copy-start.8 = (f32[128,128]{1,0:T(8,128)S(1)}, f32[128,128]{1,0:T(8,128)}, u32[]{:S(2)}) copy-start(f32[128,128]{1,0:T(8,128)} %get-tuple-element.247) | copy-start | bytes 196612
  1067.4 88.7 %copy-start.1 = (bf16[128,128]{1,0:T(8,128)(2,1)S(1)}, bf16[128,128]{1,0:T(8,128)(2,1)}, u32[]{:S(2)}) copy-start(bf16[128,128]{1,0:T(8,128)(2,1)} %param.18) | copy-start | bytes 98308
  1155.2 0.8 copy-start.2
Sparse Core Ops, SparseCore 0:
  94.1 108.9 all-gather.2
  311.0 33.2 all-reduce.5
  480.6 16.6 reduce-scatter.1
  499.0 20.5 all-gather.4
  540.4 217.2 all-reduce.11
  760.8 31.3 all-reduce.7
  797.6 260.7 all-reduce.9
where the time goes:
time: 1160 us
  blocking collectives  373 us (32%)
  other arithmetic  366 us (32%)
  waiting for transfers between devices  298 us (26%)
  local copies, waits for them, and re-layouts  74.2 us (6%)
  starting transfers between devices  31.4 us (3%)
  between operations  15 us (1%)
    psum x1, blocking collectives, body(): lax.psum((grad_self, grad_neigh, grad_bias), 'dom')  367 us
    psum x1, waiting for transfers between devices, body(): hub_total = lax.psum(hub_grad, ('dom', 'edge'))  149 us
    all_gather x1, waiting for transfers between devices, body(): hub_all = lax.all_gather(hub_feats, 'dom', axis=0, tiled=True)  110 us
    scatter-add x2, other arithmetic, gather_block(): return (carry.at[to_part].add(values), None)  98.8 us
    scatter-add x2, other arithmetic, spread_block(): return (carry.at[from_part].add(values), None)  90 us
    scatter-add x1, other arithmetic, body(): jax.ops.segment_sum(returned.reshape(-1, width), send_idx.reshape(-1), lo...  87.8 us
    scatter-add x1, other arithmetic, body(): degree_part = jax.ops.segment_sum(live_mask, edge_to, local_rows)  57 us
    gather x1, local copies, waits for them, and re-layouts, body(): node_feats[send_idx]  56.3 us
  transfers between devices with their start and end apart: 9, of which 4 were waited for; matrix products, arithmetic and copies ran while one was open for 6% of the time, Pallas kernels for 0%

commit v1 on v0

v1 whole, which is shorter than its diff:
```python
import functools

import jax
import jax.numpy as jnp
from jax import lax
from jax.experimental import pallas as pl
from jax.experimental.pallas import tpu as pltpu
from jax.sharding import PartitionSpec as P

F32 = jnp.float32
BF16 = jnp.bfloat16
VMEM = pltpu.VMEM
SMEM = pltpu.SMEM
SWAP = [(0, 1), (1, 0)]
CHUNK = 256
DST_BITS = 10
PAD = 1 << 30
DEAD = 1 << 26
HALF_BIT = 24


def params(mib=40):
    return pltpu.CompilerParams(vmem_limit_bytes=mib * 1024 * 1024)


def vspec():
    return pl.BlockSpec(memory_space=VMEM)


def sspec():
    return pl.BlockSpec(memory_space=SMEM)


def columns_of(row):
    parts = []
    for at in range(0, row.shape[1], 128):
        parts.append(jnp.broadcast_to(row[:, at : at + 128], (128, 128)).T)
    return jnp.concatenate(parts, axis=0)


def onehot_of_columns(col, width):
    lane = lax.broadcasted_iota(jnp.int32, col.shape, 1)
    parts = [
        jnp.where(col == lane + at, 1.0, 0.0).astype(BF16) for at in range(0, width, 128)
    ]
    return jnp.concatenate(parts, axis=1)


def onehot_of_rows(row, height):
    sub = lax.broadcasted_iota(jnp.int32, (height, row.shape[1]), 0)
    return jnp.where(sub == row, 1.0, 0.0).astype(BF16)


def dot(a, b):
    return jnp.dot(a, b, preferred_element_type=F32)


def dot_nt(a, b):
    return lax.dot_general(a, b, (((1,), (1,)), ((), ())), preferred_element_type=F32)


def dot_tn(a, b):
    return lax.dot_general(a, b, (((0,), (0,)), ((), ())), preferred_element_type=F32)


def outgoing_kernel(slots, idx_ref, feat_ref, hub_ref, out_ref):
    step = pl.program_id(0)
    peers = out_ref.shape[0]
    hubs = hub_ref.shape[0]
    rows = feat_ref.shape[0]
    for pair in range(peers // 4):
        at = step * (peers // 2) + pair * 2
        idx = [idx_ref[pl.ds(at + k, 1), :] for k in range(2)]
        hot = onehot_of_columns(columns_of(jnp.concatenate(idx, axis=1)), rows)
        picked = dot(hot, feat_ref[...]).astype(BF16)
        for k in range(4):
            out_ref[pair * 4 + k, :slots, :] = picked[k * slots : (k + 1) * slots]
            out_ref[pair * 4 + k, slots:, :] = hub_ref[...]


def outgoing(idx, feats, hub_rows, slots, step_peers=8):
    peers = idx.shape[0] * idx.shape[1] // slots
    hubs, width = hub_rows.shape
    return pl.pallas_call(
        functools.partial(outgoing_kernel, slots),
        grid=(peers // step_peers,),
        in_specs=[
            pl.BlockSpec(idx.shape, lambda i: (0, 0)),
            pl.BlockSpec(feats.shape, lambda i: (0, 0)),
            pl.BlockSpec(hub_rows.shape, lambda i: (0, 0)),
        ],
        out_specs=pl.BlockSpec((step_peers, slots + hubs, width), lambda i: (i, 0, 0)),
        out_shape=jax.ShapeDtypeStruct((peers, slots + hubs, width), BF16),
        compiler_params=params(),
        name="outgoing_rows",
    )(idx, feats, hub_rows)


def own_forward_kernel(count_ref, every_ref, keys_ref, own_ref, sum_ref, deg_ref):
    nodes = sum_ref.shape[0]
    own_rows = own_ref.shape[0]
    deg_ref[...] = jnp.zeros_like(deg_ref)
    sum_ref[...] = jnp.zeros_like(sum_ref)

    def degrees(c, _):
        key = every_ref[pl.ds(c, 1), :]
        dst = key & (nodes - 1)
        high = jnp.where(key < DEAD, dst >> 7, deg_ref.shape[0])
        deg_ref[...] += dot_nt(
            onehot_of_rows(high, deg_ref.shape[0]), onehot_of_rows(dst & 127, 128)
        )
        return 0

    lax.fori_loop(0, every_ref.shape[0], degrees, 0)

    def chunk(c, _):
        key = keys_ref[pl.ds(c, 1), :]
        hot = onehot_of_columns(columns_of(key >> DST_BITS), own_rows)
        values = dot(hot, own_ref[...]).astype(BF16)
        sum_ref[...] += dot(onehot_of_rows(key & (nodes - 1), nodes), values)
        return 0

    lax.fori_loop(0, pl.cdiv(count_ref[0], CHUNK), chunk, 0)


def own_forward(counts, every, keys, own, nodes):
    return pl.pallas_call(
        own_forward_kernel,
        in_specs=[sspec(), vspec(), vspec(), vspec()],
        out_specs=[vspec(), vspec()],
        out_shape=[
            jax.ShapeDtypeStruct((nodes, own.shape[1]), F32),
            jax.ShapeDtypeStruct((16, 128), F32),
        ],
        compiler_params=params(),
        name="own_forward",
    )(counts, every, keys, own)


def received_forward_kernel(
    own_rows, count_ref, low_ref, high_ref, keys_ref, table_ref, base_ref, sum_ref, values_ref
):
    nodes = sum_ref.shape[0]
    blocks = table_ref.shape[0] // CHUNK
    sum_ref[...] = base_ref[...]

    def chunk(c, _):
        key = keys_ref[pl.ds(c, 1), :]
        col = columns_of((key >> DST_BITS) - own_rows)
        values_ref[...] = jnp.zeros_like(values_ref)

        def block(b, _):
            hot = onehot_of_columns(col - b * CHUNK, CHUNK)
            start = pl.multiple_of(b * CHUNK, CHUNK)
            values_ref[...] += dot(hot, table_ref[pl.ds(start, CHUNK), :])
            return 0

        first = jnp.maximum(low_ref[c] - own_rows, 0) // CHUNK
        last = jnp.minimum(jnp.maximum(high_ref[c] - own_rows, 0) // CHUNK, blocks - 1)
        lax.fori_loop(first, last + 1, block, 0)
        sum_ref[...] += dot(
            onehot_of_rows(key & (nodes - 1), nodes), values_ref[...].astype(BF16)
        )
        return 0

    lax.fori_loop(count_ref[0] // CHUNK, pl.cdiv(count_ref[1], CHUNK), chunk, 0)


def received_forward(counts, low, high, keys, table, base, own_rows):
    return pl.pallas_call(
        functools.partial(received_forward_kernel, own_rows),
        in_specs=[sspec(), sspec(), sspec(), vspec(), vspec(), vspec()],
        out_specs=vspec(),
        out_shape=jax.ShapeDtypeStruct(base.shape, F32),
        scratch_shapes=[VMEM((CHUNK, base.shape[1]), F32)],
        compiler_params=params(),
        name="received_forward",
    )(counts, low, high, keys, table, base)


def dense_kernel(
    half_ref,
    mine_ref,
    other_ref,
    deg_ref,
    feat_ref,
    cot_ref,
    w_self_ref,
    w_neigh_ref,
    bias_ref,
    out_ref,
    grad_sum_ref,
    grad_input_ref,
    grad_w_ref,
    left_ref,
    pre_ref,
):
    nodes = feat_ref.shape[0]
    grad_bias = jnp.zeros((8, 128), F32)
    for at in range(0, nodes, 128):
        span = pl.ds(at, 128)
        h = at // 128
        divisor = jnp.maximum(columns_of(deg_ref[h : h + 1, :]), 1.0)
        feats = feat_ref[span, :]
        aggregate = ((mine_ref[span, :] + other_ref[span, :]) / divisor).astype(BF16)
        preact = dot(feats, w_self_ref[...]) + dot(aggregate, w_neigh_ref[...]) + bias_ref[...]
        sig = jax.nn.sigmoid(preact)
        out_ref[span, :] = (preact * sig).astype(BF16)
        slope = sig * (1.0 + preact * (1.0 - sig))
        grad_pre = (cot_ref[span, :].astype(F32) * slope).astype(BF16)
        pre_ref[span, :] = grad_pre
        grad_sum_ref[span, :] = (dot_nt(grad_pre, w_neigh_ref[...]) / divisor).astype(BF16)
        grad_input_ref[span, :] = dot_nt(grad_pre, w_self_ref[...])
        left_ref[span, :] = jnp.where(half_ref[0] == 0, feats.astype(F32), aggregate.astype(F32)).astype(BF16)
        wide = grad_pre.astype(F32)
        for r in range(0, 128, 8):
            grad_bias = grad_bias + wide[r : r + 8]
    grad_w_ref[:128, :] = dot_tn(left_ref[...], pre_ref[...])
    grad_w_ref[128:136, :] = jnp.broadcast_to(
        jnp.sum(grad_bias, axis=0, keepdims=True), (8, 128)
    )


def dense(half, mine, other, deg, feats, cot, w_self, w_neigh, bias):
    nodes, width = feats.shape
    return pl.pallas_call(
        dense_kernel,
        in_specs=[sspec()] + [vspec()] * 8,
        out_specs=[vspec()] * 4,
        out_shape=[
            jax.ShapeDtypeStruct((nodes, width), BF16),
            jax.ShapeDtypeStruct((nodes, width), BF16),
            jax.ShapeDtypeStruct((nodes, width), F32),
            jax.ShapeDtypeStruct((136, width), F32),
        ],
        scratch_shapes=[VMEM((nodes, width), BF16), VMEM((nodes, width), BF16)],
        compiler_params=params(),
        name="dense_part",
    )(half, mine, other, deg, feats, cot, w_self, w_neigh, bias)


def received_backward_kernel(
    own_rows, count_ref, low_ref, high_ref, keys_ref, grad_ref, out_ref, acc_ref, values_ref
):
    nodes = grad_ref.shape[0]
    blocks = acc_ref.shape[0] // CHUNK

    def clear(b, _):
        acc_ref[pl.ds(pl.multiple_of(b * CHUNK, CHUNK), CHUNK), :] = jnp.zeros(
            (CHUNK, acc_ref.shape[1]), F32
        )
        return 0

    lax.fori_loop(0, blocks, clear, 0)

    def chunk(c, _):
        key = keys_ref[pl.ds(c, 1), :]
        row = (key >> DST_BITS) - own_rows
        hot = onehot_of_columns(columns_of(key & (nodes - 1)), nodes)
        values_ref[...] = dot(hot, grad_ref[...]).astype(BF16)

        def block(b, _):
            start = pl.multiple_of(b * CHUNK, CHUNK)
            acc_ref[pl.ds(start, CHUNK), :] += dot(
                onehot_of_rows(row - b * CHUNK, CHUNK), values_ref[...]
            )
            return 0

        first = jnp.maximum(low_ref[c] - own_rows, 0) // CHUNK
        last = jnp.minimum(jnp.maximum(high_ref[c] - own_rows, 0) // CHUNK, blocks - 1)
        lax.fori_loop(first, last + 1, block, 0)
        return 0

    lax.fori_loop(count_ref[0] // CHUNK, pl.cdiv(count_ref[1], CHUNK), chunk, 0)

    def finish(b, _):
        span = pl.ds(pl.multiple_of(b * CHUNK, CHUNK), CHUNK)
        out_ref[span, :] = acc_ref[span, :].astype(BF16)
        return 0

    lax.fori_loop(0, blocks, finish, 0)


def received_backward(counts, low, high, keys, grad_sum, own_rows, table_rows):
    width = grad_sum.shape[1]
    return pl.pallas_call(
        functools.partial(received_backward_kernel, own_rows),
        in_specs=[sspec(), sspec(), sspec(), vspec(), vspec()],
        out_specs=vspec(),
        out_shape=jax.ShapeDtypeStruct((table_rows, width), BF16),
        scratch_shapes=[VMEM((table_rows, width), F32), VMEM((CHUNK, width), BF16)],
        compiler_params=params(),
        name="received_backward",
    )(counts, low, high, keys, grad_sum)


def own_backward_kernel(count_ref, keys_ref, grad_ref, out_ref):
    nodes = grad_ref.shape[0]
    own_rows = out_ref.shape[0]
    out_ref[...] = jnp.zeros_like(out_ref)

    def chunk(c, _):
        key = keys_ref[pl.ds(c, 1), :]
        hot = onehot_of_columns(columns_of(key & (nodes - 1)), nodes)
        values = dot(hot, grad_ref[...]).astype(BF16)
        out_ref[...] += dot(onehot_of_rows(key >> DST_BITS, own_rows), values)
        return 0

    lax.fori_loop(0, pl.cdiv(count_ref[0], CHUNK), chunk, 0)


def own_backward(counts, keys, grad_sum, own_rows):
    return pl.pallas_call(
        own_backward_kernel,
        in_specs=[sspec(), vspec(), vspec()],
        out_specs=vspec(),
        out_shape=jax.ShapeDtypeStruct((own_rows, grad_sum.shape[1]), F32),
        compiler_params=params(),
        name="own_backward",
    )(counts, keys, grad_sum)


def returned_kernel(slots, half_ref, idx_ref, back_ref, own_ref, part_ref, hub_ref):
    nodes = part_ref.shape[0]
    own_rows = own_ref.shape[0]
    peers = back_ref.shape[0]
    width = back_ref.shape[2]
    part_ref[...] = jnp.zeros_like(part_ref)
    part_ref[pl.ds(pl.multiple_of(half_ref[0] * own_rows, own_rows), own_rows), :] = own_ref[...]
    hub_ref[...] = jnp.zeros_like(hub_ref)

    def step(s, _):
        idx = jnp.concatenate([idx_ref[pl.ds(s * 4 + k, 1), :] for k in range(4)], axis=1)
        rows = back_ref[pl.ds(s * 8, 8), :slots, :].reshape(8 * slots, width)
        part_ref[...] += dot(onehot_of_rows(idx, nodes), rows)
        for k in range(8):
            hub_ref[...] += back_ref[s * 8 + k, slots:, :].astype(F32)
        return 0

    lax.fori_loop(0, peers // 8, step, 0)


def returned_sum(half, idx, back, own, nodes, slots):
    width = back.shape[2]
    return pl.pallas_call(
        functools.partial(returned_kernel, slots),
        in_specs=[sspec(), vspec(), vspec(), vspec()],
        out_specs=[vspec(), vspec()],
        out_shape=[
            jax.ShapeDtypeStruct((nodes, width), F32),
            jax.ShapeDtypeStruct((back.shape[1] - slots, width), F32),
        ],
        compiler_params=params(),
        name="returned_sum",
    )(half, idx, back, own)


def tree_sum(value, masks, size):
    parts = [value] + [
        lax.ppermute(value, "dom", [(i, i ^ m) for i in range(size)]) for m in masks
    ]
    while len(parts) > 1:
        parts = [parts[i] + parts[i + 1] for i in range(0, len(parts), 2)]
    return parts[0]


def body(
    node_feats,
    hub_feats,
    w_self,
    w_neigh,
    bias,
    cotangent,
    send_count,
    send_rows,
    edge_src,
    edge_dst,
    edge_count,
):
    num_dom = lax.axis_size("dom")
    half = lax.axis_index("edge")
    nodes, width = node_feats.shape
    block_rows = send_rows.shape[2]
    hubs = hub_feats.shape[0]
    slots, half_hubs, own_rows = block_rows // 2, hubs // 2, nodes // 2
    per_peer = slots + half_hubs
    half_scalar = half.astype(jnp.int32).reshape(1)

    slot_ids = jnp.arange(block_rows, dtype=jnp.int32)[None, :]
    idx_all = jnp.where(slot_ids < send_count[0][:, None], send_rows[0], nodes + 1024)
    idx = jnp.where(half == 0, idx_all[:, 0::2], idx_all[:, 1::2])
    idx = idx.reshape(num_dom * slots // 128, 128)
    hub_half = lax.dynamic_slice_in_dim(hub_feats, half * half_hubs, half_hubs, 0)
    own_half = lax.dynamic_slice_in_dim(node_feats, half * own_rows, own_rows, 0)
    out_rows = outgoing(idx, node_feats, hub_half, slots)
    table = lax.all_to_all(out_rows, "dom", split_axis=0, concat_axis=0, tiled=True)

    src = edge_src.reshape(-1)
    dst = edge_dst.reshape(-1)
    edges = src.shape[0]
    live = jnp.arange(edges, dtype=jnp.int32) < edge_count.reshape(())
    slot = src - nodes
    hub = slot - num_dom * block_rows
    is_own, is_hub = src < nodes, hub >= 0
    peer = slot // block_rows
    place = slot % block_rows
    row = jnp.where(
        is_own,
        src % own_rows,
        own_rows
        + jnp.where(
            is_hub,
            (hub // hubs) * per_peer + slots + hub % half_hubs,
            peer * per_peer + place // 2,
        ),
    )
    side = jnp.where(is_own, src // own_rows, jnp.where(is_hub, (hub % hubs) // half_hubs, place % 2))
    key = (side << HALF_BIT) + (row << DST_BITS) + dst
    key = jnp.where(live, key, DEAD)
    key, _ = lax.optimization_barrier((key, out_rows))
    key_other = lax.ppermute(key, "edge", SWAP)
    every = jnp.concatenate([key, key_other])
    mine = jnp.where((every >> HALF_BIT) == half, every & ((1 << HALF_BIT) - 1), PAD)
    keys = lax.sort(mine).reshape(-1, CHUNK)
    every = every.reshape(-1, CHUNK)
    counts = jnp.stack(
        [
            jnp.sum((keys < (own_rows << DST_BITS)).astype(jnp.int32)),
            jnp.sum((keys < PAD).astype(jnp.int32)),
        ]
    )
    low = keys[:, 0] >> DST_BITS
    high = jnp.max(jnp.where(keys < PAD, keys, 0), axis=1) >> DST_BITS

    own_sum, degree = own_forward(counts, every, keys, own_half, nodes)
    neigh = received_forward(
        counts, low, high, keys, table.reshape(num_dom * per_peer, width), own_sum, own_rows
    )
    neigh_other = lax.ppermute(neigh, "edge", SWAP)
    layer_out, grad_sum, grad_input, grad_w = dense(
        half_scalar,
        neigh,
        neigh_other,
        degree,
        node_feats,
        cotangent,
        w_self,
        w_neigh,
        bias.reshape(1, width),
    )
    row_grads = received_backward(
        counts, low, high, keys, grad_sum, own_rows, num_dom * per_peer
    )
    back = lax.all_to_all(
        row_grads.reshape(num_dom, per_peer, width), "dom", split_axis=0, concat_axis=0, tiled=True
    )
    own_grads = own_backward(counts, keys, grad_sum, own_rows)

    bits = num_dom.bit_length() - 1
    for b in range(bits):
        grad_w = tree_sum(grad_w, [1 << b], num_dom)
    grad_w_other = lax.ppermute(grad_w[:128], "edge", SWAP)
    grad_self = jnp.where(half == 0, grad_w[:128], grad_w_other)
    grad_neigh = jnp.where(half == 0, grad_w_other, grad_w[:128])
    grad_bias = grad_w[128]

    part, hub_part = returned_sum(half_scalar, idx, back, own_grads, nodes, slots)
    part_other = lax.ppermute(part, "edge", SWAP)
    hub_other = lax.ppermute(hub_part, "edge", SWAP)
    grad_feats = grad_input + (part + part_other)
    grad_hubs = jnp.where(
        half == 0,
        jnp.concatenate([hub_part, hub_other]),
        jnp.concatenate([hub_other, hub_part]),
    )
    return (layer_out, grad_feats, grad_hubs, grad_self, grad_neigh, grad_bias)


def solution(mesh):
    placed = (
        P("dom", None),
        P("dom", None),
        P(),
        P(),
        P(),
        P("dom", None),
        P("dom", None),
        P("dom", None, None),
        P("dom", "edge", None),
        P("dom", "edge", None),
        P("dom", "edge"),
    )
    return jax.shard_map(
        body,
        mesh=mesh,
        in_specs=placed,
        out_specs=(P("dom", None), P("dom", None), P("dom", None), P(), P(), P()),
        check_vma=False,
    )
```

time: 1160 us -> 250 us (0.22)
  blocking collectives: 373 us -> 0 us
  other arithmetic: 366 us -> 17.7 us
  waiting for transfers between devices: 298 us -> 87.2 us
  Pallas kernels: 0 us -> 76.8 us
  local copies, waits for them, and re-layouts: 74.2 us -> 12.8 us
  starting transfers between devices: 31.4 us -> 51.9 us
  between operations: 15 us -> 1.54 us
    psum x2 -> x0, blocking collectives: 373 us -> none  [the longest x1 367 us: body(): lax.psum((grad_self, grad_neigh, grad_bias), 'dom')]
    scatter-add x6 -> x0, other arithmetic: 334 us -> none  [the longest x2 98.8 us: gather_block(): return (carry.at[to_part].add(values), None)]
    psum x4 -> x0, waiting for transfers between devices: 149 us -> none  [the longest x1 149 us: body(): hub_total = lax.psum(hub_grad, ('dom', 'edge'))]
    all_gather x2 -> x0, waiting for transfers between devices: 132 us -> none  [the longest x1 110 us: body(): hub_all = lax.all_gather(hub_feats, 'dom', axis=0, tiled=True)]
    pallas_call x0 -> x7, Pallas kernels: none -> 76.8 us  [the longest x1 18 us: own_forward(): pl.pallas_call(own_forward_kernel, in_specs=[sspec(), vspec(), vspec(), v...]
    ppermute x0 -> x12, waiting for transfers between devices: none -> 64.3 us  [the longest x7 62.5 us: tree_sum(): lax.ppermute(value, 'dom', [(i, i ^ m) for i in range(size)])]
    gather x1 -> x0, local copies, waits for them, and re-layouts: 56.3 us -> none  [body(): node_feats[send_idx]]
    ppermute x0 -> x12, starting transfers between devices: none -> 24.5 us  [the longest x7 12.5 us: tree_sum(): lax.ppermute(value, 'dom', [(i, i ^ m) for i in range(size)])]
  transfers between devices with their start and end apart: 9 -> 14, of which waited for: 4 -> 9; matrix products, arithmetic and copies ran while one was open for 6% -> 8% of each run, Pallas kernels for 0% -> 14%
where the time goes in v1:
time: 250 us; the launch traced here: 248 us
  waiting for transfers between devices  87.2 us (35%)
  Pallas kernels  76.8 us (31%)
  starting transfers between devices  51.9 us (21%)
  other arithmetic  17.7 us (7%)
  local copies, waits for them, and re-layouts  12.8 us (5%)
    ppermute x7, waiting for transfers between devices, tree_sum(): lax.ppermute(value, 'dom', [(i, i ^ m) for i in range(size)])  62.5 us
    all_to_all x1, waiting for transfers between devices, body(): lax.all_to_all(out_rows, 'dom', split_axis=0, concat_axis=0, tiled=True)  22.9 us
    pallas_call x1, Pallas kernels, own_forward(): pl.pallas_call(own_forward_kernel, in_specs=[sspec(), vspec(), vspec(), v...  18 us
    all_to_all x1, starting transfers between devices, body(): lax.all_to_all(out_rows, 'dom', split_axis=0, concat_axis=0, tiled=True)  16.5 us
    pallas_call x1, Pallas kernels, received_backward(): pl.pallas_call(functools.partial(received_backward_kernel, own_rows), in_...  15.7 us
    pallas_call x1, Pallas kernels, received_forward(): pl.pallas_call(functools.partial(received_forward_kernel, own_rows), in_s...  15.2 us
    ppermute x7, starting transfers between devices, tree_sum(): lax.ppermute(value, 'dom', [(i, i ^ m) for i in range(size)])  12.5 us
    all_to_all x1, starting transfers between devices, body(): lax.all_to_all(row_grads.reshape(num_dom, per_peer, width), 'dom', split_...  10.9 us
  transfers between devices with their start and end apart: 14, of which 9 were waited for; matrix products, arithmetic and copies ran while one was open for 8% of the time, Pallas kernels for 14%

profile of v1, /device:TPU:1, one launch (start us, length us, event | category | flops | bytes accessed | tf_op | source)
XLA Modules:
  0.0 248.0 jit_solution(1622397673735906075)
XLA Ops:
  4.9 8.8 %outgoing_rows.1 = bf16[128,80,128]{2,1,0:T(8,128)(2,1)S(1)} custom-call(s32[64,128]{1,0:T(8,128)S(1)} %reshape.49.idx_ref, bf16[1024,128]{1,0:T(8,128)(2,1)S(1)} %copy-done.3, bf16[16,128]{1,0:T(8,128)(2,1)S(1)} %constant_dynamic-slice_fusion.1.hub_ref), custom_call_target="tpu_custom_call" | custom-call | tf_op jit(solution)/shard_map/outgoing_rows/pallas_call | solution.py:84
  15.2 16.5 %all-to-all-start = ((bf16[128,80,128]{2,1,0:T(8,128)(2,1)}), bf16[128,80,128]{2,1,0:T(8,128)(2,1)S(1)}, u32[]{:S(2)}, u32[]{:S(2)}) async-start(bf16[128,80,128]{2,1,0:T(8,128)(2,1)} %copy-done.2), calls=%async_computation | async-start | bytes 5242880 | tf_op jit(solution)/shard_map/all_to_all | solution.py:396
  37.0 8.6 %sort.14 = (s32[16384]{0:T(1024)}, s32[16384]{0:T(1024)}) sort(s32[16384]{0:T(1024)S(1)} %and_select_fusion, s32[16384]{0:T(1024)} %iota.11), dimensions={0}, to_apply=%region_0.1 | sort | flops 229376 | bytes 262144 | tf_op jit(solution)/shard_map/sort | solution.py:424
  46.5 1.5 convert_reduce_fusion.1
  50.1 18.0 %own_forward.1 = (f32[1024,128]{1,0:T(8,128)S(1)}, f32[16,128]{1,0:T(8,128)S(1)}) custom-call(s32[2]{0:T(128)S(1)} %pad_add_fusion.1.count_ref, s32[64,256]{1,0:T(8,128)S(1)} %pad_add_fusion.every_ref, s32[64,256]{1,0:T(8,128)S(1)} %reshape.50.keys_ref, bf16[512,128]{1,0:T(8,128)(2,1)S(1)} %constant_dynamic-slice_fusion.own_ref), custom_call_target="tpu_custom_call" | custom-call | tf_op jit(solution)/shard_map/own_forward/pallas_call | solution.py:127
  69.1 22.9 %all-to-all-done = bf16[128,80,128]{2,1,0:T(8,128)(2,1)S(1)} async-done(((bf16[128,80,128]{2,1,0:T(8,128)(2,1)}), bf16[128,80,128]{2,1,0:T(8,128)(2,1)S(1)}, u32[]{:S(2)}, u32[]{:S(2)}) %all-to-all-start) | async-done | bytes 2621472 | tf_op jit(solution)/shard_map/all_to_all | solution.py:396
  93.0 15.2 %received_forward.1.mine_ref = f32[1024,128]{1,0:T(8,128)S(1)} custom-call(s32[2]{0:T(128)S(1)} %pad_add_fusion.1.count_ref, s32[64]{0:T(128)S(1)} %fusion.17.low_ref, s32[64]{0:T(128)S(1)} %broadcast_shift-right-arithmetic_fusion.high_ref, s32[64,256]{1,0:T(8,128)S(1)} %reshape.50.keys_ref, bf16[10240,128]{1,0:T(8,128)(2,1)S(1)} %bitcast.16, ...), custom_call_target="tpu_custom_call" | custom-call | tf_op jit(solution)/shard_map/received_forward/pallas_call | solution.py:170
  108.3 4.4 %collective-permute-start.1 = (f32[1024,128]{1,0:T(8,128)S(1)}, f32[1024,128]{1,0:T(8,128)S(1)}, u32[]{:S(2)}, u32[]{:S(2)}) collective-permute-start(f32[1024,128]{1,0:T(8,128)S(1)} %received_forward.1.mine_ref), channel_id=1, source_target_pairs={{0,1},{1,0},{2,3},{3,2},{4,5},{5,4},{6,7},{7,6},{8,9},{9,8},{10,11... | collective-permute-start | bytes 1572872 | tf_op jit(solution)/shard_map/ppermute | solution.py:439
  112.7 1.5 collective-permute-done.1.other_ref
  114.2 2.4 dense_part.1
  117.4 15.7 %received_backward.1 = bf16[10240,128]{1,0:T(8,128)(2,1)S(1)} custom-call(s32[2]{0:T(128)S(1)} %pad_add_fusion.1.count_ref, s32[64]{0:T(128)S(1)} %fusion.17.low_ref, s32[64]{0:T(128)S(1)} %broadcast_shift-right-arithmetic_fusion.high_ref, s32[64,256]{1,0:T(8,128)S(1)} %reshape.50.keys_ref, bf16[1024,128]{1,0:T(8,128)(2,1)S(1)} %get-tuple-element.23.grad_ref), custom_call_target="tpu_custom_call" | custom-call | tf_op jit(solution)/shard_map/received_backward/pallas_call | solution.py:286
  134.6 10.9 %all-to-all-start.1 = ((bf16[128,80,128]{2,1,0:T(8,128)(2,1)}), bf16[128,80,128]{2,1,0:T(8,128)(2,1)S(1)}, u32[]{:S(2)}, u32[]{:S(2)}) async-start(bf16[128,80,128]{2,1,0:T(8,128)(2,1)} %bitcast.15), calls=%async_computation.1 | async-start | bytes 5242880 | tf_op jit(solution)/shard_map/all_to_all | solution.py:454
  146.2 6.6 %collective-permute-done.4 = f32[136,128]{1,0:T(8,128)S(1)} collective-permute-done((f32[136,128]{1,0:T(8,128)S(1)}, f32[136,128]{1,0:T(8,128)S(1)}, u32[]{:S(2)}, u32[]{:S(2)}) %collective-permute-start.4) | collective-permute-done | bytes 69664 | tf_op jit(solution)/shard_map/ppermute | solution.py:360
  153.8 4.3 %collective-permute-done.5 = f32[136,128]{1,0:T(8,128)S(1)} collective-permute-done((f32[136,128]{1,0:T(8,128)S(1)}, f32[136,128]{1,0:T(8,128)S(1)}, u32[]{:S(2)}, u32[]{:S(2)}) %collective-permute-start.5) | collective-permute-done | bytes 69664 | tf_op jit(solution)/shard_map/ppermute | solution.py:360
  159.0 43.5 %collective-permute-done.6 = f32[136,128]{1,0:T(8,128)S(1)} collective-permute-done((f32[136,128]{1,0:T(8,128)S(1)}, f32[136,128]{1,0:T(8,128)S(1)}, u32[]{:S(2)}, u32[]{:S(2)}) %collective-permute-start.6) | collective-permute-done | bytes 69664 | tf_op jit(solution)/shard_map/ppermute | solution.py:360
  203.5 3.5 %collective-permute-done.7 = f32[136,128]{1,0:T(8,128)S(1)} collective-permute-done((f32[136,128]{1,0:T(8,128)S(1)}, f32[136,128]{1,0:T(8,128)S(1)}, u32[]{:S(2)}, u32[]{:S(2)}) %collective-permute-start.7) | collective-permute-done | bytes 69664 | tf_op jit(solution)/shard_map/ppermute | solution.py:360
  207.0 4.8 %collective-permute-start.8 = (f32[136,128]{1,0:T(8,128)S(1)}, f32[136,128]{1,0:T(8,128)S(1)}, u32[]{:S(2)}, u32[]{:S(2)}) collective-permute-start(f32[136,128]{1,0:T(8,128)S(1)} %add.105), channel_id=1, source_target_pairs={{0,32},{2,34},{4,36},{6,38},{8,40},{10,42},{12,44},{14,46},{16,48}... | collective-permute-start | bytes 208904 | tf_op jit(solution)/shard_map/ppermute | solution.py:360
  211.8 2.4 collective-permute-done.8
  215.4 2.3 collective-permute-done.9
  217.7 2.9 %collective-permute-start.10 = (f32[136,128]{1,0:T(8,128)S(1)}, f32[136,128]{1,0:T(8,128)S(1)}, u32[]{:S(2)}, u32[]{:S(2)}) collective-permute-start(f32[136,128]{1,0:T(8,128)S(1)} %add.107), channel_id=1, source_target_pairs={{0,128},{2,130},{4,132},{6,134},{8,136},{10,138},{12,140},{14,142}... | collective-permute-start | bytes 208904 | tf_op jit(solution)/shard_map/ppermute | solution.py:360
  220.6 9.7 %own_backward.1.own_ref = f32[512,128]{1,0:T(8,128)S(1)} custom-call(s32[2]{0:T(128)S(1)} %pad_add_fusion.1.count_ref, s32[64,256]{1,0:T(8,128)S(1)} %reshape.50.keys_ref, bf16[1024,128]{1,0:T(8,128)(2,1)S(1)} %get-tuple-element.23.grad_ref), custom_call_target="tpu_custom_call" | custom-call | tf_op jit(solution)/shard_map/own_backward/pallas_call | solution.py:313
  230.4 5.9 %collective-permute-start.11 = (f32[128,128]{1,0:T(8,128)S(1)}, f32[128,128]{1,0:T(8,128)S(1)}, u32[]{:S(2)}, u32[]{:S(2)}) collective-permute-start(f32[128,128]{1,0:T(8,128)S(1)} %slice.23), channel_id=1, source_target_pairs={{0,1},{1,0},{2,3},{3,2},{4,5},{5,4},{6,7},{7,6},{8,9},{9,8},{10,11... | collective-permute-start | bytes 196616 | tf_op jit(solution)/shard_map/ppermute | solution.py:462
  236.4 7.1 %returned_sum.1 = (f32[1024,128]{1,0:T(8,128)S(1)}, f32[16,128]{1,0:T(8,128)S(1)}) custom-call(s32[1]{0:T(128)} %bitcast.half_ref, s32[64,128]{1,0:T(8,128)S(1)} %reshape.49.idx_ref, bf16[128,80,128]{2,1,0:T(8,128)(2,1)S(1)} %all-to-all-done.1.back_ref, f32[512,128]{1,0:T(8,128)S(1)} %own_backward.1.own_ref), custom_call_target="tpu_custom_call" | custom-call | tf_op jit(solution)/shard_map/returned_sum/pallas_call | solution.py:345
  246.1 2.0 add_add_fusion
  (73 shorter events, 25.2 us)
Async XLA Ops:
  0.6 3.3 %copy-start = (bf16[32,128]{1,0:T(8,128)(2,1)S(1)}, bf16[32,128]{1,0:T(8,128)(2,1)}, u32[]{:S(2)}) copy-start(bf16[32,128]{1,0:T(8,128)(2,1)} %param.12) | copy-start | bytes 24580
  13.7 1.5 copy-start.2
  15.2 17.1 %copy-start.12 = (s32[1,1,8192]{2,1,0:T(1,128)S(1)}, s32[1,1,8192]{2,1,0:T(1,128)}, u32[]{:S(2)}) copy-start(s32[1,1,8192]{2,1,0:T(1,128)} %param.20) | copy-start | bytes 98308
  15.2 17.1 %copy-start.13 = (s32[1,1,8192]{2,1,0:T(1,128)S(1)}, s32[1,1,8192]{2,1,0:T(1,128)}, u32[]{:S(2)}) copy-start(s32[1,1,8192]{2,1,0:T(1,128)} %param.19) | copy-start | bytes 98308
  15.2 18.4 %copy-start.4 = (bf16[1024,128]{1,0:T(8,128)(2,1)S(1)}, bf16[1024,128]{1,0:T(8,128)(2,1)}, u32[]{:S(2)}) copy-start(bf16[1024,128]{1,0:T(8,128)(2,1)} %feat_ref.3) | copy-start | bytes 786436
  15.2 76.8 %all-to-all-start = ((bf16[128,80,128]{2,1,0:T(8,128)(2,1)}), bf16[128,80,128]{2,1,0:T(8,128)(2,1)S(1)}, u32[]{:S(2)}, u32[]{:S(2)}) async-start(bf16[128,80,128]{2,1,0:T(8,128)(2,1)} %copy-done.2), calls=%async_computation | async-start | bytes 5242880 | tf_op jit(solution)/shard_map/all_to_all | solution.py:396
  32.5 2.3 collective-permute-start
  33.6 80.6 %copy-start.8 = (bf16[1024,128]{1,0:T(8,128)(2,1)S(1)}, bf16[1024,128]{1,0:T(8,128)(2,1)}, u32[]{:S(2)}) copy-start(bf16[1024,128]{1,0:T(8,128)(2,1)} %cot_ref.1) | copy-start | bytes 786436
  33.6 80.6 %copy-start.9 = (bf16[128,128]{1,0:T(8,128)(2,1)S(1)}, bf16[128,128]{1,0:T(8,128)(2,1)}, u32[]{:S(2)}) copy-start(bf16[128,128]{1,0:T(8,128)(2,1)} %w_self_ref.1) | copy-start | bytes 98308
  33.6 80.6 %copy-start.10 = (bf16[128,128]{1,0:T(8,128)(2,1)S(1)}, bf16[128,128]{1,0:T(8,128)(2,1)}, u32[]{:S(2)}) copy-start(bf16[128,128]{1,0:T(8,128)(2,1)} %w_neigh_ref.1) | copy-start | bytes 98308
  33.6 80.6 %copy-start.11 = (f32[128]{0:T(128)S(1)}, f32[128]{0:T(128)}, u32[]{:S(2)}) copy-start(f32[128]{0:T(128)} %param.15) | copy-start | bytes 1540
  108.3 6.0 %collective-permute-start.1 = (f32[1024,128]{1,0:T(8,128)S(1)}, f32[1024,128]{1,0:T(8,128)S(1)}, u32[]{:S(2)}, u32[]{:S(2)}) collective-permute-start(f32[1024,128]{1,0:T(8,128)S(1)} %received_forward.1.mine_ref), channel_id=1, source_target_pairs={{0,1},{1,0},{2,3},{3,2},{4,5},{5,4},{6,7},{7,6},{8,9},{9,8},{10,11... | collective-permute-start | bytes 1572872 | tf_op jit(solution)/shard_map/ppermute | solution.py:439
  133.1 1.5 copy-start.1
  134.6 101.8 %all-to-all-start.1 = ((bf16[128,80,128]{2,1,0:T(8,128)(2,1)}), bf16[128,80,128]{2,1,0:T(8,128)(2,1)S(1)}, u32[]{:S(2)}, u32[]{:S(2)}) async-start(bf16[128,80,128]{2,1,0:T(8,128)(2,1)} %bitcast.15), calls=%async_computation.1 | async-start | bytes 5242880 | tf_op jit(solution)/shard_map/all_to_all | solution.py:454
  145.5 7.2 %collective-permute-start.4 = (f32[136,128]{1,0:T(8,128)S(1)}, f32[136,128]{1,0:T(8,128)S(1)}, u32[]{:S(2)}, u32[]{:S(2)}) collective-permute-start(f32[136,128]{1,0:T(8,128)S(1)} %get-tuple-element.26), channel_id=1, source_target_pairs={{0,2},{2,0},{4,6},{6,4},{8,10},{10,8},{12,14},{14,12},{16,18},{18,... | collective-permute-start | bytes 208904 | tf_op jit(solution)/shard_map/ppermute | solution.py:360
  152.8 5.3 %collective-permute-start.5 = (f32[136,128]{1,0:T(8,128)S(1)}, f32[136,128]{1,0:T(8,128)S(1)}, u32[]{:S(2)}, u32[]{:S(2)}) collective-permute-start(f32[136,128]{1,0:T(8,128)S(1)} %add.102), channel_id=1, source_target_pairs={{0,4},{2,6},{4,0},{6,2},{8,12},{10,14},{12,8},{14,10},{16,20},{18,... | collective-permute-start | bytes 208904 | tf_op jit(solution)/shard_map/ppermute | solution.py:360
  158.1 44.4 %collective-permute-start.6 = (f32[136,128]{1,0:T(8,128)S(1)}, f32[136,128]{1,0:T(8,128)S(1)}, u32[]{:S(2)}, u32[]{:S(2)}) collective-permute-start(f32[136,128]{1,0:T(8,128)S(1)} %add.103), channel_id=1, source_target_pairs={{0,8},{2,10},{4,12},{6,14},{8,0},{10,2},{12,4},{14,6},{16,24},{18,... | collective-permute-start | bytes 208904 | tf_op jit(solution)/shard_map/ppermute | solution.py:360
  202.5 4.5 %collective-permute-start.7 = (f32[136,128]{1,0:T(8,128)S(1)}, f32[136,128]{1,0:T(8,128)S(1)}, u32[]{:S(2)}, u32[]{:S(2)}) collective-permute-start(f32[136,128]{1,0:T(8,128)S(1)} %add.104), channel_id=1, source_target_pairs={{0,16},{2,18},{4,20},{6,22},{8,24},{10,26},{12,28},{14,30},{16,0},... | collective-permute-start | bytes 208904 | tf_op jit(solution)/shard_map/ppermute | solution.py:360
  207.0 7.2 %collective-permute-start.8 = (f32[136,128]{1,0:T(8,128)S(1)}, f32[136,128]{1,0:T(8,128)S(1)}, u32[]{:S(2)}, u32[]{:S(2)}) collective-permute-start(f32[136,128]{1,0:T(8,128)S(1)} %add.105), channel_id=1, source_target_pairs={{0,32},{2,34},{4,36},{6,38},{8,40},{10,42},{12,44},{14,46},{16,48}... | collective-permute-start | bytes 208904 | tf_op jit(solution)/shard_map/ppermute | solution.py:360
  214.2 3.5 %collective-permute-start.9 = (f32[136,128]{1,0:T(8,128)S(1)}, f32[136,128]{1,0:T(8,128)S(1)}, u32[]{:S(2)}, u32[]{:S(2)}) collective-permute-start(f32[136,128]{1,0:T(8,128)S(1)} %add.106), channel_id=1, source_target_pairs={{0,64},{2,66},{4,68},{6,70},{8,72},{10,74},{12,76},{14,78},{16,80}... | collective-permute-start | bytes 208904 | tf_op jit(solution)/shard_map/ppermute | solution.py:360
  217.7 12.7 %collective-permute-start.10 = (f32[136,128]{1,0:T(8,128)S(1)}, f32[136,128]{1,0:T(8,128)S(1)}, u32[]{:S(2)}, u32[]{:S(2)}) collective-permute-start(f32[136,128]{1,0:T(8,128)S(1)} %add.107), channel_id=1, source_target_pairs={{0,128},{2,130},{4,132},{6,134},{8,136},{10,138},{12,140},{14,142}... | collective-permute-start | bytes 208904 | tf_op jit(solution)/shard_map/ppermute | solution.py:360
  230.4 14.1 %collective-permute-start.11 = (f32[128,128]{1,0:T(8,128)S(1)}, f32[128,128]{1,0:T(8,128)S(1)}, u32[]{:S(2)}, u32[]{:S(2)}) collective-permute-start(f32[128,128]{1,0:T(8,128)S(1)} %slice.23), channel_id=1, source_target_pairs={{0,1},{1,0},{2,3},{3,2},{4,5},{5,4},{6,7},{7,6},{8,9},{9,8},{10,11... | collective-permute-start | bytes 196616 | tf_op jit(solution)/shard_map/ppermute | solution.py:462
  243.4 2.6 %collective-permute-start.2 = (f32[1024,128]{1,0:T(8,128)S(1)}, f32[1024,128]{1,0:T(8,128)S(1)}, u32[]{:S(2)}, u32[]{:S(2)}) collective-permute-start(f32[1024,128]{1,0:T(8,128)S(1)} %get-tuple-element.24), channel_id=1, source_target_pairs={{0,1},{1,0},{2,3},{3,2},{4,5},{5,4},{6,7},{7,6},{8,9},{9,8},{10,11... | collective-permute-start | bytes 1572872 | tf_op jit(solution)/shard_map/ppermute | solution.py:468
  244.1 1.4 collective-permute-start.3
  (4 other events, 3.6 us)

commit v2 on v1

v2 whole, which is shorter than its diff:
```python
import functools

import jax
import jax.numpy as jnp
import numpy as np
from jax import lax
from jax.experimental import pallas as pl
from jax.experimental.pallas import tpu as pltpu
from jax.sharding import PartitionSpec as P

F32 = jnp.float32
BF16 = jnp.bfloat16
VMEM = pltpu.VMEM
SMEM = pltpu.SMEM
SWAP = [(0, 1), (1, 0)]
CHUNK = 256
DST_BITS = 10
PAD = 1 << 30
DEAD = 1 << 26
HALF_BIT = 24


def params(mib=40):
    return pltpu.CompilerParams(vmem_limit_bytes=mib * 1024 * 1024)


def vspec():
    return pl.BlockSpec(memory_space=VMEM)


def sspec():
    return pl.BlockSpec(memory_space=SMEM)


def columns_of(row):
    parts = []
    for at in range(0, row.shape[1], 128):
        parts.append(jnp.broadcast_to(row[:, at : at + 128], (128, 128)).T)
    return jnp.concatenate(parts, axis=0)


def onehot_of_columns(col, width):
    lane = lax.broadcasted_iota(jnp.int32, col.shape, 1)
    parts = [
        jnp.where(col == lane + at, 1.0, 0.0).astype(BF16) for at in range(0, width, 128)
    ]
    return jnp.concatenate(parts, axis=1)


def onehot_of_rows(row, height):
    sub = lax.broadcasted_iota(jnp.int32, (height, row.shape[1]), 0)
    return jnp.where(sub == row, 1.0, 0.0).astype(BF16)


def dot(a, b):
    return jnp.dot(a, b, preferred_element_type=F32)


def dot_nt(a, b):
    return lax.dot_general(a, b, (((1,), (1,)), ((), ())), preferred_element_type=F32)


def dot_tn(a, b):
    return lax.dot_general(a, b, (((0,), (0,)), ((), ())), preferred_element_type=F32)


def outgoing_kernel(slots, idx_ref, feat_ref, out_ref):
    step = pl.program_id(0)
    peers = out_ref.shape[0]
    rows = feat_ref.shape[0]
    for pair in range(peers // 4):
        at = step * (peers // 2) + pair * 2
        idx = [idx_ref[pl.ds(at + k, 1), :] for k in range(2)]
        hot = onehot_of_columns(columns_of(jnp.concatenate(idx, axis=1)), rows)
        picked = dot(hot, feat_ref[...]).astype(BF16)
        for k in range(4):
            out_ref[pair * 4 + k, :, :] = picked[k * slots : (k + 1) * slots]


def outgoing(idx, feats, slots, step_peers=8):
    peers = idx.shape[0] * idx.shape[1] // slots
    width = feats.shape[1]
    return pl.pallas_call(
        functools.partial(outgoing_kernel, slots),
        grid=(peers // step_peers,),
        in_specs=[
            pl.BlockSpec(idx.shape, lambda i: (0, 0)),
            pl.BlockSpec(feats.shape, lambda i: (0, 0)),
        ],
        out_specs=pl.BlockSpec((step_peers, slots, width), lambda i: (i, 0, 0)),
        out_shape=jax.ShapeDtypeStruct((peers, slots, width), BF16),
        compiler_params=params(),
        name="outgoing_rows",
    )(idx, feats)


def over_windows(c, low_ref, high_ref, rows, window, visit):
    low = low_ref[c] // 128 * 128

    def step(w, _):
        base = low + w * window
        visit(pl.multiple_of(jnp.minimum(base, rows - window), 128), base)
        return 0

    lax.fori_loop(0, (high_ref[c] - low) // window + 1, step, 0)


def gather_add(c, offset, window, low_ref, high_ref, keys_ref, table_ref, sum_ref, values_ref):
    nodes = sum_ref.shape[0]
    key = keys_ref[pl.ds(c, 1), :]
    row = (key >> DST_BITS) - offset
    values_ref[...] = jnp.zeros_like(values_ref)

    def visit(start, base):
        hot = onehot_of_columns(columns_of(jnp.where(row >= base, row - start, -1)), window)
        values_ref[...] += dot(hot, table_ref[pl.ds(start, window), :])

    over_windows(c, low_ref, high_ref, table_ref.shape[0], window, visit)
    sum_ref[...] += dot(onehot_of_rows(key & (nodes - 1), nodes), values_ref[...].astype(BF16))


def spread_add(c, offset, window, low_ref, high_ref, keys_ref, grad_ref, acc_ref):
    nodes = grad_ref.shape[0]
    key = keys_ref[pl.ds(c, 1), :]
    row = (key >> DST_BITS) - offset
    hot = onehot_of_columns(columns_of(key & (nodes - 1)), nodes)
    values = dot(hot, grad_ref[...]).astype(BF16)

    def visit(start, base):
        hot = onehot_of_rows(jnp.where(row >= base, row - start, -1), window)
        acc_ref[pl.ds(start, window), :] += dot(hot, values)

    over_windows(c, low_ref, high_ref, acc_ref.shape[0], window, visit)


def near_forward_kernel(
    window, count_ref, low_ref, high_ref, every_ref, keys_ref, table_ref, sum_ref, deg_ref, values_ref
):
    nodes = sum_ref.shape[0]
    deg_ref[...] = jnp.zeros_like(deg_ref)
    sum_ref[...] = jnp.zeros_like(sum_ref)

    def degrees(c, _):
        key = every_ref[pl.ds(c, 1), :]
        dst = key & (nodes - 1)
        high = jnp.where(key < DEAD, dst >> 7, deg_ref.shape[0])
        deg_ref[...] += dot_nt(
            onehot_of_rows(high, deg_ref.shape[0]), onehot_of_rows(dst & 127, 128)
        )
        return 0

    lax.fori_loop(0, every_ref.shape[0], degrees, 0)

    def chunk(c, _):
        gather_add(c, 0, window, low_ref, high_ref, keys_ref, table_ref, sum_ref, values_ref)
        return 0

    lax.fori_loop(0, pl.cdiv(count_ref[0], CHUNK), chunk, 0)


def near_forward(counts, low, high, every, keys, table, nodes, window=640):
    width = table.shape[1]
    return pl.pallas_call(
        functools.partial(near_forward_kernel, min(window, table.shape[0])),
        in_specs=[sspec(), sspec(), sspec(), vspec(), vspec(), vspec()],
        out_specs=[vspec(), vspec()],
        out_shape=[
            jax.ShapeDtypeStruct((nodes, width), F32),
            jax.ShapeDtypeStruct((16, 128), F32),
        ],
        scratch_shapes=[VMEM((CHUNK, width), F32)],
        compiler_params=params(),
        name="near_forward",
    )(counts, low, high, every, keys, table)


def far_forward_kernel(
    offset, window, count_ref, low_ref, high_ref, keys_ref, table_ref, base_ref, sum_ref, values_ref
):
    sum_ref[...] = base_ref[...]

    def chunk(c, _):
        gather_add(c, offset, window, low_ref, high_ref, keys_ref, table_ref, sum_ref, values_ref)
        return 0

    lax.fori_loop(count_ref[0] // CHUNK, pl.cdiv(count_ref[1], CHUNK), chunk, 0)


def far_forward(counts, low, high, keys, table, base, offset, window=1280):
    return pl.pallas_call(
        functools.partial(far_forward_kernel, offset, min(window, table.shape[0])),
        in_specs=[sspec(), sspec(), sspec(), vspec(), vspec(), vspec()],
        out_specs=vspec(),
        out_shape=jax.ShapeDtypeStruct(base.shape, F32),
        scratch_shapes=[VMEM((CHUNK, base.shape[1]), F32)],
        compiler_params=params(),
        name="far_forward",
    )(counts, low, high, keys, table, base)


def dense_kernel(
    half_ref,
    mine_ref,
    other_ref,
    deg_ref,
    feat_ref,
    cot_ref,
    w_self_ref,
    w_neigh_ref,
    bias_ref,
    out_ref,
    grad_sum_ref,
    grad_input_ref,
    grad_w_ref,
    left_ref,
    pre_ref,
):
    nodes = feat_ref.shape[0]
    grad_bias = jnp.zeros((8, 128), F32)
    for at in range(0, nodes, 128):
        span = pl.ds(at, 128)
        h = at // 128
        divisor = jnp.maximum(columns_of(deg_ref[h : h + 1, :]), 1.0)
        feats = feat_ref[span, :]
        aggregate = ((mine_ref[span, :] + other_ref[span, :]) / divisor).astype(BF16)
        preact = dot(feats, w_self_ref[...]) + dot(aggregate, w_neigh_ref[...]) + bias_ref[...]
        sig = jax.nn.sigmoid(preact)
        out_ref[span, :] = (preact * sig).astype(BF16)
        slope = sig * (1.0 + preact * (1.0 - sig))
        grad_pre = (cot_ref[span, :].astype(F32) * slope).astype(BF16)
        pre_ref[span, :] = grad_pre
        grad_sum_ref[span, :] = (dot_nt(grad_pre, w_neigh_ref[...]) / divisor).astype(BF16)
        grad_input_ref[span, :] = dot_nt(grad_pre, w_self_ref[...])
        left_ref[span, :] = jnp.where(half_ref[0] == 0, feats.astype(F32), aggregate.astype(F32)).astype(BF16)
        wide = grad_pre.astype(F32)
        for r in range(0, 128, 8):
            grad_bias = grad_bias + wide[r : r + 8]
    grad_w_ref[:128, :] = dot_tn(left_ref[...], pre_ref[...])
    grad_w_ref[128:, :] = jnp.broadcast_to(
        jnp.sum(grad_bias, axis=0, keepdims=True), (grad_w_ref.shape[0] - 128, 128)
    )


def dense(half, mine, other, deg, feats, cot, w_self, w_neigh, bias):
    nodes, width = feats.shape
    return pl.pallas_call(
        dense_kernel,
        in_specs=[sspec()] + [vspec()] * 8,
        out_specs=[vspec()] * 4,
        out_shape=[
            jax.ShapeDtypeStruct((nodes, width), BF16),
            jax.ShapeDtypeStruct((nodes, width), BF16),
            jax.ShapeDtypeStruct((nodes, width), F32),
            jax.ShapeDtypeStruct((192, width), F32),
        ],
        scratch_shapes=[VMEM((nodes, width), BF16), VMEM((nodes, width), BF16)],
        compiler_params=params(),
        name="dense_part",
    )(half, mine, other, deg, feats, cot, w_self, w_neigh, bias)


def far_backward_kernel(
    offset, window, count_ref, low_ref, high_ref, keys_ref, grad_ref, out_ref, acc_ref
):
    rows = acc_ref.shape[0]
    block = min(512, rows)

    def clear(b, _):
        span = pl.ds(pl.multiple_of(b * block, block), block)
        acc_ref[span, :] = jnp.zeros((block, acc_ref.shape[1]), F32)
        return 0

    lax.fori_loop(0, rows // block, clear, 0)

    def chunk(c, _):
        spread_add(c, offset, window, low_ref, high_ref, keys_ref, grad_ref, acc_ref)
        return 0

    lax.fori_loop(count_ref[0] // CHUNK, pl.cdiv(count_ref[1], CHUNK), chunk, 0)

    def finish(b, _):
        span = pl.ds(pl.multiple_of(b * block, block), block)
        out_ref[span, :] = acc_ref[span, :].astype(BF16)
        return 0

    lax.fori_loop(0, rows // block, finish, 0)


def far_backward(counts, low, high, keys, grad_sum, offset, rows, window=1280):
    width = grad_sum.shape[1]
    return pl.pallas_call(
        functools.partial(far_backward_kernel, offset, min(window, rows)),
        in_specs=[sspec(), sspec(), sspec(), vspec(), vspec()],
        out_specs=vspec(),
        out_shape=jax.ShapeDtypeStruct((rows, width), BF16),
        scratch_shapes=[VMEM((rows, width), F32)],
        compiler_params=params(),
        name="far_backward",
    )(counts, low, high, keys, grad_sum)


def near_backward_kernel(window, count_ref, low_ref, high_ref, keys_ref, grad_ref, out_ref):
    out_ref[...] = jnp.zeros_like(out_ref)

    def chunk(c, _):
        spread_add(c, 0, window, low_ref, high_ref, keys_ref, grad_ref, out_ref)
        return 0

    lax.fori_loop(0, pl.cdiv(count_ref[0], CHUNK), chunk, 0)


def near_backward(counts, low, high, keys, grad_sum, rows, window=640):
    return pl.pallas_call(
        functools.partial(near_backward_kernel, min(window, rows)),
        in_specs=[sspec(), sspec(), sspec(), vspec(), vspec()],
        out_specs=vspec(),
        out_shape=jax.ShapeDtypeStruct((rows, grad_sum.shape[1]), F32),
        compiler_params=params(),
        name="near_backward",
    )(counts, low, high, keys, grad_sum)


def returned_kernel(half_ref, idx_ref, back_ref, near_ref, part_ref):
    nodes = part_ref.shape[0]
    own_rows = nodes // 2
    peers, slots, width = back_ref.shape
    part_ref[...] = jnp.zeros_like(part_ref)
    own_span = pl.ds(pl.multiple_of(half_ref[0] * own_rows, own_rows), own_rows)
    part_ref[own_span, :] = near_ref[:own_rows, :]

    def step(s, _):
        idx = jnp.concatenate([idx_ref[pl.ds(s * 4 + k, 1), :] for k in range(4)], axis=1)
        rows = back_ref[pl.ds(s * 8, 8), :, :].reshape(8 * slots, width)
        part_ref[...] += dot(onehot_of_rows(idx, nodes), rows)
        return 0

    lax.fori_loop(0, peers // 8, step, 0)


def returned_sum(half, idx, back, near, nodes):
    return pl.pallas_call(
        returned_kernel,
        in_specs=[sspec(), vspec(), vspec(), vspec()],
        out_specs=vspec(),
        out_shape=jax.ShapeDtypeStruct((nodes, back.shape[2]), F32),
        compiler_params=params(),
        name="returned_sum",
    )(half, idx, back, near)


def torus_of(size):
    side = 4 if size >= 64 else 2
    return side, size // (side * side), side


def groups_of(size, axis):
    sizes = torus_of(size)
    ids = np.arange(size).reshape(sizes)
    return np.moveaxis(ids, axis, -1).reshape(-1, sizes[axis]).tolist()


X_AXIS, Z_AXIS, Y_AXIS = 0, 1, 2


def exchange(blocks, axis, size):
    return lax.all_to_all(
        blocks, "dom", 0, 0, axis_index_groups=groups_of(size, axis), tiled=True
    )


def partners(size, axis):
    step, count = ((torus_of(size)[2] * torus_of(size)[1], torus_of(size)[0]) if axis == X_AXIS
                   else (1, torus_of(size)[2]))
    return [[(i, i ^ (step * j)) for i in range(size)] for j in range(1, count)]


def swap_blocks(blocks, axis, size):
    return [blocks[0]] + [
        lax.ppermute(block, "dom", pairs) for block, pairs in zip(blocks[1:], partners(size, axis))
    ]


def pair_sum(parts):
    while len(parts) > 1:
        parts = [parts[i] + parts[i + 1] for i in range(0, len(parts), 2)]
    return parts[0]


def after(value, *earlier):
    return lax.optimization_barrier((value,) + earlier)[0]


def body(
    node_feats,
    hub_feats,
    w_self,
    w_neigh,
    bias,
    cotangent,
    send_count,
    send_rows,
    edge_src,
    edge_dst,
    edge_count,
):
    num_dom = lax.axis_size("dom")
    half = lax.axis_index("edge")
    nodes, width = node_feats.shape
    block_rows = send_rows.shape[2]
    hubs = hub_feats.shape[0]
    slots, half_hubs, own_rows = block_rows // 2, hubs // 2, nodes // 2
    half_scalar = half.astype(jnp.int32).reshape(1)
    xs, zs, ys = torus_of(num_dom)
    hub_rows = num_dom * half_hubs
    near_rows, far_rows = own_rows + hub_rows, num_dom * slots

    hub_half = lax.dynamic_slice_in_dim(hub_feats, half * half_hubs, half_hubs, 0)
    hub_z = exchange(jnp.broadcast_to(hub_half[None], (zs,) + hub_half.shape), Z_AXIS, num_dom)

    slot_ids = jnp.arange(block_rows, dtype=jnp.int32)[None, :]
    idx_all = jnp.where(slot_ids < send_count[0][:, None], send_rows[0], nodes + 1024)
    idx = jnp.where(half == 0, idx_all[:, 0::2], idx_all[:, 1::2])
    idx = idx.reshape(num_dom * slots // 128, 128)
    out_rows = outgoing(idx, node_feats, slots)
    out_rows, hub_z = lax.optimization_barrier((out_rows, hub_z))
    table = lax.all_to_all(out_rows, "dom", split_axis=0, concat_axis=0, tiled=True)
    hub_z = after(hub_z.reshape(zs * half_hubs, width), out_rows)
    hub_x = jnp.concatenate(swap_blocks([hub_z] * xs, X_AXIS, num_dom))
    hub_y = jnp.concatenate(swap_blocks([hub_x] * ys, Y_AXIS, num_dom))
    own_half = lax.dynamic_slice_in_dim(node_feats, half * own_rows, own_rows, 0)
    near_table = jnp.concatenate([own_half, hub_y.reshape(hub_rows, width)])

    src = edge_src.reshape(-1)
    dst = edge_dst.reshape(-1)
    edges = src.shape[0]
    live = jnp.arange(edges, dtype=jnp.int32) < edge_count.reshape(())
    slot = src - nodes
    hub = slot - num_dom * block_rows
    is_own, is_hub = src < nodes, hub >= 0
    master = hub // hubs
    me = lax.axis_index("dom")
    far_y, far_x = (master ^ me) & (ys - 1), (master ^ me) // (ys * zs)
    master_place = (far_y * xs + far_x) * zs + (master // ys) % zs
    row = jnp.where(
        is_own,
        src % own_rows,
        jnp.where(
            is_hub,
            own_rows + master_place * half_hubs + hub % half_hubs,
            near_rows + slot // 2,
        ),
    )
    side = jnp.where(is_own, src // own_rows, jnp.where(is_hub, (hub % hubs) // half_hubs, slot % 2))
    key = (side << HALF_BIT) + (row << DST_BITS) + dst
    key = after(jnp.where(live, key, DEAD), out_rows)
    key_other = lax.ppermute(key, "edge", SWAP)
    every = jnp.concatenate([key, key_other])
    mine = jnp.where((every >> HALF_BIT) == half, every & ((1 << HALF_BIT) - 1), PAD)
    keys = lax.sort(mine).reshape(-1, CHUNK)
    every = every.reshape(-1, CHUNK)
    near_edge = keys < (near_rows << DST_BITS)
    live_edge = keys < PAD
    counts = jnp.stack([jnp.sum(near_edge.astype(jnp.int32)), jnp.sum(live_edge.astype(jnp.int32))])
    near_low = jnp.minimum(keys[:, 0] >> DST_BITS, near_rows - 1)
    near_high = jnp.max(jnp.where(near_edge, keys, 0), axis=1) >> DST_BITS
    far_low = jnp.min(jnp.where(near_edge, PAD, keys), axis=1) >> DST_BITS
    far_low = jnp.minimum(far_low - near_rows, far_rows - 1)
    far_high = jnp.max(jnp.where(live_edge, keys, 0), axis=1) >> DST_BITS
    far_high = jnp.maximum(far_high - near_rows, 0)

    near_sum, degree = near_forward(counts, near_low, near_high, every, keys, near_table, nodes)
    neigh = far_forward(
        counts, far_low, far_high, keys, table.reshape(far_rows, width), near_sum, near_rows
    )
    neigh_other = lax.ppermute(neigh, "edge", SWAP)
    layer_out, grad_sum, grad_input, grad_w = dense(
        half_scalar,
        neigh,
        neigh_other,
        degree,
        node_feats,
        cotangent,
        w_self,
        w_neigh,
        bias.reshape(1, width),
    )
    share = grad_w.shape[0] // zs
    grad_w = exchange(grad_w.reshape(zs, share, width), Z_AXIS, num_dom)
    row_grads = far_backward(counts, far_low, far_high, keys, grad_sum, near_rows, far_rows)
    row_grads, grad_w = lax.optimization_barrier((row_grads, grad_w))
    back = lax.all_to_all(
        row_grads.reshape(num_dom, slots, width), "dom", split_axis=0, concat_axis=0, tiled=True
    )
    near_grads = near_backward(
        counts, near_low, near_high, after(keys, row_grads), grad_sum, near_rows
    )

    grad_w = jnp.sum(grad_w, axis=0)
    hub_part = near_grads[own_rows:]
    for axis, parts in ((Y_AXIS, ys), (X_AXIS, xs)):
        blocks = jnp.split(hub_part, parts)
        kept = blocks[0].shape[0]
        both = pair_sum(
            swap_blocks([jnp.concatenate([block, grad_w]) for block in blocks], axis, num_dom)
        )
        hub_part, grad_w = both[:kept], both[kept:]
    hub_part = hub_part.reshape(zs, half_hubs, width)
    both = jnp.concatenate([hub_part, jnp.broadcast_to(grad_w[None], (zs,) + grad_w.shape)], axis=1)
    both = exchange(after(both, back), Z_AXIS, num_dom)
    hub_part = jnp.sum(both[:, :half_hubs], axis=0)
    grad_w = both[:, half_hubs:].reshape(zs * share, width)

    part = returned_sum(half_scalar, idx, back, near_grads, nodes)
    part_other = lax.ppermute(part, "edge", SWAP)
    small = jnp.concatenate([grad_w[:width], hub_part])
    small_other = lax.ppermute(small, "edge", SWAP)
    first = jnp.where(half == 0, small, small_other)
    second = jnp.where(half == 0, small_other, small)
    grad_self, grad_neigh, grad_bias = first[:width], second[:width], grad_w[width]
    grad_hubs = jnp.concatenate([first[width:], second[width:]])
    grad_feats = grad_input + (part + part_other)
    return (layer_out, grad_feats, grad_hubs, grad_self, grad_neigh, grad_bias)


def solution(mesh):
    placed = (
        P("dom", None),
        P("dom", None),
        P(),
        P(),
        P(),
        P("dom", None),
        P("dom", None),
        P("dom", None, None),
        P("dom", "edge", None),
        P("dom", "edge", None),
        P("dom", "edge"),
    )
    return jax.shard_map(
        body,
        mesh=mesh,
        in_specs=placed,
        out_specs=(P("dom", None), P("dom", None), P("dom", None), P(), P(), P()),
        check_vma=False,
    )
```

time: 250 us -> 230 us (0.920)
  waiting for transfers between devices: 87.2 us -> 38.1 us
  starting transfers between devices: 51.9 us -> 75.8 us
  local copies, waits for them, and re-layouts: 12.8 us -> 23.8 us
  Pallas kernels: 76.8 us -> 73.5 us
    ppermute x9 -> x13, waiting for transfers between devices: 62.8 us -> 36.6 us  [the longest x12 36.2 us: swap_blocks(): lax.ppermute(block, 'dom', pairs)]
    all_to_all x1 -> x4, starting transfers between devices: 10.9 us -> 34.1 us  [the longest x3 21.2 us: exchange(): lax.all_to_all(blocks, 'dom', 0, 0, axis_index_groups=groups_of(size, axi...]
    all_to_all x1, waiting for transfers between devices: 22.9 us -> 0.01 us  [body(): lax.all_to_all(out_rows, 'dom', split_axis=0, concat_axis=0, tiled=True)]
    unnamed x29 -> x61, local copies, waits for them, and re-layouts: 7.21 us -> 16.7 us
    ppermute x1, starting transfers between devices: 0.11 us -> 5.09 us  [body(): part_other = lax.ppermute(part, 'edge', SWAP)]
    pallas_call x5, Pallas kernels: 65.7 us -> 62.3 us  [the longest x1 23.4 us: near_forward(): pl.pallas_call(functools.partial(near_forward_kernel, min(window, table.s...]
    ppermute x9 -> x13, starting transfers between devices: 18.9 us -> 17.6 us  [the longest x12 15.8 us: swap_blocks(): lax.ppermute(block, 'dom', pairs)]
  transfers between devices with their start and end apart: 14 -> 21, of which waited for: 9 -> 9; matrix products, arithmetic and copies ran while one was open for 8% -> 11% of each run, Pallas kernels for 14% -> 27%
where the time goes in v2:
time: 230 us
  starting transfers between devices  75.8 us (33%)
  Pallas kernels  73.5 us (32%)
  waiting for transfers between devices  38.1 us (17%)
  local copies, waits for them, and re-layouts  23.8 us (10%)
  other arithmetic  17 us (7%)
    ppermute x12, waiting for transfers between devices, swap_blocks(): lax.ppermute(block, 'dom', pairs)  36.2 us
    pallas_call x1, Pallas kernels, near_forward(): pl.pallas_call(functools.partial(near_forward_kernel, min(window, table.s...  23.4 us
    all_to_all x3, starting transfers between devices, exchange(): lax.all_to_all(blocks, 'dom', 0, 0, axis_index_groups=groups_of(size, axi...  21.2 us
    unnamed x61, local copies, waits for them, and re-layouts  16.7 us
    ppermute x12, starting transfers between devices, swap_blocks(): lax.ppermute(block, 'dom', pairs)  15.8 us
    all_to_all x1, starting transfers between devices, body(): lax.all_to_all(out_rows, 'dom', split_axis=0, concat_axis=0, tiled=True)  14.1 us
    pallas_call x1, Pallas kernels, near_backward(): pl.pallas_call(functools.partial(near_backward_kernel, min(window, rows))...  12.9 us
    all_to_all x1, starting transfers between devices, body(): lax.all_to_all(row_grads.reshape(num_dom, slots, width), 'dom', split_axi...  12.9 us
  transfers between devices with their start and end apart: 21, of which 9 were waited for; matrix products, arithmetic and copies ran while one was open for 11% of the time, Pallas kernels for 27%

profile of v2, /device:TPU:1, one launch (start us, length us, event | category | flops | bytes accessed | tf_op | source)
XLA Modules:
  0.0 230.0 jit_solution(10235906229980608449)
XLA Ops:
  2.0 9.0 %all-to-all-start = ((bf16[8,16,128]{2,1,0:T(8,128)(2,1)}), bf16[8,16,128]{2,1,0:T(8,128)(2,1)S(1)}, u32[]{:S(2)}, u32[]{:S(2)}) async-start(bf16[8,16,128]{2,1,0:T(8,128)(2,1)} %broadcast_in_dim.34), calls=%async_computation | async-start | bytes 65536 | tf_op jit(solution)/shard_map/all_to_all | solution.py:366
  15.2 8.8 %outgoing_rows.1 = bf16[128,64,128]{2,1,0:T(8,128)(2,1)S(1)} custom-call(s32[64,128]{1,0:T(8,128)S(1)} %reshape.65.idx_ref, bf16[1024,128]{1,0:T(8,128)(2,1)S(1)} %copy-done.3), custom_call_target="tpu_custom_call" | custom-call | tf_op jit(solution)/shard_map/outgoing_rows/pallas_call | solution.py:83
  25.4 14.1 %all-to-all-start.1 = ((bf16[128,64,128]{2,1,0:T(8,128)(2,1)}), bf16[128,64,128]{2,1,0:T(8,128)(2,1)S(1)}, u32[]{:S(2)}, u32[]{:S(2)}) async-start(bf16[128,64,128]{2,1,0:T(8,128)(2,1)} %copy-done.1), calls=%async_computation.1 | async-start | bytes 4194304 | tf_op jit(solution)/shard_map/all_to_all | solution.py:426
  43.7 2.8 %collective-permute-start.2 = (bf16[128,128]{1,0:T(8,128)(2,1)S(1)}, bf16[128,128]{1,0:T(8,128)(2,1)S(1)}, u32[]{:S(2)}, u32[]{:S(2)}) collective-permute-start(bf16[128,128]{1,0:T(8,128)(2,1)S(1)} %bitcast.26), channel_id=1, source_target_pairs={{0,128},{2,130},{4,132},{6,134},{8,136},{10,138},{12,140},{14,142}... | collective-permute-start | bytes 98312 | tf_op jit(solution)/shard_map/ppermute | solution.py:379
  47.9 2.3 %collective-permute-done.2 = bf16[128,128]{1,0:T(8,128)(2,1)S(1)} collective-permute-done((bf16[128,128]{1,0:T(8,128)(2,1)S(1)}, bf16[128,128]{1,0:T(8,128)(2,1)S(1)}, u32[]{:S(2)}, u32[]{:S(2)}) %collective-permute-start.2) | collective-permute-done | bytes 32800 | tf_op jit(solution)/shard_map/ppermute | solution.py:379
  50.8 7.7 %sort.14 = (s32[16384]{0:T(1024)S(1)}, s32[16384]{0:T(1024)}) sort(s32[16384]{0:T(1024)S(1)} %and_select_fusion, s32[16384]{0:T(1024)S(1)} %iota.11), dimensions={0}, to_apply=%region_0.1 | sort | flops 229376 | bytes 262144 | tf_op jit(solution)/shard_map/sort | solution.py:459
  62.0 2.0 collective-permute-start.5
  66.7 7.0 %collective-permute-done.5 = bf16[512,128]{1,0:T(8,128)(2,1)S(1)} collective-permute-done((bf16[512,128]{1,0:T(8,128)(2,1)S(1)}, bf16[512,128]{1,0:T(8,128)(2,1)S(1)}, u32[]{:S(2)}, u32[]{:S(2)}) %collective-permute-start.5) | collective-permute-done | bytes 131104 | tf_op jit(solution)/shard_map/ppermute | solution.py:379
  76.6 23.4 %near_forward.1 = (f32[1024,128]{1,0:T(8,128)S(1)}, f32[16,128]{1,0:T(8,128)S(1)}) custom-call(s32[2]{0:T(128)S(1)} %pad_add_fusion.1.count_ref, s32[64]{0:T(128)S(1)} %fusion.28.low_ref, s32[64]{0:T(128)S(1)} %broadcast_shift-right-arithmetic_fusion.high_ref, s32[64,256]{1,0:T(8,128)S(1)} %pad_add_fusion.every_ref, s32[64,256]{1,0:T(8,128)S(1)} %reshape.66.keys_ref, ...), custom_call_target="tpu_custom_call" | custom-call | tf_op jit(solution)/shard_map/near_forward/pallas_call | solution.py:163
  102.0 9.0 %far_forward.1.mine_ref = f32[1024,128]{1,0:T(8,128)S(1)} custom-call(s32[2]{0:T(128)S(1)} %copy-done.12, s32[64]{0:T(128)S(1)} %copy-done.17, s32[64]{0:T(128)S(1)} %copy-done.15, s32[64,256]{1,0:T(8,128)S(1)} %reshape.66.keys_ref, bf16[8192,128]{1,0:T(8,128)(2,1)S(1)} %bitcast.19, f32[1024,128]{1,0:T(8,128)S(1)} %get-tuple-element.27.base_ref), custom_call_target="tpu_custom_call" | custom-call | tf_op jit(solution)/shard_map/far_forward/pallas_call | solution.py:190
  111.0 3.3 %collective-permute-start.7 = (f32[1024,128]{1,0:T(8,128)S(1)}, f32[1024,128]{1,0:T(8,128)S(1)}, u32[]{:S(2)}, u32[]{:S(2)}) collective-permute-start(f32[1024,128]{1,0:T(8,128)S(1)} %far_forward.1.mine_ref), channel_id=1, source_target_pairs={{0,1},{1,0},{2,3},{3,2},{4,5},{5,4},{6,7},{7,6},{8,9},{9,8},{10,11... | collective-permute-start | bytes 1572872 | tf_op jit(solution)/shard_map/ppermute | solution.py:475
  118.2 2.4 %dense_part.1 = (bf16[1024,128]{1,0:T(8,128)(2,1)}, bf16[1024,128]{1,0:T(8,128)(2,1)S(1)}, f32[1024,128]{1,0:T(8,128)S(1)}, f32[192,128]{1,0:T(8,128)}) custom-call(s32[1]{0:T(128)} %bitcast.half_ref, f32[1024,128]{1,0:T(8,128)S(1)} %far_forward.1.mine_ref, f32[1024,128]{1,0:T(8,128)S(1)} %collective-permute-done.7.other_ref, ...), custom_call_target="tpu_custom_call" | custom-call | tf_op jit(solution)/shard_map/dense_part/pallas_call | solution.py:246
  121.4 5.8 %all-to-all-start.2 = ((f32[8,24,128]{2,1,0:T(8,128)}), f32[8,24,128]{2,1,0:T(8,128)S(1)}, u32[]{:S(2)}, u32[]{:S(2)}) async-start(f32[8,24,128]{2,1,0:T(8,128)} %bitcast.11), calls=%async_computation.2 | async-start | bytes 196608 | tf_op jit(solution)/shard_map/all_to_all | solution.py:366
  129.1 9.2 %far_backward.1 = bf16[8192,128]{1,0:T(8,128)(2,1)S(1)} custom-call(s32[2]{0:T(128)S(1)} %copy-done.13, s32[64]{0:T(128)S(1)} %copy-done.18, s32[64]{0:T(128)S(1)} %copy-done.16, s32[64,256]{1,0:T(8,128)S(1)} %reshape.66.keys_ref, bf16[1024,128]{1,0:T(8,128)(2,1)S(1)} %get-tuple-element.31.grad_ref), custom_call_target="tpu_custom_call" | custom-call | tf_op jit(solution)/shard_map/far_backward/pallas_call | solution.py:291
  140.3 12.9 %all-to-all-start.3 = ((bf16[128,64,128]{2,1,0:T(8,128)(2,1)}), bf16[128,64,128]{2,1,0:T(8,128)(2,1)S(1)}, u32[]{:S(2)}, u32[]{:S(2)}) async-start(bf16[128,64,128]{2,1,0:T(8,128)(2,1)} %bitcast.20), calls=%async_computation.3 | async-start | bytes 4194304 | tf_op jit(solution)/shard_map/all_to_all | solution.py:491
  154.2 12.9 %near_backward.1.near_ref = f32[2560,128]{1,0:T(8,128)S(1)} custom-call(s32[2]{0:T(128)S(1)} %copy-done.14, s32[64]{0:T(128)S(1)} %copy-done.20, s32[64]{0:T(128)S(1)} %copy-done.22, s32[64,256]{1,0:T(8,128)S(1)} %reshape.66.keys_ref, bf16[1024,128]{1,0:T(8,128)(2,1)S(1)} %copy-done.6), custom_call_target="tpu_custom_call" | custom-call | tf_op jit(solution)/shard_map/near_backward/pallas_call | solution.py:313
  172.1 6.3 %collective-permute-done.9 = f32[536,128]{1,0:T(8,128)S(1)} collective-permute-done((f32[536,128]{1,0:T(8,128)S(1)}, f32[536,128]{1,0:T(8,128)S(1)}, u32[]{:S(2)}, u32[]{:S(2)}) %collective-permute-start.9) | collective-permute-done | bytes 274464 | tf_op jit(solution)/shard_map/ppermute | solution.py:379
  178.4 13.4 %collective-permute-done.10 = f32[536,128]{1,0:T(8,128)S(1)} collective-permute-done((f32[536,128]{1,0:T(8,128)S(1)}, f32[536,128]{1,0:T(8,128)S(1)}, u32[]{:S(2)}, u32[]{:S(2)}) %collective-permute-start.10) | collective-permute-done | bytes 274464 | tf_op jit(solution)/shard_map/ppermute | solution.py:379
  193.3 2.5 %collective-permute-start.13 = (f32[152,128]{1,0:T(8,128)S(1)}, f32[152,128]{1,0:T(8,128)S(1)}, u32[]{:S(2)}, u32[]{:S(2)}) collective-permute-start(f32[152,128]{1,0:T(8,128)S(1)} %get-tuple-element.59), channel_id=1, source_target_pairs={{0,128},{2,130},{4,132},{6,134},{8,136},{10,138},{12,140},{14,142}... | collective-permute-start | bytes 233480 | tf_op jit(solution)/shard_map/ppermute | solution.py:379
  195.9 3.6 %collective-permute-done.13 = f32[152,128]{1,0:T(8,128)S(1)} collective-permute-done((f32[152,128]{1,0:T(8,128)S(1)}, f32[152,128]{1,0:T(8,128)S(1)}, u32[]{:S(2)}, u32[]{:S(2)}) %collective-permute-start.13) | collective-permute-done | bytes 77856 | tf_op jit(solution)/shard_map/ppermute | solution.py:379
  202.2 6.4 %all-to-all-start.4 = ((f32[8,40,128]{2,1,0:T(8,128)}), f32[8,40,128]{2,1,0:T(8,128)}, u32[]{:S(2)}, u32[]{:S(2)}) async-start(f32[8,40,128]{2,1,0:T(8,128)} %pad_maximum_fusion.4), calls=%async_computation.4 | async-start | bytes 327680 | tf_op jit(solution)/shard_map/all_to_all | solution.py:366
  208.6 7.8 %returned_sum.1 = f32[1024,128]{1,0:T(8,128)} custom-call(s32[1]{0:T(128)} %bitcast.half_ref, s32[64,128]{1,0:T(8,128)S(1)} %reshape.65.idx_ref, bf16[128,64,128]{2,1,0:T(8,128)(2,1)S(1)} %all-to-all-done.3.back_ref, f32[2560,128]{1,0:T(8,128)S(1)} %near_backward.1.near_ref), custom_call_target="tpu_custom_call" | custom-call | tf_op jit(solution)/shard_map/returned_sum/pallas_call | solution.py:341
  216.4 5.1 %collective-permute-start.8 = (f32[1024,128]{1,0:T(8,128)}, f32[1024,128]{1,0:T(8,128)S(1)}, u32[]{:S(2)}, u32[]{:S(2)}) collective-permute-start(f32[1024,128]{1,0:T(8,128)} %returned_sum.1), channel_id=1, source_target_pairs={{0,1},{1,0},{2,3},{3,2},{4,5},{5,4},{6,7},{7,6},{8,9},{9,8},{10,11... | collective-permute-start | bytes 1572872 | tf_op jit(solution)/shard_map/ppermute | solution.py:514
  227.9 2.1 add_add_fusion
  (135 shorter events, 48.4 us)
Async XLA Ops:
  2.0 23.4 %all-to-all-start = ((bf16[8,16,128]{2,1,0:T(8,128)(2,1)}), bf16[8,16,128]{2,1,0:T(8,128)(2,1)S(1)}, u32[]{:S(2)}, u32[]{:S(2)}) async-start(bf16[8,16,128]{2,1,0:T(8,128)(2,1)} %broadcast_in_dim.34), calls=%async_computation | async-start | bytes 65536 | tf_op jit(solution)/shard_map/all_to_all | solution.py:366
  25.4 74.6 %all-to-all-start.1 = ((bf16[128,64,128]{2,1,0:T(8,128)(2,1)}), bf16[128,64,128]{2,1,0:T(8,128)(2,1)S(1)}, u32[]{:S(2)}, u32[]{:S(2)}) async-start(bf16[128,64,128]{2,1,0:T(8,128)(2,1)} %copy-done.1), calls=%async_computation.1 | async-start | bytes 4194304 | tf_op jit(solution)/shard_map/all_to_all | solution.py:426
  41.0 6.2 %collective-permute-start = (s32[8192]{0:T(1024)S(1)}, s32[8192]{0:T(1024)S(1)}, u32[]{:S(2)}, u32[]{:S(2)}) collective-permute-start(s32[8192]{0:T(1024)S(1)} %fusion.11), channel_id=1, source_target_pairs={{0,1},{1,0},{2,3},{3,2},{4,5},{5,4},{6,7},{7,6},{8,9},{9,8},{10,11... | collective-permute-start | bytes 98312 | tf_op jit(solution)/shard_map/ppermute | solution.py:456
  42.6 4.6 %collective-permute-start.1 = (bf16[128,128]{1,0:T(8,128)(2,1)S(1)}, bf16[128,128]{1,0:T(8,128)(2,1)S(1)}, u32[]{:S(2)}, u32[]{:S(2)}) collective-permute-start(bf16[128,128]{1,0:T(8,128)(2,1)S(1)} %bitcast.25), channel_id=1, source_target_pairs={{0,64},{2,66},{4,68},{6,70},{8,72},{10,74},{12,76},{14,78},{16,80}... | collective-permute-start | bytes 98312 | tf_op jit(solution)/shard_map/ppermute | solution.py:379
  43.7 6.5 %collective-permute-start.2 = (bf16[128,128]{1,0:T(8,128)(2,1)S(1)}, bf16[128,128]{1,0:T(8,128)(2,1)S(1)}, u32[]{:S(2)}, u32[]{:S(2)}) collective-permute-start(bf16[128,128]{1,0:T(8,128)(2,1)S(1)} %bitcast.26), channel_id=1, source_target_pairs={{0,128},{2,130},{4,132},{6,134},{8,136},{10,138},{12,140},{14,142}... | collective-permute-start | bytes 98312 | tf_op jit(solution)/shard_map/ppermute | solution.py:379
  46.5 12.0 %collective-permute-start.3 = (bf16[128,128]{1,0:T(8,128)(2,1)S(1)}, bf16[128,128]{1,0:T(8,128)(2,1)S(1)}, u32[]{:S(2)}, u32[]{:S(2)}) collective-permute-start(bf16[128,128]{1,0:T(8,128)(2,1)S(1)} %bitcast.27), channel_id=1, source_target_pairs={{0,192},{2,194},{4,196},{6,198},{8,200},{10,202},{12,204},{14,206}... | collective-permute-start | bytes 98312 | tf_op jit(solution)/shard_map/ppermute | solution.py:379
  59.2 6.8 %collective-permute-start.4 = (bf16[512,128]{1,0:T(8,128)(2,1)S(1)}, bf16[512,128]{1,0:T(8,128)(2,1)S(1)}, u32[]{:S(2)}, u32[]{:S(2)}) collective-permute-start(bf16[512,128]{1,0:T(8,128)(2,1)S(1)} %get-tuple-element.51), channel_id=1, source_target_pairs={{0,2},{2,0},{4,6},{6,4},{8,10},{10,8},{12,14},{14,12},{16,18},{18,... | collective-permute-start | bytes 393224 | tf_op jit(solution)/shard_map/ppermute | solution.py:379
  61.3 38.7 %copy-start.21 = (s32[64]{0:T(128)}, s32[64]{0:T(128)S(1)}, u32[]{:S(2)}) copy-start(s32[64]{0:T(128)S(1)} %broadcast_shift-right-arithmetic_fusion.high_ref) | copy-start | bytes 772
  62.0 38.1 %copy-start.19 = (s32[64]{0:T(128)}, s32[64]{0:T(128)S(1)}, u32[]{:S(2)}) copy-start(s32[64]{0:T(128)S(1)} %fusion.28.low_ref) | copy-start | bytes 772
  62.0 11.7 %collective-permute-start.5 = (bf16[512,128]{1,0:T(8,128)(2,1)S(1)}, bf16[512,128]{1,0:T(8,128)(2,1)S(1)}, u32[]{:S(2)}, u32[]{:S(2)}) collective-permute-start(bf16[512,128]{1,0:T(8,128)(2,1)S(1)} %get-tuple-element.51), channel_id=1, source_target_pairs={{0,4},{2,6},{4,0},{6,2},{8,12},{10,14},{12,8},{14,10},{16,20},{18,... | collective-permute-start | bytes 393224 | tf_op jit(solution)/shard_map/ppermute | solution.py:379
  64.0 12.0 %collective-permute-start.6 = (bf16[512,128]{1,0:T(8,128)(2,1)S(1)}, bf16[512,128]{1,0:T(8,128)(2,1)S(1)}, u32[]{:S(2)}, u32[]{:S(2)}) collective-permute-start(bf16[512,128]{1,0:T(8,128)(2,1)S(1)} %get-tuple-element.51), channel_id=1, source_target_pairs={{0,6},{2,4},{4,2},{6,0},{8,14},{10,12},{12,10},{14,8},{16,22},{18,... | collective-permute-start | bytes 393224 | tf_op jit(solution)/shard_map/ppermute | solution.py:379
  74.3 41.5 %copy-start.9 = (bf16[128,128]{1,0:T(8,128)(2,1)S(1)}, bf16[128,128]{1,0:T(8,128)(2,1)}, u32[]{:S(2)}) copy-start(bf16[128,128]{1,0:T(8,128)(2,1)} %w_self_ref.1) | copy-start | bytes 98308
  111.0 4.8 %collective-permute-start.7 = (f32[1024,128]{1,0:T(8,128)S(1)}, f32[1024,128]{1,0:T(8,128)S(1)}, u32[]{:S(2)}, u32[]{:S(2)}) collective-permute-start(f32[1024,128]{1,0:T(8,128)S(1)} %far_forward.1.mine_ref), channel_id=1, source_target_pairs={{0,1},{1,0},{2,3},{3,2},{4,5},{5,4},{6,7},{7,6},{8,9},{9,8},{10,11... | collective-permute-start | bytes 1572872 | tf_op jit(solution)/shard_map/ppermute | solution.py:475
  121.4 18.3 %all-to-all-start.2 = ((f32[8,24,128]{2,1,0:T(8,128)}), f32[8,24,128]{2,1,0:T(8,128)S(1)}, u32[]{:S(2)}, u32[]{:S(2)}) async-start(f32[8,24,128]{2,1,0:T(8,128)} %bitcast.11), calls=%async_computation.2 | async-start | bytes 196608 | tf_op jit(solution)/shard_map/all_to_all | solution.py:366
  140.3 61.9 %all-to-all-start.3 = ((bf16[128,64,128]{2,1,0:T(8,128)(2,1)}), bf16[128,64,128]{2,1,0:T(8,128)(2,1)S(1)}, u32[]{:S(2)}, u32[]{:S(2)}) async-start(bf16[128,64,128]{2,1,0:T(8,128)(2,1)} %bitcast.20), calls=%async_computation.3 | async-start | bytes 4194304 | tf_op jit(solution)/shard_map/all_to_all | solution.py:491
  168.1 10.3 %collective-permute-start.9 = (f32[536,128]{1,0:T(8,128)S(1)}, f32[536,128]{1,0:T(8,128)S(1)}, u32[]{:S(2)}, u32[]{:S(2)}) collective-permute-start(f32[536,128]{1,0:T(8,128)S(1)} %get-tuple-element.62), channel_id=1, source_target_pairs={{0,2},{2,0},{4,6},{6,4},{8,10},{10,8},{12,14},{14,12},{16,18},{18,... | collective-permute-start | bytes 823304 | tf_op jit(solution)/shard_map/ppermute | solution.py:379
  169.5 22.3 %collective-permute-start.10 = (f32[536,128]{1,0:T(8,128)S(1)}, f32[536,128]{1,0:T(8,128)S(1)}, u32[]{:S(2)}, u32[]{:S(2)}) collective-permute-start(f32[536,128]{1,0:T(8,128)S(1)} %get-tuple-element.63), channel_id=1, source_target_pairs={{0,4},{2,6},{4,0},{6,2},{8,12},{10,14},{12,8},{14,10},{16,20},{18,... | collective-permute-start | bytes 823304 | tf_op jit(solution)/shard_map/ppermute | solution.py:379
  171.1 20.8 %collective-permute-start.11 = (f32[536,128]{1,0:T(8,128)S(1)}, f32[536,128]{1,0:T(8,128)S(1)}, u32[]{:S(2)}, u32[]{:S(2)}) collective-permute-start(f32[536,128]{1,0:T(8,128)S(1)} %get-tuple-element.61), channel_id=1, source_target_pairs={{0,6},{2,4},{4,2},{6,0},{8,14},{10,12},{12,10},{14,8},{16,22},{18,... | collective-permute-start | bytes 823304 | tf_op jit(solution)/shard_map/ppermute | solution.py:379
  192.0 4.0 %collective-permute-start.12 = (f32[152,128]{1,0:T(8,128)S(1)}, f32[152,128]{1,0:T(8,128)S(1)}, u32[]{:S(2)}, u32[]{:S(2)}) collective-permute-start(f32[152,128]{1,0:T(8,128)S(1)} %get-tuple-element.60), channel_id=1, source_target_pairs={{0,64},{2,66},{4,68},{6,70},{8,72},{10,74},{12,76},{14,78},{16,80}... | collective-permute-start | bytes 233480 | tf_op jit(solution)/shard_map/ppermute | solution.py:379
  193.3 6.3 %collective-permute-start.13 = (f32[152,128]{1,0:T(8,128)S(1)}, f32[152,128]{1,0:T(8,128)S(1)}, u32[]{:S(2)}, u32[]{:S(2)}) collective-permute-start(f32[152,128]{1,0:T(8,128)S(1)} %get-tuple-element.59), channel_id=1, source_target_pairs={{0,128},{2,130},{4,132},{6,134},{8,136},{10,138},{12,140},{14,142}... | collective-permute-start | bytes 233480 | tf_op jit(solution)/shard_map/ppermute | solution.py:379
  195.7 5.7 %collective-permute-start.14 = (f32[152,128]{1,0:T(8,128)S(1)}, f32[152,128]{1,0:T(8,128)S(1)}, u32[]{:S(2)}, u32[]{:S(2)}) collective-permute-start(f32[152,128]{1,0:T(8,128)S(1)} %concatenate.67), channel_id=1, source_target_pairs={{0,192},{2,194},{4,196},{6,198},{8,200},{10,202},{12,204},{14,206}... | collective-permute-start | bytes 233480 | tf_op jit(solution)/shard_map/ppermute | solution.py:379
  202.2 19.3 %all-to-all-start.4 = ((f32[8,40,128]{2,1,0:T(8,128)}), f32[8,40,128]{2,1,0:T(8,128)}, u32[]{:S(2)}, u32[]{:S(2)}) async-start(f32[8,40,128]{2,1,0:T(8,128)} %pad_maximum_fusion.4), calls=%async_computation.4 | async-start | bytes 327680 | tf_op jit(solution)/shard_map/all_to_all | solution.py:366
  216.4 11.5 %collective-permute-start.8 = (f32[1024,128]{1,0:T(8,128)}, f32[1024,128]{1,0:T(8,128)S(1)}, u32[]{:S(2)}, u32[]{:S(2)}) collective-permute-start(f32[1024,128]{1,0:T(8,128)} %returned_sum.1), channel_id=1, source_target_pairs={{0,1},{1,0},{2,3},{3,2},{4,5},{5,4},{6,7},{7,6},{8,9},{9,8},{10,11... | collective-permute-start | bytes 1572872 | tf_op jit(solution)/shard_map/ppermute | solution.py:514
  223.3 2.7 %collective-permute-start.15 = (f32[144,128]{1,0:T(8,128)S(1)}, f32[144,128]{1,0:T(8,128)S(1)}, u32[]{:S(2)}, u32[]{:S(2)}) collective-permute-start(f32[144,128]{1,0:T(8,128)S(1)} %pad_maximum_fusion.8), channel_id=1, source_target_pairs={{0,1},{1,0},{2,3},{3,2},{4,5},{5,4},{6,7},{7,6},{8,9},{9,8},{10,11... | collective-permute-start | bytes 221192 | tf_op jit(solution)/shard_map/ppermute | solution.py:516
  (24 other events, 151.6 us)

commit v3 on v2

--- a/solution.py
+++ b/solution.py
@@ -10,14 +10,17 @@
 
 F32 = jnp.float32
 BF16 = jnp.bfloat16
+I16 = jnp.int16
 VMEM = pltpu.VMEM
 SMEM = pltpu.SMEM
 SWAP = [(0, 1), (1, 0)]
 CHUNK = 256
+UNROLL = 4
 DST_BITS = 10
 PAD = 1 << 30
 DEAD = 1 << 26
 HALF_BIT = 24
+META = NEAR_LOW, NEAR_HIGH, FAR_LOW, FAR_HIGH, COUNTS = 0, 1, 2, 3, 4
 
 
 def params(mib=40):
@@ -40,16 +43,16 @@
 
 
 def onehot_of_columns(col, width):
-    lane = lax.broadcasted_iota(jnp.int32, col.shape, 1)
-    parts = [
-        jnp.where(col == lane + at, 1.0, 0.0).astype(BF16) for at in range(0, width, 128)
-    ]
-    return jnp.concatenate(parts, axis=1)
+    lane = lax.broadcasted_iota(jnp.int32, col.shape, 1).astype(I16)
+    col = col.astype(I16)
+    one, zero = jnp.ones((), BF16), jnp.zeros((), BF16)
+    parts = [jnp.where(col == lane + I16(at), one, zero) for at in range(0, width, 128)]
+    return parts[0] if len(parts) == 1 else jnp.concatenate(parts, axis=1)
 
 
 def onehot_of_rows(row, height):
-    sub = lax.broadcasted_iota(jnp.int32, (height, row.shape[1]), 0)
-    return jnp.where(sub == row, 1.0, 0.0).astype(BF16)
+    sub = lax.broadcasted_iota(jnp.int32, (height, row.shape[1]), 0).astype(I16)
+    return jnp.where(sub == row.astype(I16), jnp.ones((), BF16), jnp.zeros((), BF16))
 
 
 def dot(a, b):
@@ -64,24 +67,44 @@
     return lax.dot_general(a, b, (((0,), (0,)), ((), ())), preferred_element_type=F32)
 
 
-def outgoing_kernel(slots, idx_ref, feat_ref, out_ref):
+def pick(col, wide):
+    rows = wide.shape[0]
+    both = dot(onehot_of_columns(jnp.where(col >= rows, col - rows, col), rows), wide)
+    return jnp.where(col >= rows, both[:, 128:], both[:, :128])
+
+
+def spread(row, col, values, rows):
+    left = col.astype(I16) < I16(rows)
+    zero = jnp.zeros((), BF16)
+    pair = jnp.concatenate([jnp.where(left, values, zero), jnp.where(left, zero, values)], axis=1)
+    return dot(onehot_of_rows(jnp.where(row >= rows, row - rows, row), rows), pair)
+
+
+def join(refs_at):
+    return jnp.concatenate(refs_at, axis=1)
+
+
+def outgoing_kernel(idx_ref, feat_ref, out_ref, wide_ref):
     step = pl.program_id(0)
-    peers = out_ref.shape[0]
-    rows = feat_ref.shape[0]
-    for pair in range(peers // 4):
-        at = step * (peers // 2) + pair * 2
-        idx = [idx_ref[pl.ds(at + k, 1), :] for k in range(2)]
-        hot = onehot_of_columns(columns_of(jnp.concatenate(idx, axis=1)), rows)
-        picked = dot(hot, feat_ref[...]).astype(BF16)
-        for k in range(4):
-            out_ref[pair * 4 + k, :, :] = picked[k * slots : (k + 1) * slots]
-
-
-def outgoing(idx, feats, slots, step_peers=8):
+    peers, slots, width = out_ref.shape
+    nodes = feat_ref.shape[0]
+    lines = peers * slots // 128
+
+    @pl.when(step == 0)
+    def _():
+        wide_ref[:, :width] = feat_ref[: nodes // 2, :]
+        wide_ref[:, width:] = feat_ref[nodes // 2 :, :]
+
+    row = join([idx_ref[pl.ds(step * lines + k, 1), :] for k in range(lines)])
+    out_ref[...] = pick(columns_of(row), wide_ref[...]).astype(BF16).reshape(peers, slots, width)
+
+
+def outgoing(idx, feats, slots, step_peers=32):
     peers = idx.shape[0] * idx.shape[1] // slots
-    width = feats.shape[1]
+    nodes, width = feats.shape
+    step_peers = min(step_peers, peers)
     return pl.pallas_call(
-        functools.partial(outgoing_kernel, slots),
+        outgoing_kernel,
         grid=(peers // step_peers,),
         in_specs=[
             pl.BlockSpec(idx.shape, lambda i: (0, 0)),
@@ -89,59 +112,110 @@
         ],
         out_specs=pl.BlockSpec((step_peers, slots, width), lambda i: (i, 0, 0)),
         out_shape=jax.ShapeDtypeStruct((peers, slots, width), BF16),
+        scratch_shapes=[VMEM((nodes // 2, 2 * width), BF16)],
         compiler_params=params(),
         name="outgoing_rows",
     )(idx, feats)
 
 
-def over_windows(c, low_ref, high_ref, rows, window, visit):
-    low = low_ref[c] // 128 * 128
-
-    def step(w, _):
-        base = low + w * window
-        visit(pl.multiple_of(jnp.minimum(base, rows - window), 128), base)
+def relative(row, base, start, window):
+    return jnp.where((row >= base) & (row < start + window), row - start, -1)
+
+
+def window_of(meta_ref, low_at, c, w, rows, window):
+    base = meta_ref[low_at, c] // 128 * 128 + w * window
+    return base, pl.multiple_of(jnp.minimum(base, rows - window), 128)
+
+
+def windows_of(meta_ref, low_at, c, window):
+    return (meta_ref[low_at + 1, c] - meta_ref[low_at, c] // 128 * 128) // window + 1
+
+
+def keys_of(keys_ref, c, end):
+    at = jnp.minimum(c, keys_ref.shape[0] - 1)
+    return at, jnp.where(c < end, keys_ref[pl.ds(at, 1), :], PAD)
+
+
+def gather_add(first, end, offset, window, low_at, meta_ref, keys_ref, table_ref, sum_ref, values_ref):
+    half_nodes = sum_ref.shape[0]
+    rows = table_ref.shape[0]
+    half = window // 2
+
+    def picked(c, w, col):
+        base, start = window_of(meta_ref, low_at, c, w, rows, window)
+        wide = join([table_ref[pl.ds(start, half), :], table_ref[pl.ds(start + half, half), :]])
+        return pick(relative((col >> DST_BITS) - offset, base, start, window), wide)
+
+    keys, cols = [], []
+    for u in range(UNROLL):
+        c, key = keys_of(keys_ref, first + u, end)
+        keys.append(key)
+        cols.append(columns_of(key))
+        values_ref[u * CHUNK : (u + 1) * CHUNK, :] = picked(c, 0, cols[u])
+    for u in range(UNROLL):
+        c, key = keys_of(keys_ref, first + u, end)
+
+        def more(w, _, c=c, key=key, u=u):
+            values_ref[u * CHUNK : (u + 1) * CHUNK, :] += picked(c, w, columns_of(key))
+            return 0
+
+        lax.fori_loop(1, windows_of(meta_ref, low_at, c, window), more, 0)
+    nodes = 2 * half_nodes
+    sum_ref[...] += spread(
+        join(keys) & (nodes - 1),
+        jnp.concatenate(cols, axis=0) & (nodes - 1),
+        values_ref[...].astype(BF16),
+        half_nodes,
+    )
+
+
+def spread_add(first, end, offset, window, low_at, meta_ref, keys_ref, grad_ref, acc_ref, values_ref):
+    nodes = 2 * grad_ref.shape[0]
+    rows = acc_ref.shape[0]
+    half = window // 2
+
+    def add(c, w, key, col, values):
+        base, start = window_of(meta_ref, low_at, c, w, rows, window)
+        row, col = (
+            relative((k >> DST_BITS) - offset, base, start, window) for k in (key, col)
+        )
+        both = spread(row, col, values, half)
+        acc_ref[pl.ds(start, half), :] += both[:, :128]
+        acc_ref[pl.ds(start + half, half), :] += both[:, 128:]
+
+    keys = [keys_of(keys_ref, first + u, end) for u in range(UNROLL)]
+    cols = [columns_of(key) for _, key in keys]
+    values = pick(jnp.concatenate(cols, axis=0) & (nodes - 1), grad_ref[...]).astype(BF16)
+    values_ref[...] = values
+    for u, (c, key) in enumerate(keys):
+        add(c, 0, key, cols[u], values[u * CHUNK : (u + 1) * CHUNK])
+    for u in range(UNROLL):
+        c, key = keys_of(keys_ref, first + u, end)
+
+        def more(w, _, c=c, key=key, u=u):
+            add(c, w, key, columns_of(key), values_ref[u * CHUNK : (u + 1) * CHUNK, :])
+            return 0
+
+        lax.fori_loop(1, windows_of(meta_ref, low_at, c, window), more, 0)
+
+
+def over_chunks(first, end, visit):
+    def step(i, _):
+        visit(first + i * UNROLL)
         return 0
 
-    lax.fori_loop(0, (high_ref[c] - low) // window + 1, step, 0)
-
-
-def gather_add(c, offset, window, low_ref, high_ref, keys_ref, table_ref, sum_ref, values_ref):
-    nodes = sum_ref.shape[0]
-    key = keys_ref[pl.ds(c, 1), :]
-    row = (key >> DST_BITS) - offset
-    values_ref[...] = jnp.zeros_like(values_ref)
-
-    def visit(start, base):
-        hot = onehot_of_columns(columns_of(jnp.where(row >= base, row - start, -1)), window)
-        values_ref[...] += dot(hot, table_ref[pl.ds(start, window), :])
-
-    over_windows(c, low_ref, high_ref, table_ref.shape[0], window, visit)
-    sum_ref[...] += dot(onehot_of_rows(key & (nodes - 1), nodes), values_ref[...].astype(BF16))
-
-
-def spread_add(c, offset, window, low_ref, high_ref, keys_ref, grad_ref, acc_ref):
-    nodes = grad_ref.shape[0]
-    key = keys_ref[pl.ds(c, 1), :]
-    row = (key >> DST_BITS) - offset
-    hot = onehot_of_columns(columns_of(key & (nodes - 1)), nodes)
-    values = dot(hot, grad_ref[...]).astype(BF16)
-
-    def visit(start, base):
-        hot = onehot_of_rows(jnp.where(row >= base, row - start, -1), window)
-        acc_ref[pl.ds(start, window), :] += dot(hot, values)
-
-    over_windows(c, low_ref, high_ref, acc_ref.shape[0], window, visit)
+    lax.fori_loop(0, pl.cdiv(end - first, UNROLL), step, 0)
 
 
 def near_forward_kernel(
-    window, count_ref, low_ref, high_ref, every_ref, keys_ref, table_ref, sum_ref, deg_ref, values_ref
+    window, meta_ref, every_ref, keys_ref, table_ref, sum_ref, deg_ref, values_ref
 ):
-    nodes = sum_ref.shape[0]
+    nodes = 2 * sum_ref.shape[0]
     deg_ref[...] = jnp.zeros_like(deg_ref)
     sum_ref[...] = jnp.zeros_like(sum_ref)
 
     def degrees(c, _):
-        key = every_ref[pl.ds(c, 1), :]
+        key = join([every_ref[pl.ds(c * UNROLL + u, 1), :] for u in range(UNROLL)])
         dst = key & (nodes - 1)
         high = jnp.where(key < DEAD, dst >> 7, deg_ref.shape[0])
         deg_ref[...] += dot_nt(
@@ -149,53 +223,57 @@
         )
         return 0
 
-    lax.fori_loop(0, every_ref.shape[0], degrees, 0)
-
-    def chunk(c, _):
-        gather_add(c, 0, window, low_ref, high_ref, keys_ref, table_ref, sum_ref, values_ref)
-        return 0
-
-    lax.fori_loop(0, pl.cdiv(count_ref[0], CHUNK), chunk, 0)
-
-
-def near_forward(counts, low, high, every, keys, table, nodes, window=640):
+    lax.fori_loop(0, every_ref.shape[0] // UNROLL, degrees, 0)
+    end = pl.cdiv(meta_ref[COUNTS, 0], CHUNK)
+    over_chunks(
+        0,
+        end,
+        lambda c: gather_add(
+            c, end, 0, window, NEAR_LOW, meta_ref, keys_ref, table_ref, sum_ref, values_ref
+        ),
+    )
+
+
+def near_forward(meta, every, keys, table, nodes, window=768):
     width = table.shape[1]
     return pl.pallas_call(
         functools.partial(near_forward_kernel, min(window, table.shape[0])),
-        in_specs=[sspec(), sspec(), sspec(), vspec(), vspec(), vspec()],
+        in_specs=[sspec(), vspec(), vspec(), vspec()],
         out_specs=[vspec(), vspec()],
         out_shape=[
-            jax.ShapeDtypeStruct((nodes, width), F32),
+            jax.ShapeDtypeStruct((nodes // 2, 2 * width), F32),
             jax.ShapeDtypeStruct((16, 128), F32),
         ],
-        scratch_shapes=[VMEM((CHUNK, width), F32)],
+        scratch_shapes=[VMEM((UNROLL * CHUNK, width), F32)],
         compiler_params=params(),
         name="near_forward",
-    )(counts, low, high, every, keys, table)
+    )(meta, every, keys, table)
 
 
 def far_forward_kernel(
-    offset, window, count_ref, low_ref, high_ref, keys_ref, table_ref, base_ref, sum_ref, values_ref
+    offset, window, meta_ref, keys_ref, table_ref, base_ref, sum_ref, values_ref
 ):
     sum_ref[...] = base_ref[...]
-
-    def chunk(c, _):
-        gather_add(c, offset, window, low_ref, high_ref, keys_ref, table_ref, sum_ref, values_ref)
-        return 0
-
-    lax.fori_loop(count_ref[0] // CHUNK, pl.cdiv(count_ref[1], CHUNK), chunk, 0)
-
-
-def far_forward(counts, low, high, keys, table, base, offset, window=1280):
+    end = pl.cdiv(meta_ref[COUNTS, 1], CHUNK)
+    over_chunks(
+        meta_ref[COUNTS, 0] // CHUNK,
+        end,
+        lambda c: gather_add(
+            c, end, offset, window, FAR_LOW, meta_ref, keys_ref, table_ref, sum_ref, values_ref
+        ),
+    )
+
+
+def far_forward(meta, keys, table, base, offset, window=1280):
     return pl.pallas_call(
         functools.partial(far_forward_kernel, offset, min(window, table.shape[0])),
-        in_specs=[sspec(), sspec(), sspec(), vspec(), vspec(), vspec()],
+        in_specs=[sspec(), vspec(), vspec(), vspec()],
         out_specs=vspec(),
         out_shape=jax.ShapeDtypeStruct(base.shape, F32),
-        scratch_shapes=[VMEM((CHUNK, base.shape[1]), F32)],
+        scratch_shapes=[VMEM((UNROLL * CHUNK, table.shape[1]), F32)],
         compiler_params=params(),
         name="far_forward",
-    )(counts, low, high, keys, table, base)
+    )(meta, keys, table, base)
 
 
 def dense_kernel(
@@ -222,14 +300,15 @@
         h = at // 128
         divisor = jnp.maximum(columns_of(deg_ref[h : h + 1, :]), 1.0)
         feats = feat_ref[span, :]
-        aggregate = ((mine_ref[span, :] + other_ref[span, :]) / divisor).astype(BF16)
+        place = (pl.ds(at % (nodes // 2), 128), pl.ds(at // (nodes // 2) * 128, 128))
+        aggregate = ((mine_ref[place] + other_ref[place]) / divisor).astype(BF16)
         preact = dot(feats, w_self_ref[...]) + dot(aggregate, w_neigh_ref[...]) + bias_ref[...]
         sig = jax.nn.sigmoid(preact)
         out_ref[span, :] = (preact * sig).astype(BF16)
         slope = sig * (1.0 + preact * (1.0 - sig))
         grad_pre = (cot_ref[span, :].astype(F32) * slope).astype(BF16)
         pre_ref[span, :] = grad_pre
-        grad_sum_ref[span, :] = (dot_nt(grad_pre, w_neigh_ref[...]) / divisor).astype(BF16)
+        grad_sum_ref[place] = (dot_nt(grad_pre, w_neigh_ref[...]) / divisor).astype(BF16)
         grad_input_ref[span, :] = dot_nt(grad_pre, w_self_ref[...])
         left_ref[span, :] = jnp.where(half_ref[0] == 0, feats.astype(F32), aggregate.astype(F32)).astype(BF16)
         wide = grad_pre.astype(F32)
@@ -249,7 +328,7 @@
         out_specs=[vspec()] * 4,
         out_shape=[
             jax.ShapeDtypeStruct((nodes, width), BF16),
-            jax.ShapeDtypeStruct((nodes, width), BF16),
+            jax.ShapeDtypeStruct((nodes // 2, 2 * width), BF16),
             jax.ShapeDtypeStruct((nodes, width), F32),
             jax.ShapeDtypeStruct((192, width), F32),
         ],
@@ -259,9 +338,7 @@
     )(half, mine, other, deg, feats, cot, w_self, w_neigh, bias)
 
 
-def far_backward_kernel(
-    offset, window, count_ref, low_ref, high_ref, keys_ref, grad_ref, out_ref, acc_ref
-):
+def far_backward_kernel(offset, window, meta_ref, keys_ref, grad_ref, out_ref, acc_ref, values_ref):
     rows = acc_ref.shape[0]
     block = min(512, rows)
 
@@ -271,12 +348,14 @@
         return 0
 
     lax.fori_loop(0, rows // block, clear, 0)
-
-    def chunk(c, _):
-        spread_add(c, offset, window, low_ref, high_ref, keys_ref, grad_ref, acc_ref)
-        return 0
-
-    lax.fori_loop(count_ref[0] // CHUNK, pl.cdiv(count_ref[1], CHUNK), chunk, 0)
+    end = pl.cdiv(meta_ref[COUNTS, 1], CHUNK)
+    over_chunks(
+        meta_ref[COUNTS, 0] // CHUNK,
+        end,
+        lambda c: spread_add(
+            c, end, offset, window, FAR_LOW, meta_ref, keys_ref, grad_ref, acc_ref, values_ref
+        ),
+    )
 
     def finish(b, _):
         span = pl.ds(pl.multiple_of(b * block, block), block)
@@ -286,63 +365,72 @@
     lax.fori_loop(0, rows // block, finish, 0)
 
 
-def far_backward(counts, low, high, keys, grad_sum, offset, rows, window=1280):
-    width = grad_sum.shape[1]
+def far_backward(meta, keys, grad_sum, offset, rows, window=1280):
+    width = grad_sum.shape[1] // 2
     return pl.pallas_call(
         functools.partial(far_backward_kernel, offset, min(window, rows)),
-        in_specs=[sspec(), sspec(), sspec(), vspec(), vspec()],
+        in_specs=[sspec(), vspec(), vspec()],
         out_specs=vspec(),
         out_shape=jax.ShapeDtypeStruct((rows, width), BF16),
-        scratch_shapes=[VMEM((rows, width), F32)],
+        scratch_shapes=[VMEM((rows, width), F32), VMEM((UNROLL * CHUNK, width), BF16)],
         compiler_params=params(),
         name="far_backward",
-    )(counts, low, high, keys, grad_sum)
-
-
-def near_backward_kernel(window, count_ref, low_ref, high_ref, keys_ref, grad_ref, out_ref):
+    )(meta, keys, grad_sum)
+
+
+def near_backward_kernel(window, meta_ref, keys_ref, grad_ref, out_ref, values_ref):
     out_ref[...] = jnp.zeros_like(out_ref)
-
-    def chunk(c, _):
-        spread_add(c, 0, window, low_ref, high_ref, keys_ref, grad_ref, out_ref)
-        return 0
-
-    lax.fori_loop(0, pl.cdiv(count_ref[0], CHUNK), chunk, 0)
-
-
-def near_backward(counts, low, high, keys, grad_sum, rows, window=640):
+    end = pl.cdiv(meta_ref[COUNTS, 0], CHUNK)
+    over_chunks(
+        0,
+        end,
+        lambda c: spread_add(
+            c, end, 0, window, NEAR_LOW, meta_ref, keys_ref, grad_ref, out_ref, values_ref
+        ),
+    )
+
+
+def near_backward(meta, keys, grad_sum, rows, window=768):
+    width = grad_sum.shape[1] // 2
     return pl.pallas_call(
         functools.partial(near_backward_kernel, min(window, rows)),
-        in_specs=[sspec(), sspec(), sspec(), vspec(), vspec()],
+        in_specs=[sspec(), vspec(), vspec()],
         out_specs=vspec(),
-        out_shape=jax.ShapeDtypeStruct((rows, grad_sum.shape[1]), F32),
+        out_shape=jax.ShapeDtypeStruct((rows, width), F32),
+        scratch_shapes=[VMEM((UNROLL * CHUNK, width), BF16)],
         compiler_params=params(),
         name="near_backward",
-    )(counts, low, high, keys, grad_sum)
-
-
-def returned_kernel(half_ref, idx_ref, back_ref, near_ref, part_ref):
+    )(meta, keys, grad_sum)
+
+
+def returned_kernel(peers_step, half_ref, idx_ref, back_ref, near_ref, part_ref, acc_ref):
     nodes = part_ref.shape[0]
     own_rows = nodes // 2
     peers, slots, width = back_ref.shape
-    part_ref[...] = jnp.zeros_like(part_ref)
+    lines = peers_step * slots // 128
+    acc_ref[...] = jnp.zeros_like(acc_ref)
+
+    def step(s, _):
+        row = join([idx_ref[pl.ds(s * lines + k, 1), :] for k in range(lines)])
+        rows = back_ref[pl.ds(s * peers_step, peers_step), :, :].reshape(peers_step * slots, width)
+        acc_ref[...] += spread(row, columns_of(row), rows, own_rows)
+        return 0
+
+    lax.fori_loop(0, peers // peers_step, step, 0)
+    part_ref[:own_rows, :] = acc_ref[:, :width]
+    part_ref[own_rows:, :] = acc_ref[:, width:]
     own_span = pl.ds(pl.multiple_of(half_ref[0] * own_rows, own_rows), own_rows)
-    part_ref[own_span, :] = near_ref[:own_rows, :]
-
-    def step(s, _):
-        idx = jnp.concatenate([idx_ref[pl.ds(s * 4 + k, 1), :] for k in range(4)], axis=1)
-        rows = back_ref[pl.ds(s * 8, 8), :, :].reshape(8 * slots, width)
-        part_ref[...] += dot(onehot_of_rows(idx, nodes), rows)
-        return 0
-
-    lax.fori_loop(0, peers // 8, step, 0)
+    part_ref[own_span, :] += near_ref[:own_rows, :]
 
 
 def returned_sum(half, idx, back, near, nodes):
+    width = back.shape[2]
     return pl.pallas_call(
-        returned_kernel,
+        functools.partial(returned_kernel, min(32, back.shape[0])),
         in_specs=[sspec(), vspec(), vspec(), vspec()],
         out_specs=vspec(),
-        out_shape=jax.ShapeDtypeStruct((nodes, back.shape[2]), F32),
+        out_shape=jax.ShapeDtypeStruct((nodes, width), F32),
+        scratch_shapes=[VMEM((nodes // 2, 2 * width), F32)],
         compiler_params=params(),
         name="returned_sum",
     )(half, idx, back, near)
@@ -418,7 +506,7 @@
     hub_z = exchange(jnp.broadcast_to(hub_half[None], (zs,) + hub_half.shape), Z_AXIS, num_dom)
 
     slot_ids = jnp.arange(block_rows, dtype=jnp.int32)[None, :]
-    idx_all = jnp.where(slot_ids < send_count[0][:, None], send_rows[0], nodes + 1024)
+    idx_all = jnp.where(slot_ids < send_count[0][:, None], send_rows[0], -1)
     idx = jnp.where(half == 0, idx_all[:, 0::2], idx_all[:, 1::2])
     idx = idx.reshape(num_dom * slots // 128, 128)
     out_rows = outgoing(idx, node_feats, slots)
@@ -460,7 +548,7 @@
     every = every.reshape(-1, CHUNK)
     near_edge = keys < (near_rows << DST_BITS)
     live_edge = keys < PAD
-    counts = jnp.stack([jnp.sum(near_edge.astype(jnp.int32)), jnp.sum(live_edge.astype(jnp.int32))])
+    counts = [jnp.sum(edge.astype(jnp.int32)) for edge in (near_edge, live_edge)]
     near_low = jnp.minimum(keys[:, 0] >> DST_BITS, near_rows - 1)
     near_high = jnp.max(jnp.where(near_edge, keys, 0), axis=1) >> DST_BITS
     far_low = jnp.min(jnp.where(near_edge, PAD, keys), axis=1) >> DST_BITS
@@ -468,10 +556,12 @@
     far_high = jnp.max(jnp.where(live_edge, keys, 0), axis=1) >> DST_BITS
     far_high = jnp.maximum(far_high - near_rows, 0)
 
-    near_sum, degree = near_forward(counts, near_low, near_high, every, keys, near_table, nodes)
-    neigh = far_forward(
-        counts, far_low, far_high, keys, table.reshape(far_rows, width), near_sum, near_rows
-    )
+    lines = keys.shape[0]
+    counts = jnp.where(jnp.arange(lines) == 0, counts[0], counts[1])
+    meta = jnp.stack([near_low, near_high, far_low, far_high, counts])
+
+    near_sum, degree = near_forward(meta, every, keys, near_table, nodes)
+    neigh = far_forward(meta, keys, table.reshape(far_rows, width), near_sum, near_rows)
     neigh_other = lax.ppermute(neigh, "edge", SWAP)
     layer_out, grad_sum, grad_input, grad_w = dense(
         half_scalar,
@@ -486,14 +576,12 @@
     )
     share = grad_w.shape[0] // zs
     grad_w = exchange(grad_w.reshape(zs, share, width), Z_AXIS, num_dom)
-    row_grads = far_backward(counts, far_low, far_high, keys, grad_sum, near_rows, far_rows)
+    row_grads = far_backward(meta, keys, grad_sum, near_rows, far_rows)
     row_grads, grad_w = lax.optimization_barrier((row_grads, grad_w))
     back = lax.all_to_all(
         row_grads.reshape(num_dom, slots, width), "dom", split_axis=0, concat_axis=0, tiled=True
     )
-    near_grads = near_backward(
-        counts, near_low, near_high, after(keys, row_grads), grad_sum, near_rows
-    )
+    near_grads = near_backward(meta, after(keys, row_grads), grad_sum, near_rows)
 
     grad_w = jnp.sum(grad_w, axis=0)
     hub_part = near_grads[own_rows:]

time: 230 us -> 194 us (0.84)
  Pallas kernels: 73.5 us -> 30.2 us
  waiting for transfers between devices: 38.1 us -> 53.2 us
  starting transfers between devices: 75.8 us -> 71.9 us
  local copies, waits for them, and re-layouts: 23.8 us -> 20 us
    pallas_call x1, Pallas kernels: 23.4 us -> 8.41 us  [near_forward(): pl.pallas_call(functools.partial(near_forward_kernel, min(window, table.s...]
    all_to_all x1, waiting for transfers between devices: 0.01 us -> 11.4 us  [body(): lax.all_to_all(out_rows, 'dom', split_axis=0, concat_axis=0, tiled=True)]
    pallas_call x2, Pallas kernels: 16.6 us -> 7.29 us  [the longest x1 4.18 us: returned_sum(): pl.pallas_call(functools.partial(returned_kernel, min(32, back.shape[0]))...]
    pallas_call x1, Pallas kernels: 12.9 us -> 5.01 us  [near_backward(): pl.pallas_call(functools.partial(near_backward_kernel, min(window, rows))...]
    ppermute x12, waiting for transfers between devices: 36.2 us -> 29.4 us  [swap_blocks(): lax.ppermute(block, 'dom', pairs)]
    pallas_call x1, Pallas kernels: 8.96 us -> 2.96 us  [far_forward(): pl.pallas_call(functools.partial(far_forward_kernel, offset, min(window,...]
    all_to_all x1, waiting for transfers between devices: 0.03 us -> 5.73 us  [body(): lax.all_to_all(row_grads.reshape(num_dom, slots, width), 'dom', split_axi...]
    pallas_call x1, Pallas kernels: 9.19 us -> 4.11 us  [far_backward(): pl.pallas_call(functools.partial(far_backward_kernel, offset, min(window,...]
  transfers between devices with their start and end apart: 21 -> 21, of which waited for: 9 -> 13; matrix products, arithmetic and copies ran while one was open for 11% -> 13% of each run, Pallas kernels for 27% -> 13%
where the time goes in v3:
time: 194 us; the launch traced here: 193 us
  starting transfers between devices  71.9 us (37%)
  waiting for transfers between devices  53.2 us (27%)
  Pallas kernels  30.2 us (16%)
  local copies, waits for them, and re-layouts  20 us (10%)
  other arithmetic  16.5 us (9%)
    ppermute x12, waiting for transfers between devices, swap_blocks(): lax.ppermute(block, 'dom', pairs)  29.4 us
    all_to_all x3, starting transfers between devices, exchange(): lax.all_to_all(blocks, 'dom', 0, 0, axis_index_groups=groups_of(size, axi...  19 us
    ppermute x12, starting transfers between devices, swap_blocks(): lax.ppermute(block, 'dom', pairs)  17.1 us
    all_to_all x1, starting transfers between devices, body(): lax.all_to_all(out_rows, 'dom', split_axis=0, concat_axis=0, tiled=True)  14.1 us
    unnamed x41, local copies, waits for them, and re-layouts  12.8 us
    all_to_all x1, waiting for transfers between devices, body(): lax.all_to_all(out_rows, 'dom', split_axis=0, concat_axis=0, tiled=True)  11.4 us
    all_to_all x1, starting transfers between devices, body(): lax.all_to_all(row_grads.reshape(num_dom, slots, width), 'dom', split_axi...  10.2 us
    pallas_call x1, Pallas kernels, near_forward(): pl.pallas_call(functools.partial(near_forward_kernel, min(window, table.s...  8.41 us
  transfers between devices with their start and end apart: 21, of which 13 were waited for; matrix products, arithmetic and copies ran while one was open for 13% of the time, Pallas kernels for 13%

profile of v3, /device:TPU:1, one launch (start us, length us, event | category | flops | bytes accessed | tf_op | source)
XLA Modules:
  0.0 193.3 jit_solution(1115766641878173267)
XLA Ops:
  2.0 9.0 %all-to-all-start = ((bf16[8,16,128]{2,1,0:T(8,128)(2,1)}), bf16[8,16,128]{2,1,0:T(8,128)(2,1)S(1)}, u32[]{:S(2)}, u32[]{:S(2)}) async-start(bf16[8,16,128]{2,1,0:T(8,128)(2,1)} %broadcast_in_dim.44), calls=%async_computation | async-start | bytes 65536 | tf_op jit(solution)/shard_map/all_to_all | solution.py:454
  15.2 3.1 %outgoing_rows.1 = bf16[128,64,128]{2,1,0:T(8,128)(2,1)S(1)} custom-call(s32[64,128]{1,0:T(8,128)S(1)} %reshape.135.idx_ref, bf16[1024,128]{1,0:T(8,128)(2,1)S(1)} %copy-done.3), custom_call_target="tpu_custom_call" | custom-call | tf_op jit(solution)/shard_map/outgoing_rows/pallas_call | solution.py:106
  19.7 14.1 %all-to-all-start.1 = ((bf16[128,64,128]{2,1,0:T(8,128)(2,1)}), bf16[128,64,128]{2,1,0:T(8,128)(2,1)S(1)}, u32[]{:S(2)}, u32[]{:S(2)}) async-start(bf16[128,64,128]{2,1,0:T(8,128)(2,1)} %copy-done.1), calls=%async_computation.1 | async-start | bytes 4194304 | tf_op jit(solution)/shard_map/all_to_all | solution.py:514
  38.0 2.8 %collective-permute-start.2 = (bf16[128,128]{1,0:T(8,128)(2,1)S(1)}, bf16[128,128]{1,0:T(8,128)(2,1)S(1)}, u32[]{:S(2)}, u32[]{:S(2)}) collective-permute-start(bf16[128,128]{1,0:T(8,128)(2,1)S(1)} %bitcast.31), channel_id=1, source_target_pairs={{0,128},{2,130},{4,132},{6,134},{8,136},{10,138},{12,140},{14,142}... | collective-permute-start | bytes 98312 | tf_op jit(solution)/shard_map/ppermute | solution.py:467
  47.0 2.6 %collective-permute-start.5 = (bf16[512,128]{1,0:T(8,128)(2,1)S(1)}, bf16[512,128]{1,0:T(8,128)(2,1)S(1)}, u32[]{:S(2)}, u32[]{:S(2)}) collective-permute-start(bf16[512,128]{1,0:T(8,128)(2,1)S(1)} %get-tuple-element.51), channel_id=1, source_target_pairs={{0,4},{2,6},{4,0},{6,2},{8,12},{10,14},{12,8},{14,10},{16,20},{18,... | collective-permute-start | bytes 393224 | tf_op jit(solution)/shard_map/ppermute | solution.py:467
  50.3 7.7 %sort.14 = (s32[16384]{0:T(1024)S(1)}, s32[16384]{0:T(1024)}) sort(s32[16384]{0:T(1024)S(1)} %and_select_fusion, s32[16384]{0:T(1024)S(1)} %iota.15), dimensions={0}, to_apply=%region_0.1 | sort | flops 229376 | bytes 262144 | tf_op jit(solution)/shard_map/sort | solution.py:547
  62.4 8.4 %near_forward.1 = (f32[512,256]{1,0:T(8,128)S(1)}, f32[16,128]{1,0:T(8,128)S(1)}) custom-call(s32[5,64]{1,0:T(8,128)S(1)} %stack.2.meta_ref, s32[64,256]{1,0:T(8,128)S(1)} %pad_add_fusion.every_ref, s32[64,256]{1,0:T(8,128)S(1)} %reshape.136.keys_ref, bf16[2560,128]{1,0:T(8,128)(2,1)} %constant_dynamic-update-slice_fusion.5.table_ref), custom_call_target="tpu_custom_call" | custom-call | tf_op jit(solution)/shard_map/near_forward/pallas_call | solution.py:239
  71.4 11.4 %all-to-all-done.1 = bf16[128,64,128]{2,1,0:T(8,128)(2,1)S(1)} async-done(((bf16[128,64,128]{2,1,0:T(8,128)(2,1)}), bf16[128,64,128]{2,1,0:T(8,128)(2,1)S(1)}, u32[]{:S(2)}, u32[]{:S(2)}) %all-to-all-start.1) | async-done | bytes 2097184 | tf_op jit(solution)/shard_map/all_to_all | solution.py:514
  82.8 3.0 %far_forward.1.mine_ref = f32[512,256]{1,0:T(8,128)S(1)} custom-call(s32[5,64]{1,0:T(8,128)S(1)} %stack.2.meta_ref, s32[64,256]{1,0:T(8,128)S(1)} %reshape.136.keys_ref, bf16[8192,128]{1,0:T(8,128)(2,1)S(1)} %bitcast.24, f32[512,256]{1,0:T(8,128)S(1)} %get-tuple-element.27.base_ref), custom_call_target="tpu_custom_call" | custom-call | tf_op jit(solution)/shard_map/far_forward/pallas_call | solution.py:268
  85.8 5.8 %collective-permute-start.7 = (f32[512,256]{1,0:T(8,128)S(1)}, f32[512,256]{1,0:T(8,128)S(1)}, u32[]{:S(2)}, u32[]{:S(2)}) collective-permute-start(f32[512,256]{1,0:T(8,128)S(1)} %far_forward.1.mine_ref), channel_id=1, source_target_pairs={{0,1},{1,0},{2,3},{3,2},{4,5},{5,4},{6,7},{7,6},{8,9},{9,8},{10,11... | collective-permute-start | bytes 1572872 | tf_op jit(solution)/shard_map/ppermute | solution.py:565
  98.0 3.4 %all-to-all-start.2 = ((f32[8,24,128]{2,1,0:T(8,128)}), f32[8,24,128]{2,1,0:T(8,128)S(1)}, u32[]{:S(2)}, u32[]{:S(2)}) async-start(f32[8,24,128]{2,1,0:T(8,128)} %bitcast.12), calls=%async_computation.2 | async-start | bytes 196608 | tf_op jit(solution)/shard_map/all_to_all | solution.py:454
  101.5 4.1 %far_backward.1 = bf16[8192,128]{1,0:T(8,128)(2,1)S(1)} custom-call(s32[5,64]{1,0:T(8,128)S(1)} %stack.2.meta_ref, s32[64,256]{1,0:T(8,128)S(1)} %reshape.136.keys_ref, bf16[512,256]{1,0:T(8,128)(2,1)S(1)} %get-tuple-element.31.grad_ref), custom_call_target="tpu_custom_call" | custom-call | tf_op jit(solution)/shard_map/far_backward/pallas_call | solution.py:370
  109.6 10.2 %all-to-all-start.3 = ((bf16[128,64,128]{2,1,0:T(8,128)(2,1)}), bf16[128,64,128]{2,1,0:T(8,128)(2,1)S(1)}, u32[]{:S(2)}, u32[]{:S(2)}) async-start(bf16[128,64,128]{2,1,0:T(8,128)(2,1)} %bitcast.25), calls=%async_computation.3 | async-start | bytes 4194304 | tf_op jit(solution)/shard_map/all_to_all | solution.py:581
  120.7 5.0 %near_backward.1.near_ref = f32[2560,128]{1,0:T(8,128)S(1)} custom-call(s32[5,64]{1,0:T(8,128)S(1)} %stack.2.meta_ref, s32[64,256]{1,0:T(8,128)S(1)} %reshape.136.keys_ref, bf16[512,256]{1,0:T(8,128)(2,1)S(1)} %copy-done.6), custom_call_target="tpu_custom_call" | custom-call | tf_op jit(solution)/shard_map/near_backward/pallas_call | solution.py:395
  126.8 2.8 %collective-permute-start.9 = (f32[536,128]{1,0:T(8,128)S(1)}, f32[536,128]{1,0:T(8,128)S(1)}, u32[]{:S(2)}, u32[]{:S(2)}) collective-permute-start(f32[536,128]{1,0:T(8,128)S(1)} %get-tuple-element.62), channel_id=1, source_target_pairs={{0,2},{2,0},{4,6},{6,4},{8,10},{10,8},{12,14},{14,12},{16,18},{18,... | collective-permute-start | bytes 823304 | tf_op jit(solution)/shard_map/ppermute | solution.py:467
  132.1 8.8 %collective-permute-done.9 = f32[536,128]{1,0:T(8,128)S(1)} collective-permute-done((f32[536,128]{1,0:T(8,128)S(1)}, f32[536,128]{1,0:T(8,128)S(1)}, u32[]{:S(2)}, u32[]{:S(2)}) %collective-permute-start.9) | collective-permute-done | bytes 274464 | tf_op jit(solution)/shard_map/ppermute | solution.py:467
  140.9 12.5 %collective-permute-done.10 = f32[536,128]{1,0:T(8,128)S(1)} collective-permute-done((f32[536,128]{1,0:T(8,128)S(1)}, f32[536,128]{1,0:T(8,128)S(1)}, u32[]{:S(2)}, u32[]{:S(2)}) %collective-permute-start.10) | collective-permute-done | bytes 274464 | tf_op jit(solution)/shard_map/ppermute | solution.py:467
  153.7 3.3 %collective-permute-start.13 = (f32[152,128]{1,0:T(8,128)S(1)}, f32[152,128]{1,0:T(8,128)S(1)}, u32[]{:S(2)}, u32[]{:S(2)}) collective-permute-start(f32[152,128]{1,0:T(8,128)S(1)} %get-tuple-element.59), channel_id=1, source_target_pairs={{0,128},{2,130},{4,132},{6,134},{8,136},{10,138},{12,140},{14,142}... | collective-permute-start | bytes 233480 | tf_op jit(solution)/shard_map/ppermute | solution.py:467
  157.7 2.7 %collective-permute-done.13 = f32[152,128]{1,0:T(8,128)S(1)} collective-permute-done((f32[152,128]{1,0:T(8,128)S(1)}, f32[152,128]{1,0:T(8,128)S(1)}, u32[]{:S(2)}, u32[]{:S(2)}) %collective-permute-start.13) | collective-permute-done | bytes 77856 | tf_op jit(solution)/shard_map/ppermute | solution.py:467
  163.3 5.7 %all-to-all-done.3.back_ref = bf16[128,64,128]{2,1,0:T(8,128)(2,1)S(1)} async-done(((bf16[128,64,128]{2,1,0:T(8,128)(2,1)}), bf16[128,64,128]{2,1,0:T(8,128)(2,1)S(1)}, u32[]{:S(2)}, u32[]{:S(2)}) %all-to-all-start.3) | async-done | bytes 2097184 | tf_op jit(solution)/shard_map/all_to_all | solution.py:581
  169.0 6.5 %all-to-all-start.4 = ((f32[8,40,128]{2,1,0:T(8,128)}), f32[8,40,128]{2,1,0:T(8,128)}, u32[]{:S(2)}, u32[]{:S(2)}) async-start(f32[8,40,128]{2,1,0:T(8,128)} %pad_maximum_fusion.4), calls=%async_computation.4 | async-start | bytes 327680 | tf_op jit(solution)/shard_map/all_to_all | solution.py:454
  175.6 4.2 %returned_sum.1 = f32[1024,128]{1,0:T(8,128)} custom-call(s32[1]{0:T(128)} %bitcast.half_ref, s32[64,128]{1,0:T(8,128)S(1)} %reshape.135.idx_ref, bf16[128,64,128]{2,1,0:T(8,128)(2,1)S(1)} %all-to-all-done.3.back_ref, f32[2560,128]{1,0:T(8,128)S(1)} %near_backward.1.near_ref), custom_call_target="tpu_custom_call" | custom-call | tf_op jit(solution)/shard_map/returned_sum/pallas_call | solution.py:428
  181.3 2.7 %all-to-all-done.4 = f32[8,40,128]{2,1,0:T(8,128)} async-done(((f32[8,40,128]{2,1,0:T(8,128)}), f32[8,40,128]{2,1,0:T(8,128)}, u32[]{:S(2)}, u32[]{:S(2)}) %all-to-all-start.4) | async-done | bytes 163872 | tf_op jit(solution)/shard_map/all_to_all | solution.py:454
  185.7 2.7 %collective-permute-start.15 = (f32[144,128]{1,0:T(8,128)S(1)}, f32[144,128]{1,0:T(8,128)S(1)}, u32[]{:S(2)}, u32[]{:S(2)}) collective-permute-start(f32[144,128]{1,0:T(8,128)S(1)} %pad_maximum_fusion.8), channel_id=1, source_target_pairs={{0,1},{1,0},{2,3},{3,2},{4,5},{5,4},{6,7},{7,6},{8,9},{9,8},{10,11... | collective-permute-start | bytes 221192 | tf_op jit(solution)/shard_map/ppermute | solution.py:604
  (116 shorter events, 49.0 us)
Async XLA Ops:
  2.0 17.8 %all-to-all-start = ((bf16[8,16,128]{2,1,0:T(8,128)(2,1)}), bf16[8,16,128]{2,1,0:T(8,128)(2,1)S(1)}, u32[]{:S(2)}, u32[]{:S(2)}) async-start(bf16[8,16,128]{2,1,0:T(8,128)(2,1)} %broadcast_in_dim.44), calls=%async_computation | async-start | bytes 65536 | tf_op jit(solution)/shard_map/all_to_all | solution.py:454
  19.7 15.5 %copy-start.16 = (s32[1,1,8192]{2,1,0:T(1,128)S(1)}, s32[1,1,8192]{2,1,0:T(1,128)}, u32[]{:S(2)}) copy-start(s32[1,1,8192]{2,1,0:T(1,128)} %param.19) | copy-start | bytes 98308
  19.7 63.1 %all-to-all-start.1 = ((bf16[128,64,128]{2,1,0:T(8,128)(2,1)}), bf16[128,64,128]{2,1,0:T(8,128)(2,1)S(1)}, u32[]{:S(2)}, u32[]{:S(2)}) async-start(bf16[128,64,128]{2,1,0:T(8,128)(2,1)} %copy-done.1), calls=%async_computation.1 | async-start | bytes 4194304 | tf_op jit(solution)/shard_map/all_to_all | solution.py:514
  35.4 14.9 %collective-permute-start = (s32[8192]{0:T(1024)S(1)}, s32[8192]{0:T(1024)S(1)}, u32[]{:S(2)}, u32[]{:S(2)}) collective-permute-start(s32[8192]{0:T(1024)S(1)} %fusion.11), channel_id=1, source_target_pairs={{0,1},{1,0},{2,3},{3,2},{4,5},{5,4},{6,7},{7,6},{8,9},{9,8},{10,11... | collective-permute-start | bytes 98312 | tf_op jit(solution)/shard_map/ppermute | solution.py:544
  37.0 4.6 %collective-permute-start.1 = (bf16[128,128]{1,0:T(8,128)(2,1)S(1)}, bf16[128,128]{1,0:T(8,128)(2,1)S(1)}, u32[]{:S(2)}, u32[]{:S(2)}) collective-permute-start(bf16[128,128]{1,0:T(8,128)(2,1)S(1)} %bitcast.30), channel_id=1, source_target_pairs={{0,64},{2,66},{4,68},{6,70},{8,72},{10,74},{12,76},{14,78},{16,80}... | collective-permute-start | bytes 98312 | tf_op jit(solution)/shard_map/ppermute | solution.py:467
  38.0 6.5 %collective-permute-start.2 = (bf16[128,128]{1,0:T(8,128)(2,1)S(1)}, bf16[128,128]{1,0:T(8,128)(2,1)S(1)}, u32[]{:S(2)}, u32[]{:S(2)}) collective-permute-start(bf16[128,128]{1,0:T(8,128)(2,1)S(1)} %bitcast.31), channel_id=1, source_target_pairs={{0,128},{2,130},{4,132},{6,134},{8,136},{10,138},{12,140},{14,142}... | collective-permute-start | bytes 98312 | tf_op jit(solution)/shard_map/ppermute | solution.py:467
  40.9 4.9 %collective-permute-start.3 = (bf16[128,128]{1,0:T(8,128)(2,1)S(1)}, bf16[128,128]{1,0:T(8,128)(2,1)S(1)}, u32[]{:S(2)}, u32[]{:S(2)}) collective-permute-start(bf16[128,128]{1,0:T(8,128)(2,1)S(1)} %bitcast.32), channel_id=1, source_target_pairs={{0,192},{2,194},{4,196},{6,198},{8,200},{10,202},{12,204},{14,206}... | collective-permute-start | bytes 98312 | tf_op jit(solution)/shard_map/ppermute | solution.py:467
  46.4 14.0 %collective-permute-start.4 = (bf16[512,128]{1,0:T(8,128)(2,1)S(1)}, bf16[512,128]{1,0:T(8,128)(2,1)S(1)}, u32[]{:S(2)}, u32[]{:S(2)}) collective-permute-start(bf16[512,128]{1,0:T(8,128)(2,1)S(1)} %get-tuple-element.51), channel_id=1, source_target_pairs={{0,2},{2,0},{4,6},{6,4},{8,10},{10,8},{12,14},{14,12},{16,18},{18,... | collective-permute-start | bytes 393224 | tf_op jit(solution)/shard_map/ppermute | solution.py:467
  47.0 14.0 %collective-permute-start.5 = (bf16[512,128]{1,0:T(8,128)(2,1)S(1)}, bf16[512,128]{1,0:T(8,128)(2,1)S(1)}, u32[]{:S(2)}, u32[]{:S(2)}) collective-permute-start(bf16[512,128]{1,0:T(8,128)(2,1)S(1)} %get-tuple-element.51), channel_id=1, source_target_pairs={{0,4},{2,6},{4,0},{6,2},{8,12},{10,14},{12,8},{14,10},{16,20},{18,... | collective-permute-start | bytes 393224 | tf_op jit(solution)/shard_map/ppermute | solution.py:467
  49.6 12.1 %collective-permute-start.6 = (bf16[512,128]{1,0:T(8,128)(2,1)S(1)}, bf16[512,128]{1,0:T(8,128)(2,1)S(1)}, u32[]{:S(2)}, u32[]{:S(2)}) collective-permute-start(bf16[512,128]{1,0:T(8,128)(2,1)S(1)} %get-tuple-element.51), channel_id=1, source_target_pairs={{0,6},{2,4},{4,2},{6,0},{8,14},{10,12},{12,10},{14,8},{16,22},{18,... | collective-permute-start | bytes 393224 | tf_op jit(solution)/shard_map/ppermute | solution.py:467
  61.7 31.4 %copy-start.9 = (bf16[128,128]{1,0:T(8,128)(2,1)S(1)}, bf16[128,128]{1,0:T(8,128)(2,1)}, u32[]{:S(2)}) copy-start(bf16[128,128]{1,0:T(8,128)(2,1)} %w_self_ref.1) | copy-start | bytes 98308
  61.7 31.4 %copy-start.13 = (f32[128]{0:T(128)S(1)}, f32[128]{0:T(128)}, u32[]{:S(2)}) copy-start(f32[128]{0:T(128)} %param.15) | copy-start | bytes 1540
  85.8 7.3 %collective-permute-start.7 = (f32[512,256]{1,0:T(8,128)S(1)}, f32[512,256]{1,0:T(8,128)S(1)}, u32[]{:S(2)}, u32[]{:S(2)}) collective-permute-start(f32[512,256]{1,0:T(8,128)S(1)} %far_forward.1.mine_ref), channel_id=1, source_target_pairs={{0,1},{1,0},{2,3},{3,2},{4,5},{5,4},{6,7},{7,6},{8,9},{9,8},{10,11... | collective-permute-start | bytes 1572872 | tf_op jit(solution)/shard_map/ppermute | solution.py:565
  98.0 10.9 %all-to-all-start.2 = ((f32[8,24,128]{2,1,0:T(8,128)}), f32[8,24,128]{2,1,0:T(8,128)S(1)}, u32[]{:S(2)}, u32[]{:S(2)}) async-start(f32[8,24,128]{2,1,0:T(8,128)} %bitcast.12), calls=%async_computation.2 | async-start | bytes 196608 | tf_op jit(solution)/shard_map/all_to_all | solution.py:454
  109.6 59.5 %all-to-all-start.3 = ((bf16[128,64,128]{2,1,0:T(8,128)(2,1)}), bf16[128,64,128]{2,1,0:T(8,128)(2,1)S(1)}, u32[]{:S(2)}, u32[]{:S(2)}) async-start(bf16[128,64,128]{2,1,0:T(8,128)(2,1)} %bitcast.25), calls=%async_computation.3 | async-start | bytes 4194304 | tf_op jit(solution)/shard_map/all_to_all | solution.py:581
  126.8 14.1 %collective-permute-start.9 = (f32[536,128]{1,0:T(8,128)S(1)}, f32[536,128]{1,0:T(8,128)S(1)}, u32[]{:S(2)}, u32[]{:S(2)}) collective-permute-start(f32[536,128]{1,0:T(8,128)S(1)} %get-tuple-element.62), channel_id=1, source_target_pairs={{0,2},{2,0},{4,6},{6,4},{8,10},{10,8},{12,14},{14,12},{16,18},{18,... | collective-permute-start | bytes 823304 | tf_op jit(solution)/shard_map/ppermute | solution.py:467
  129.6 23.8 %collective-permute-start.10 = (f32[536,128]{1,0:T(8,128)S(1)}, f32[536,128]{1,0:T(8,128)S(1)}, u32[]{:S(2)}, u32[]{:S(2)}) collective-permute-start(f32[536,128]{1,0:T(8,128)S(1)} %get-tuple-element.63), channel_id=1, source_target_pairs={{0,4},{2,6},{4,0},{6,2},{8,12},{10,14},{12,8},{14,10},{16,20},{18,... | collective-permute-start | bytes 823304 | tf_op jit(solution)/shard_map/ppermute | solution.py:467
  131.2 22.2 %collective-permute-start.11 = (f32[536,128]{1,0:T(8,128)S(1)}, f32[536,128]{1,0:T(8,128)S(1)}, u32[]{:S(2)}, u32[]{:S(2)}) collective-permute-start(f32[536,128]{1,0:T(8,128)S(1)} %get-tuple-element.61), channel_id=1, source_target_pairs={{0,6},{2,4},{4,2},{6,0},{8,14},{10,12},{12,10},{14,8},{16,22},{18,... | collective-permute-start | bytes 823304 | tf_op jit(solution)/shard_map/ppermute | solution.py:467
  153.6 4.2 %collective-permute-start.12 = (f32[152,128]{1,0:T(8,128)S(1)}, f32[152,128]{1,0:T(8,128)S(1)}, u32[]{:S(2)}, u32[]{:S(2)}) collective-permute-start(f32[152,128]{1,0:T(8,128)S(1)} %get-tuple-element.60), channel_id=1, source_target_pairs={{0,64},{2,66},{4,68},{6,70},{8,72},{10,74},{12,76},{14,78},{16,80}... | collective-permute-start | bytes 233480 | tf_op jit(solution)/shard_map/ppermute | solution.py:467
  153.7 6.8 %collective-permute-start.13 = (f32[152,128]{1,0:T(8,128)S(1)}, f32[152,128]{1,0:T(8,128)S(1)}, u32[]{:S(2)}, u32[]{:S(2)}) collective-permute-start(f32[152,128]{1,0:T(8,128)S(1)} %get-tuple-element.59), channel_id=1, source_target_pairs={{0,128},{2,130},{4,132},{6,134},{8,136},{10,138},{12,140},{14,142}... | collective-permute-start | bytes 233480 | tf_op jit(solution)/shard_map/ppermute | solution.py:467
  157.0 5.6 %collective-permute-start.14 = (f32[152,128]{1,0:T(8,128)S(1)}, f32[152,128]{1,0:T(8,128)S(1)}, u32[]{:S(2)}, u32[]{:S(2)}) collective-permute-start(f32[152,128]{1,0:T(8,128)S(1)} %concatenate.67), channel_id=1, source_target_pairs={{0,192},{2,194},{4,196},{6,198},{8,200},{10,202},{12,204},{14,206}... | collective-permute-start | bytes 233480 | tf_op jit(solution)/shard_map/ppermute | solution.py:467
  169.0 14.9 %all-to-all-start.4 = ((f32[8,40,128]{2,1,0:T(8,128)}), f32[8,40,128]{2,1,0:T(8,128)}, u32[]{:S(2)}, u32[]{:S(2)}) async-start(f32[8,40,128]{2,1,0:T(8,128)} %pad_maximum_fusion.4), calls=%async_computation.4 | async-start | bytes 327680 | tf_op jit(solution)/shard_map/all_to_all | solution.py:454
  179.7 11.5 %collective-permute-start.8 = (f32[1024,128]{1,0:T(8,128)}, f32[1024,128]{1,0:T(8,128)S(1)}, u32[]{:S(2)}, u32[]{:S(2)}) collective-permute-start(f32[1024,128]{1,0:T(8,128)} %returned_sum.1), channel_id=1, source_target_pairs={{0,1},{1,0},{2,3},{3,2},{4,5},{5,4},{6,7},{7,6},{8,9},{9,8},{10,11... | collective-permute-start | bytes 1572872 | tf_op jit(solution)/shard_map/ppermute | solution.py:602
  185.7 3.6 %collective-permute-start.15 = (f32[144,128]{1,0:T(8,128)S(1)}, f32[144,128]{1,0:T(8,128)S(1)}, u32[]{:S(2)}, u32[]{:S(2)}) collective-permute-start(f32[144,128]{1,0:T(8,128)S(1)} %pad_maximum_fusion.8), channel_id=1, source_target_pairs={{0,1},{1,0},{2,3},{3,2},{4,5},{5,4},{6,7},{7,6},{8,9},{9,8},{10,11... | collective-permute-start | bytes 221192 | tf_op jit(solution)/shard_map/ppermute | solution.py:604
  (14 other events, 60.5 us)

commit v4 on v3

--- a/solution.py
+++ b/solution.py
@@ -84,7 +84,7 @@
     return jnp.concatenate(refs_at, axis=1)
 
 
-def outgoing_kernel(idx_ref, feat_ref, out_ref, wide_ref):
+def outgoing_kernel(flip_ref, count_ref, rows_ref, feat_ref, out_ref, idx_ref, wide_ref, all_ref):
     step = pl.program_id(0)
     peers, slots, width = out_ref.shape
     nodes = feat_ref.shape[0]
@@ -94,28 +94,46 @@
     def _():
         wide_ref[:, :width] = feat_ref[: nodes // 2, :]
         wide_ref[:, width:] = feat_ref[nodes // 2 :, :]
+        count = columns_of(count_ref[...])[: rows_ref.shape[0], :]
+        lane = lax.broadcasted_iota(jnp.int32, rows_ref.shape, 1)
+        all_ref[...] = jnp.where(lane < count, rows_ref[...], -1)
+        pairs = rows_ref.shape[0] // 2
+        even = all_ref[pl.ds(0, pairs, stride=2), :]
+        odd = all_ref[pl.ds(1, pairs, stride=2), :]
+        low = lax.broadcasted_iota(jnp.int32, even.shape, 1) < slots
+        crossed = pltpu.roll(jnp.where(low, odd, even), slots, 1)
+        idx_ref[...] = jnp.where(flip_ref[0] == 0, jnp.where(low, even, odd), crossed)
 
     row = join([idx_ref[pl.ds(step * lines + k, 1), :] for k in range(lines)])
     out_ref[...] = pick(columns_of(row), wide_ref[...]).astype(BF16).reshape(peers, slots, width)
 
 
-def outgoing(idx, feats, slots, step_peers=32):
-    peers = idx.shape[0] * idx.shape[1] // slots
+def outgoing(flip, count, rows, feats, step_peers=32):
+    peers, slots = rows.shape[0], rows.shape[1] // 2
     nodes, width = feats.shape
     step_peers = min(step_peers, peers)
+    lines = peers * slots // 128
     return pl.pallas_call(
         outgoing_kernel,
         grid=(peers // step_peers,),
         in_specs=[
-            pl.BlockSpec(idx.shape, lambda i: (0, 0)),
+            sspec(),
+            pl.BlockSpec(count.shape, lambda i: (0, 0)),
+            pl.BlockSpec(rows.shape, lambda i: (0, 0)),
             pl.BlockSpec(feats.shape, lambda i: (0, 0)),
         ],
-        out_specs=pl.BlockSpec((step_peers, slots, width), lambda i: (i, 0, 0)),
-        out_shape=jax.ShapeDtypeStruct((peers, slots, width), BF16),
-        scratch_shapes=[VMEM((nodes // 2, 2 * width), BF16)],
+        out_specs=[
+            pl.BlockSpec((step_peers, slots, width), lambda i: (i, 0, 0)),
+            pl.BlockSpec((lines, 128), lambda i: (0, 0)),
+        ],
+        out_shape=[
+            pltpu.HBM((peers, slots, width), BF16),
+            jax.ShapeDtypeStruct((lines, 128), jnp.int32),
+        ],
+        scratch_shapes=[VMEM((nodes // 2, 2 * width), BF16), VMEM(rows.shape, jnp.int32)],
         compiler_params=params(),
         name="outgoing_rows",
-    )(idx, feats)
+    )(flip, count, rows, feats)
 
 
 def relative(row, base, start, window):
@@ -288,10 +306,9 @@
     bias_ref,
     out_ref,
     grad_sum_ref,
-    grad_input_ref,
+    pre_ref,
     grad_w_ref,
     left_ref,
-    pre_ref,
 ):
     nodes = feat_ref.shape[0]
     grad_bias = jnp.zeros((8, 128), F32)
@@ -309,7 +326,6 @@
         grad_pre = (cot_ref[span, :].astype(F32) * slope).astype(BF16)
         pre_ref[span, :] = grad_pre
         grad_sum_ref[place] = (dot_nt(grad_pre, w_neigh_ref[...]) / divisor).astype(BF16)
-        grad_input_ref[span, :] = dot_nt(grad_pre, w_self_ref[...])
         left_ref[span, :] = jnp.where(half_ref[0] == 0, feats.astype(F32), aggregate.astype(F32)).astype(BF16)
         wide = grad_pre.astype(F32)
         for r in range(0, 128, 8):
@@ -329,10 +345,10 @@
         out_shape=[
             jax.ShapeDtypeStruct((nodes, width), BF16),
             jax.ShapeDtypeStruct((nodes // 2, 2 * width), BF16),
-            jax.ShapeDtypeStruct((nodes, width), F32),
+            jax.ShapeDtypeStruct((nodes, width), BF16),
             jax.ShapeDtypeStruct((192, width), F32),
         ],
-        scratch_shapes=[VMEM((nodes, width), BF16), VMEM((nodes, width), BF16)],
+        scratch_shapes=[VMEM((nodes, width), BF16)],
         compiler_params=params(),
         name="dense_part",
     )(half, mine, other, deg, feats, cot, w_self, w_neigh, bias)
@@ -340,46 +356,55 @@
 
 def far_backward_kernel(offset, window, meta_ref, keys_ref, grad_ref, out_ref, acc_ref, values_ref):
     rows = acc_ref.shape[0]
-    block = min(512, rows)
-
-    def clear(b, _):
-        span = pl.ds(pl.multiple_of(b * block, block), block)
-        acc_ref[span, :] = jnp.zeros((block, acc_ref.shape[1]), F32)
-        return 0
-
-    lax.fori_loop(0, rows // block, clear, 0)
-    end = pl.cdiv(meta_ref[COUNTS, 1], CHUNK)
-    over_chunks(
-        meta_ref[COUNTS, 0] // CHUNK,
-        end,
-        lambda c: spread_add(
-            c, end, offset, window, FAR_LOW, meta_ref, keys_ref, grad_ref, acc_ref, values_ref
-        ),
-    )
-
-    def finish(b, _):
-        span = pl.ds(pl.multiple_of(b * block, block), block)
-        out_ref[span, :] = acc_ref[span, :].astype(BF16)
-        return 0
-
-    lax.fori_loop(0, rows // block, finish, 0)
+    block = out_ref.shape[0]
+
+    @pl.when(pl.program_id(0) == 0)
+    def _():
+        def clear(b, _):
+            span = pl.ds(pl.multiple_of(b * block, block), block)
+            acc_ref[span, :] = jnp.zeros((block, acc_ref.shape[1]), F32)
+            return 0
+
+        lax.fori_loop(0, rows // block, clear, 0)
+        end = pl.cdiv(meta_ref[COUNTS, 1], CHUNK)
+        over_chunks(
+            meta_ref[COUNTS, 0] // CHUNK,
+            end,
+            lambda c: spread_add(
+                c, end, offset, window, FAR_LOW, meta_ref, keys_ref, grad_ref, acc_ref, values_ref
+            ),
+        )
+
+    at = pl.multiple_of(pl.program_id(0) * block, block)
+    out_ref[...] = acc_ref[pl.ds(at, block), :].astype(BF16)
 
 
 def far_backward(meta, keys, grad_sum, offset, rows, window=1280):
     width = grad_sum.shape[1] // 2
+    block = min(1024, rows)
     return pl.pallas_call(
         functools.partial(far_backward_kernel, offset, min(window, rows)),
-        in_specs=[sspec(), vspec(), vspec()],
-        out_specs=vspec(),
-        out_shape=jax.ShapeDtypeStruct((rows, width), BF16),
+        grid=(rows // block,),
+        in_specs=[
+            sspec(),
+            pl.BlockSpec(keys.shape, lambda i: (0, 0)),
+            pl.BlockSpec(grad_sum.shape, lambda i: (0, 0)),
+        ],
+        out_specs=pl.BlockSpec((block, width), lambda i: (i, 0)),
+        out_shape=pltpu.HBM((rows, width), BF16),
         scratch_shapes=[VMEM((rows, width), F32), VMEM((UNROLL * CHUNK, width), BF16)],
         compiler_params=params(),
         name="far_backward",
     )(meta, keys, grad_sum)
 
 
-def near_backward_kernel(window, meta_ref, keys_ref, grad_ref, out_ref, values_ref):
-    out_ref[...] = jnp.zeros_like(out_ref)
+def near_backward_kernel(
+    window, half_ref, meta_ref, keys_ref, grad_ref, pre_ref, w_self_ref, out_ref, values_ref
+):
+    own_rows = pre_ref.shape[0] // 2
+    mine = pl.ds(pl.multiple_of(half_ref[0] * own_rows, own_rows), own_rows)
+    out_ref[:own_rows, :] = dot_nt(pre_ref[mine, :], w_self_ref[...])
+    out_ref[own_rows:, :] = jnp.zeros((out_ref.shape[0] - own_rows, out_ref.shape[1]), F32)
     end = pl.cdiv(meta_ref[COUNTS, 0], CHUNK)
     over_chunks(
         0,
@@ -390,17 +415,17 @@
     )
 
 
-def near_backward(meta, keys, grad_sum, rows, window=768):
+def near_backward(half, meta, keys, grad_sum, grad_pre, w_self, rows, window=768):
     width = grad_sum.shape[1] // 2
     return pl.pallas_call(
         functools.partial(near_backward_kernel, min(window, rows)),
-        in_specs=[sspec(), vspec(), vspec()],
+        in_specs=[sspec(), sspec()] + [vspec()] * 4,
         out_specs=vspec(),
         out_shape=jax.ShapeDtypeStruct((rows, width), F32),
         scratch_shapes=[VMEM((UNROLL * CHUNK, width), BF16)],
         compiler_params=params(),
         name="near_backward",
-    )(meta, keys, grad_sum)
+    )(half, meta, keys, grad_sum, grad_pre, w_self)
 
 
 def returned_kernel(peers_step, half_ref, idx_ref, back_ref, near_ref, part_ref, acc_ref):
@@ -472,6 +497,12 @@
     while len(parts) > 1:
         parts = [parts[i] + parts[i + 1] for i in range(0, len(parts), 2)]
     return parts[0]
+
+
+def split_exactly(value):
+    high = lax.reduce_precision(value, 8, 7)
+    middle = lax.reduce_precision(value - high, 8, 7)
+    return [part.astype(BF16) for part in (high, middle, value - high - middle)]
 
 
 def after(value, *earlier):
@@ -505,11 +536,10 @@
     hub_half = lax.dynamic_slice_in_dim(hub_feats, half * half_hubs, half_hubs, 0)
     hub_z = exchange(jnp.broadcast_to(hub_half[None], (zs,) + hub_half.shape), Z_AXIS, num_dom)
 
-    slot_ids = jnp.arange(block_rows, dtype=jnp.int32)[None, :]
-    idx_all = jnp.where(slot_ids < send_count[0][:, None], send_rows[0], -1)
-    idx = jnp.where(half == 0, idx_all[:, 0::2], idx_all[:, 1::2])
-    idx = idx.reshape(num_dom * slots // 128, 128)
-    out_rows = outgoing(idx, node_feats, slots)
+    me = lax.axis_index("dom")
+    counts_row = jnp.pad(send_count, ((0, 0), (0, -num_dom % 128)))
+    flip = ((half ^ me) & 1).astype(jnp.int32).reshape(1)
+    out_rows, idx = outgoing(flip, counts_row, send_rows[0], node_feats)
     out_rows, hub_z = lax.optimization_barrier((out_rows, hub_z))
     table = lax.all_to_all(out_rows, "dom", split_axis=0, concat_axis=0, tiled=True)
     hub_z = after(hub_z.reshape(zs * half_hubs, width), out_rows)
@@ -526,7 +556,6 @@
     hub = slot - num_dom * block_rows
     is_own, is_hub = src < nodes, hub >= 0
     master = hub // hubs
-    me = lax.axis_index("dom")
     far_y, far_x = (master ^ me) & (ys - 1), (master ^ me) // (ys * zs)
     master_place = (far_y * xs + far_x) * zs + (master // ys) % zs
     row = jnp.where(
@@ -535,10 +564,11 @@
         jnp.where(
             is_hub,
             own_rows + master_place * half_hubs + hub % half_hubs,
-            near_rows + slot // 2,
+            near_rows + slot // block_rows * slots + slot % slots,
         ),
     )
-    side = jnp.where(is_own, src // own_rows, jnp.where(is_hub, (hub % hubs) // half_hubs, slot % 2))
+    slot_side = (slot // slots ^ slot // block_rows ^ me) & 1
+    side = jnp.where(is_own, src // own_rows, jnp.where(is_hub, (hub % hubs) // half_hubs, slot_side))
     key = (side << HALF_BIT) + (row << DST_BITS) + dst
     key = after(jnp.where(live, key, DEAD), out_rows)
     key_other = lax.ppermute(key, "edge", SWAP)
@@ -563,7 +593,7 @@
     near_sum, degree = near_forward(meta, every, keys, near_table, nodes)
     neigh = far_forward(meta, keys, table.reshape(far_rows, width), near_sum, near_rows)
     neigh_other = lax.ppermute(neigh, "edge", SWAP)
-    layer_out, grad_sum, grad_input, grad_w = dense(
+    layer_out, grad_sum, grad_pre, grad_w = dense(
         half_scalar,
         neigh,
         neigh_other,
@@ -581,32 +611,46 @@
     back = lax.all_to_all(
         row_grads.reshape(num_dom, slots, width), "dom", split_axis=0, concat_axis=0, tiled=True
     )
-    near_grads = near_backward(meta, after(keys, row_grads), grad_sum, near_rows)
+    near_grads = near_backward(
+        half_scalar, meta, after(keys, row_grads), grad_sum, grad_pre, w_self, near_rows
+    )
 
     grad_w = jnp.sum(grad_w, axis=0)
-    hub_part = near_grads[own_rows:]
-    for axis, parts in ((Y_AXIS, ys), (X_AXIS, xs)):
-        blocks = jnp.split(hub_part, parts)
-        kept = blocks[0].shape[0]
-        both = pair_sum(
-            swap_blocks([jnp.concatenate([block, grad_w]) for block in blocks], axis, num_dom)
-        )
-        hub_part, grad_w = both[:kept], both[kept:]
-    hub_part = hub_part.reshape(zs, half_hubs, width)
-    both = jnp.concatenate([hub_part, jnp.broadcast_to(grad_w[None], (zs,) + grad_w.shape)], axis=1)
+    blocks = jnp.split(near_grads[own_rows:].astype(BF16), ys)
+    kept = blocks[0].shape[0]
+    pieces = split_exactly(grad_w)
+    both = swap_blocks([jnp.concatenate([block] + pieces) for block in blocks], Y_AXIS, num_dom)
+    both = [part.astype(F32) for part in both]
+    hub_part = pair_sum([part[:kept] for part in both])
+    grad_w = pair_sum(
+        [part[kept : kept + share] + (part[kept + share : -share] + part[-share:]) for part in both]
+    )
+    blocks = jnp.split(hub_part, xs)
+    kept = blocks[0].shape[0]
+    both = pair_sum(
+        swap_blocks([jnp.concatenate([block, grad_w]) for block in blocks], X_AXIS, num_dom)
+    )
+    other = lax.ppermute(both, "edge", SWAP)
+    first = jnp.where(half == 0, both, other)
+    second = jnp.where(half == 0, other, both)
+    shares = jnp.concatenate([first[kept:], second[kept:]])
+    both = jnp.concatenate(
+        [
+            first[:kept].reshape(zs, half_hubs, width),
+            second[:kept].reshape(zs, half_hubs, width),
+            jnp.broadcast_to(shares[None], (zs,) + shares.shape),
+        ],
+        axis=1,
+    )
     both = exchange(after(both, back), Z_AXIS, num_dom)
-    hub_part = jnp.sum(both[:, :half_hubs], axis=0)
-    grad_w = both[:, half_hubs:].reshape(zs * share, width)
+    grad_hubs = jnp.sum(both[:, :hubs], axis=0)
+    first = both[:, hubs : hubs + share].reshape(zs * share, width)
+    second = both[:, hubs + share :].reshape(zs * share, width)
+    grad_self, grad_neigh, grad_bias = first[:width], second[:width], first[width]
 
     part = returned_sum(half_scalar, idx, back, near_grads, nodes)
     part_other = lax.ppermute(part, "edge", SWAP)
-    small = jnp.concatenate([grad_w[:width], hub_part])
-    small_other = lax.ppermute(small, "edge", SWAP)
-    first = jnp.where(half == 0, small, small_other)
-    second = jnp.where(half == 0, small_other, small)
-    grad_self, grad_neigh, grad_bias = first[:width], second[:width], grad_w[width]
-    grad_hubs = jnp.concatenate([first[width:], second[width:]])
-    grad_feats = grad_input + (part + part_other)
+    grad_feats = part + part_other
     return (layer_out, grad_feats, grad_hubs, grad_self, grad_neigh, grad_bias)
 
 

time: 194 us -> 191 us (0.985)
  waiting for transfers between devices: 53.2 us -> 49.1 us
  Pallas kernels: 30.2 us -> 32.9 us
    ppermute x12, waiting for transfers between devices: 29.4 us -> 23.3 us  [swap_blocks(): lax.ppermute(block, 'dom', pairs)]
    pallas_call x1, Pallas kernels: 4.11 us -> 7.41 us  [far_backward(): pl.pallas_call(functools.partial(far_backward_kernel, offset, min(window,...]
    slice x9 -> x5, local copies, waits for them, and re-layouts: 3.21 us -> 0.97 us  [the longest x1 0.96 us: body(): second = both[:, hubs + share:].reshape(zs * share, width)]
    unnamed x41 -> x47, local copies, waits for them, and re-layouts: 12.8 us -> 13.5 us
  transfers between devices with their start and end apart: 21 -> 21, of which waited for: 13 -> 17; matrix products, arithmetic and copies ran while one was open for 13% -> 11% of each run, Pallas kernels for 13% -> 15%
where the time goes in v4:
time: 191 us; the launch traced here: 189 us
  starting transfers between devices  70.3 us (37%)
  waiting for transfers between devices  49.1 us (26%)
  Pallas kernels  32.9 us (17%)
  local copies, waits for them, and re-layouts  18.8 us (10%)
  other arithmetic  16.3 us (9%)
    ppermute x12, waiting for transfers between devices, swap_blocks(): lax.ppermute(block, 'dom', pairs)  23.3 us
    all_to_all x3, starting transfers between devices, exchange(): lax.all_to_all(blocks, 'dom', 0, 0, axis_index_groups=groups_of(size, axi...  20.1 us
    ppermute x12, starting transfers between devices, swap_blocks(): lax.ppermute(block, 'dom', pairs)  15.8 us
    all_to_all x1, starting transfers between devices, body(): lax.all_to_all(out_rows, 'dom', split_axis=0, concat_axis=0, tiled=True)  13.8 us
    unnamed x47, local copies, waits for them, and re-layouts  13.5 us
    all_to_all x1, waiting for transfers between devices, body(): lax.all_to_all(out_rows, 'dom', split_axis=0, concat_axis=0, tiled=True)  12.3 us
    all_to_all x1, starting transfers between devices, body(): lax.all_to_all(row_grads.reshape(num_dom, slots, width), 'dom', split_axi...  10.8 us
    pallas_call x1, Pallas kernels, near_forward(): pl.pallas_call(functools.partial(near_forward_kernel, min(window, table.s...  7.92 us
  transfers between devices with their start and end apart: 21, of which 17 were waited for; matrix products, arithmetic and copies ran while one was open for 11% of the time, Pallas kernels for 15%

profile of v4, /device:TPU:1, one launch (start us, length us, event | category | flops | bytes accessed | tf_op | source)
XLA Modules:
  0.0 189.1 jit_solution(18159583247097230473)
XLA Ops:
  2.0 9.0 %all-to-all-start = ((bf16[8,16,128]{2,1,0:T(8,128)(2,1)}), bf16[8,16,128]{2,1,0:T(8,128)(2,1)S(1)}, u32[]{:S(2)}, u32[]{:S(2)}) async-start(bf16[8,16,128]{2,1,0:T(8,128)(2,1)} %broadcast_in_dim.38), calls=%async_computation | async-start | bytes 65536 | tf_op jit(solution)/shard_map/all_to_all | solution.py:479
  13.4 4.1 %outgoing_rows.1 = (bf16[128,64,128]{2,1,0:T(8,128)(2,1)}, s32[64,128]{1,0:T(8,128)S(1)}) custom-call(s32[1]{0:T(128)} %bitcast.4.flip_ref, s32[1,128]{1,0:T(1,128)S(1)} %copy-done.15, s32[128,128]{1,0:T(8,128)S(1)} %bitcast.26, bf16[1024,128]{1,0:T(8,128)(2,1)S(1)} %copy-done.1), custom_call_target="tpu_custom_call" | custom-call | tf_op jit(solution)/shard_map/outgoing_rows/pallas_call | solution.py:116
  17.9 13.8 %all-to-all-start.1 = ((bf16[128,64,128]{2,1,0:T(8,128)(2,1)}), bf16[128,64,128]{2,1,0:T(8,128)(2,1)S(1)}, u32[]{:S(2)}, u32[]{:S(2)}) async-start(bf16[128,64,128]{2,1,0:T(8,128)(2,1)} %get-tuple-element.25), calls=%async_computation.1 | async-start | bytes 4194304 | tf_op jit(solution)/shard_map/all_to_all | solution.py:544
  34.2 2.6 %collective-permute-start.3 = (bf16[128,128]{1,0:T(8,128)(2,1)S(1)}, bf16[128,128]{1,0:T(8,128)(2,1)S(1)}, u32[]{:S(2)}, u32[]{:S(2)}) collective-permute-start(bf16[128,128]{1,0:T(8,128)(2,1)S(1)} %bitcast.34), channel_id=1, source_target_pairs={{0,192},{2,194},{4,196},{6,198},{8,200},{10,202},{12,204},{14,206}... | collective-permute-start | bytes 98312 | tf_op jit(solution)/shard_map/ppermute | solution.py:492
  38.1 2.5 %collective-permute-done.1 = bf16[128,128]{1,0:T(8,128)(2,1)S(1)} collective-permute-done((bf16[128,128]{1,0:T(8,128)(2,1)S(1)}, bf16[128,128]{1,0:T(8,128)(2,1)S(1)}, u32[]{:S(2)}, u32[]{:S(2)}) %collective-permute-start.1) | collective-permute-done | bytes 32800 | tf_op jit(solution)/shard_map/ppermute | solution.py:492
  42.6 2.4 %collective-permute-start.6 = (bf16[512,128]{1,0:T(8,128)(2,1)}, bf16[512,128]{1,0:T(8,128)(2,1)S(1)}, u32[]{:S(2)}, u32[]{:S(2)}) collective-permute-start(bf16[512,128]{1,0:T(8,128)(2,1)} %get-tuple-element.58), channel_id=1, source_target_pairs={{0,6},{2,4},{4,2},{6,0},{8,14},{10,12},{12,10},{14,8},{16,22},{18,... | collective-permute-start | bytes 393224 | tf_op jit(solution)/shard_map/ppermute | solution.py:492
  45.9 7.7 %sort.14 = (s32[16384]{0:T(1024)S(1)}, s32[16384]{0:T(1024)}) sort(s32[16384]{0:T(1024)S(1)} %and_select_fusion, s32[16384]{0:T(1024)S(1)} %iota.11), dimensions={0}, to_apply=%region_0.1 | sort | flops 229376 | bytes 262144 | tf_op jit(solution)/shard_map/sort | solution.py:577
  59.0 7.9 %near_forward.1 = (f32[512,256]{1,0:T(8,128)S(1)}, f32[16,128]{1,0:T(8,128)S(1)}) custom-call(s32[5,64]{1,0:T(8,128)S(1)} %stack.2.meta_ref, s32[64,256]{1,0:T(8,128)S(1)} %pad_add_fusion.every_ref, s32[64,256]{1,0:T(8,128)S(1)} %reshape.141.keys_ref, bf16[2560,128]{1,0:T(8,128)(2,1)S(1)} %constant_dynamic-update-slice_fusion.5.table_ref), custom_call_target="tpu_custom_call" | custom-call | tf_op jit(solution)/shard_map/near_forward/pallas_call | solution.py:257
  68.3 12.3 %all-to-all-done.1 = bf16[128,64,128]{2,1,0:T(8,128)(2,1)S(1)} async-done(((bf16[128,64,128]{2,1,0:T(8,128)(2,1)}), bf16[128,64,128]{2,1,0:T(8,128)(2,1)S(1)}, u32[]{:S(2)}, u32[]{:S(2)}) %all-to-all-start.1) | async-done | bytes 2097184 | tf_op jit(solution)/shard_map/all_to_all | solution.py:544
  81.7 3.6 %far_forward.1.mine_ref = f32[512,256]{1,0:T(8,128)S(1)} custom-call(s32[5,64]{1,0:T(8,128)S(1)} %stack.2.meta_ref, s32[64,256]{1,0:T(8,128)S(1)} %reshape.141.keys_ref, bf16[8192,128]{1,0:T(8,128)(2,1)S(1)} %bitcast.25, f32[512,256]{1,0:T(8,128)S(1)} %copy-done.6), custom_call_target="tpu_custom_call" | custom-call | tf_op jit(solution)/shard_map/far_forward/pallas_call | solution.py:286
  85.3 4.6 %collective-permute-start.7 = (f32[512,256]{1,0:T(8,128)S(1)}, f32[512,256]{1,0:T(8,128)S(1)}, u32[]{:S(2)}, u32[]{:S(2)}) collective-permute-start(f32[512,256]{1,0:T(8,128)S(1)} %far_forward.1.mine_ref), channel_id=1, source_target_pairs={{0,1},{1,0},{2,3},{3,2},{4,5},{5,4},{6,7},{7,6},{8,9},{9,8},{10,11... | collective-permute-start | bytes 1572872 | tf_op jit(solution)/shard_map/ppermute | solution.py:595
  94.5 4.6 %all-to-all-start.2 = ((f32[8,24,128]{2,1,0:T(8,128)}), f32[8,24,128]{2,1,0:T(8,128)S(1)}, u32[]{:S(2)}, u32[]{:S(2)}) async-start(f32[8,24,128]{2,1,0:T(8,128)} %bitcast.12), calls=%async_computation.2 | async-start | bytes 196608 | tf_op jit(solution)/shard_map/all_to_all | solution.py:479
  99.1 7.4 %far_backward.1 = bf16[8192,128]{1,0:T(8,128)(2,1)} custom-call(s32[5,64]{1,0:T(8,128)S(1)} %stack.2.meta_ref, s32[64,256]{1,0:T(8,128)S(1)} %reshape.141.keys_ref, bf16[512,256]{1,0:T(8,128)(2,1)S(1)} %get-tuple-element.34.grad_ref), custom_call_target="tpu_custom_call" | custom-call | tf_op jit(solution)/shard_map/far_backward/pallas_call | solution.py:385
  107.2 10.8 %all-to-all-start.3 = ((bf16[128,64,128]{2,1,0:T(8,128)(2,1)}), bf16[128,64,128]{2,1,0:T(8,128)(2,1)S(1)}, u32[]{:S(2)}, u32[]{:S(2)}) async-start(bf16[128,64,128]{2,1,0:T(8,128)(2,1)} %bitcast.28), calls=%async_computation.3 | async-start | bytes 4194304 | tf_op jit(solution)/shard_map/all_to_all | solution.py:611
  120.0 5.1 %near_backward.1.near_ref = f32[2560,128]{1,0:T(8,128)S(1)} custom-call(s32[1]{0:T(128)} %bitcast.half_ref, s32[5,64]{1,0:T(8,128)S(1)} %stack.2.meta_ref, s32[64,256]{1,0:T(8,128)S(1)} %reshape.141.keys_ref, bf16[512,256]{1,0:T(8,128)(2,1)S(1)} %copy-done.4, bf16[1024,128]{1,0:T(8,128)(2,1)S(1)} %copy-done.8, bf16[128,128]{1,0:T(8,128)(2,1)S(1)} %copy-done.10), custom_call_target="tpu_custom_call" | custom-call | tf_op jit(solution)/shard_map/near_backward/pallas_call | solution.py:420
  128.1 2.8 %collective-permute-start.9 = (bf16[584,128]{1,0:T(8,128)(2,1)S(1)}, bf16[584,128]{1,0:T(8,128)(2,1)S(1)}, u32[]{:S(2)}, u32[]{:S(2)}) collective-permute-start(bf16[584,128]{1,0:T(8,128)(2,1)S(1)} %get-tuple-element.67), channel_id=1, source_target_pairs={{0,2},{2,0},{4,6},{6,4},{8,10},{10,8},{12,14},{14,12},{16,18},{18,... | collective-permute-start | bytes 448520 | tf_op jit(solution)/shard_map/ppermute | solution.py:492
  133.4 3.0 %collective-permute-done.9 = bf16[584,128]{1,0:T(8,128)(2,1)S(1)} collective-permute-done((bf16[584,128]{1,0:T(8,128)(2,1)S(1)}, bf16[584,128]{1,0:T(8,128)(2,1)S(1)}, u32[]{:S(2)}, u32[]{:S(2)}) %collective-permute-start.9) | collective-permute-done | bytes 149536 | tf_op jit(solution)/shard_map/ppermute | solution.py:492
  136.4 5.5 %collective-permute-done.10 = bf16[584,128]{1,0:T(8,128)(2,1)S(1)} collective-permute-done((bf16[584,128]{1,0:T(8,128)(2,1)S(1)}, bf16[584,128]{1,0:T(8,128)(2,1)S(1)}, u32[]{:S(2)}, u32[]{:S(2)}) %collective-permute-start.10) | collective-permute-done | bytes 149536 | tf_op jit(solution)/shard_map/ppermute | solution.py:492
  141.9 5.6 %collective-permute-done.11 = bf16[584,128]{1,0:T(8,128)(2,1)S(1)} collective-permute-done((bf16[584,128]{1,0:T(8,128)(2,1)S(1)}, bf16[584,128]{1,0:T(8,128)(2,1)S(1)}, u32[]{:S(2)}, u32[]{:S(2)}) %collective-permute-start.11) | collective-permute-done | bytes 149536 | tf_op jit(solution)/shard_map/ppermute | solution.py:492
  154.0 3.3 %collective-permute-done.13 = f32[152,128]{1,0:T(8,128)S(1)} collective-permute-done((f32[152,128]{1,0:T(8,128)S(1)}, f32[152,128]{1,0:T(8,128)S(1)}, u32[]{:S(2)}, u32[]{:S(2)}) %collective-permute-start.13) | collective-permute-done | bytes 77856 | tf_op jit(solution)/shard_map/ppermute | solution.py:492
  161.8 5.3 %all-to-all-done.3.back_ref = bf16[128,64,128]{2,1,0:T(8,128)(2,1)S(1)} async-done(((bf16[128,64,128]{2,1,0:T(8,128)(2,1)}), bf16[128,64,128]{2,1,0:T(8,128)(2,1)S(1)}, u32[]{:S(2)}, u32[]{:S(2)}) %all-to-all-start.3) | async-done | bytes 2097184 | tf_op jit(solution)/shard_map/all_to_all | solution.py:611
  167.1 6.5 %all-to-all-start.4 = ((f32[8,80,128]{2,1,0:T(8,128)}), f32[8,80,128]{2,1,0:T(8,128)}, u32[]{:S(2)}, u32[]{:S(2)}) async-start(f32[8,80,128]{2,1,0:T(8,128)} %pad_maximum_fusion), calls=%async_computation.4 | async-start | bytes 655360 | tf_op jit(solution)/shard_map/all_to_all | solution.py:479
  173.6 3.4 %returned_sum.1 = f32[1024,128]{1,0:T(8,128)S(1)} custom-call(s32[1]{0:T(128)} %bitcast.half_ref, s32[64,128]{1,0:T(8,128)S(1)} %get-tuple-element.33.idx_ref, bf16[128,64,128]{2,1,0:T(8,128)(2,1)S(1)} %all-to-all-done.3.back_ref, f32[2560,128]{1,0:T(8,128)S(1)} %near_backward.1.near_ref), custom_call_target="tpu_custom_call" | custom-call | tf_op jit(solution)/shard_map/returned_sum/pallas_call | solution.py:453
  181.3 3.6 %all-to-all-done.4 = f32[8,80,128]{2,1,0:T(8,128)} async-done(((f32[8,80,128]{2,1,0:T(8,128)}), f32[8,80,128]{2,1,0:T(8,128)}, u32[]{:S(2)}, u32[]{:S(2)}) %all-to-all-start.4) | async-done | bytes 327712 | tf_op jit(solution)/shard_map/all_to_all | solution.py:479
  (119 shorter events, 49.9 us)
Async XLA Ops:
  2.0 15.9 %all-to-all-start = ((bf16[8,16,128]{2,1,0:T(8,128)(2,1)}), bf16[8,16,128]{2,1,0:T(8,128)(2,1)S(1)}, u32[]{:S(2)}, u32[]{:S(2)}) async-start(bf16[8,16,128]{2,1,0:T(8,128)(2,1)} %broadcast_in_dim.38), calls=%async_computation | async-start | bytes 65536 | tf_op jit(solution)/shard_map/all_to_all | solution.py:479
  17.9 14.5 %copy-start.19 = (s32[1,1,8192]{2,1,0:T(1,128)S(1)}, s32[1,1,8192]{2,1,0:T(1,128)}, u32[]{:S(2)}) copy-start(s32[1,1,8192]{2,1,0:T(1,128)} %param.19) | copy-start | bytes 98308
  17.9 62.8 %all-to-all-start.1 = ((bf16[128,64,128]{2,1,0:T(8,128)(2,1)}), bf16[128,64,128]{2,1,0:T(8,128)(2,1)S(1)}, u32[]{:S(2)}, u32[]{:S(2)}) async-start(bf16[128,64,128]{2,1,0:T(8,128)(2,1)} %get-tuple-element.25), calls=%async_computation.1 | async-start | bytes 4194304 | tf_op jit(solution)/shard_map/all_to_all | solution.py:544
  32.6 13.3 %collective-permute-start = (s32[8192]{0:T(1024)S(1)}, s32[8192]{0:T(1024)S(1)}, u32[]{:S(2)}, u32[]{:S(2)}) collective-permute-start(s32[8192]{0:T(1024)S(1)} %fusion.11), channel_id=1, source_target_pairs={{0,1},{1,0},{2,3},{3,2},{4,5},{5,4},{6,7},{7,6},{8,9},{9,8},{10,11... | collective-permute-start | bytes 98312 | tf_op jit(solution)/shard_map/ppermute | solution.py:574
  34.2 7.8 %collective-permute-start.3 = (bf16[128,128]{1,0:T(8,128)(2,1)S(1)}, bf16[128,128]{1,0:T(8,128)(2,1)S(1)}, u32[]{:S(2)}, u32[]{:S(2)}) collective-permute-start(bf16[128,128]{1,0:T(8,128)(2,1)S(1)} %bitcast.34), channel_id=1, source_target_pairs={{0,192},{2,194},{4,196},{6,198},{8,200},{10,202},{12,204},{14,206}... | collective-permute-start | bytes 98312 | tf_op jit(solution)/shard_map/ppermute | solution.py:492
  36.8 4.6 %collective-permute-start.2 = (bf16[128,128]{1,0:T(8,128)(2,1)S(1)}, bf16[128,128]{1,0:T(8,128)(2,1)S(1)}, u32[]{:S(2)}, u32[]{:S(2)}) collective-permute-start(bf16[128,128]{1,0:T(8,128)(2,1)S(1)} %bitcast.35), channel_id=1, source_target_pairs={{0,128},{2,130},{4,132},{6,134},{8,136},{10,138},{12,140},{14,142}... | collective-permute-start | bytes 98312 | tf_op jit(solution)/shard_map/ppermute | solution.py:492
  37.0 3.6 %collective-permute-start.1 = (bf16[128,128]{1,0:T(8,128)(2,1)S(1)}, bf16[128,128]{1,0:T(8,128)(2,1)S(1)}, u32[]{:S(2)}, u32[]{:S(2)}) collective-permute-start(bf16[128,128]{1,0:T(8,128)(2,1)S(1)} %bitcast.36), channel_id=1, source_target_pairs={{0,64},{2,66},{4,68},{6,70},{8,72},{10,74},{12,76},{14,78},{16,80}... | collective-permute-start | bytes 98312 | tf_op jit(solution)/shard_map/ppermute | solution.py:492
  42.6 16.3 %collective-permute-start.6 = (bf16[512,128]{1,0:T(8,128)(2,1)}, bf16[512,128]{1,0:T(8,128)(2,1)S(1)}, u32[]{:S(2)}, u32[]{:S(2)}) collective-permute-start(bf16[512,128]{1,0:T(8,128)(2,1)} %get-tuple-element.58), channel_id=1, source_target_pairs={{0,6},{2,4},{4,2},{6,0},{8,14},{10,12},{12,10},{14,8},{16,22},{18,... | collective-permute-start | bytes 393224 | tf_op jit(solution)/shard_map/ppermute | solution.py:492
  45.1 12.9 %collective-permute-start.5 = (bf16[512,128]{1,0:T(8,128)(2,1)}, bf16[512,128]{1,0:T(8,128)(2,1)}, u32[]{:S(2)}, u32[]{:S(2)}) collective-permute-start(bf16[512,128]{1,0:T(8,128)(2,1)} %get-tuple-element.58), channel_id=1, source_target_pairs={{0,4},{2,6},{4,0},{6,2},{8,12},{10,14},{12,8},{14,10},{16,20},{18,... | collective-permute-start | bytes 393224 | tf_op jit(solution)/shard_map/ppermute | solution.py:492
  45.8 11.2 %collective-permute-start.4 = (bf16[512,128]{1,0:T(8,128)(2,1)}, bf16[512,128]{1,0:T(8,128)(2,1)}, u32[]{:S(2)}, u32[]{:S(2)}) collective-permute-start(bf16[512,128]{1,0:T(8,128)(2,1)} %get-tuple-element.58), channel_id=1, source_target_pairs={{0,2},{2,0},{4,6},{6,4},{8,10},{10,8},{12,14},{14,12},{16,18},{18,... | collective-permute-start | bytes 393224 | tf_op jit(solution)/shard_map/ppermute | solution.py:492
  58.9 32.5 %copy-start.10 = (bf16[128,128]{1,0:T(8,128)(2,1)S(1)}, bf16[128,128]{1,0:T(8,128)(2,1)}, u32[]{:S(2)}) copy-start(bf16[128,128]{1,0:T(8,128)(2,1)} %w_self_ref.3) | copy-start | bytes 98308
  58.9 32.5 %copy-start.16 = (f32[128]{0:T(128)S(1)}, f32[128]{0:T(128)}, u32[]{:S(2)}) copy-start(f32[128]{0:T(128)} %param.15) | copy-start | bytes 1540
  85.3 6.2 %collective-permute-start.7 = (f32[512,256]{1,0:T(8,128)S(1)}, f32[512,256]{1,0:T(8,128)S(1)}, u32[]{:S(2)}, u32[]{:S(2)}) collective-permute-start(f32[512,256]{1,0:T(8,128)S(1)} %far_forward.1.mine_ref), channel_id=1, source_target_pairs={{0,1},{1,0},{2,3},{3,2},{4,5},{5,4},{6,7},{7,6},{8,9},{9,8},{10,11... | collective-permute-start | bytes 1572872 | tf_op jit(solution)/shard_map/ppermute | solution.py:595
  94.5 12.0 %all-to-all-start.2 = ((f32[8,24,128]{2,1,0:T(8,128)}), f32[8,24,128]{2,1,0:T(8,128)S(1)}, u32[]{:S(2)}, u32[]{:S(2)}) async-start(f32[8,24,128]{2,1,0:T(8,128)} %bitcast.12), calls=%async_computation.2 | async-start | bytes 196608 | tf_op jit(solution)/shard_map/all_to_all | solution.py:479
  107.2 59.9 %all-to-all-start.3 = ((bf16[128,64,128]{2,1,0:T(8,128)(2,1)}), bf16[128,64,128]{2,1,0:T(8,128)(2,1)S(1)}, u32[]{:S(2)}, u32[]{:S(2)}) async-start(bf16[128,64,128]{2,1,0:T(8,128)(2,1)} %bitcast.28), calls=%async_computation.3 | async-start | bytes 4194304 | tf_op jit(solution)/shard_map/all_to_all | solution.py:611
  128.1 8.3 %collective-permute-start.9 = (bf16[584,128]{1,0:T(8,128)(2,1)S(1)}, bf16[584,128]{1,0:T(8,128)(2,1)S(1)}, u32[]{:S(2)}, u32[]{:S(2)}) collective-permute-start(bf16[584,128]{1,0:T(8,128)(2,1)S(1)} %get-tuple-element.67), channel_id=1, source_target_pairs={{0,2},{2,0},{4,6},{6,4},{8,10},{10,8},{12,14},{14,12},{16,18},{18,... | collective-permute-start | bytes 448520 | tf_op jit(solution)/shard_map/ppermute | solution.py:492
  130.9 11.0 %collective-permute-start.10 = (bf16[584,128]{1,0:T(8,128)(2,1)S(1)}, bf16[584,128]{1,0:T(8,128)(2,1)S(1)}, u32[]{:S(2)}, u32[]{:S(2)}) collective-permute-start(bf16[584,128]{1,0:T(8,128)(2,1)S(1)} %get-tuple-element.68), channel_id=1, source_target_pairs={{0,4},{2,6},{4,0},{6,2},{8,12},{10,14},{12,8},{14,10},{16,20},{18,... | collective-permute-start | bytes 448520 | tf_op jit(solution)/shard_map/ppermute | solution.py:492
  132.5 15.0 %collective-permute-start.11 = (bf16[584,128]{1,0:T(8,128)(2,1)S(1)}, bf16[584,128]{1,0:T(8,128)(2,1)S(1)}, u32[]{:S(2)}, u32[]{:S(2)}) collective-permute-start(bf16[584,128]{1,0:T(8,128)(2,1)S(1)} %get-tuple-element.69), channel_id=1, source_target_pairs={{0,6},{2,4},{4,2},{6,0},{8,14},{10,12},{12,10},{14,8},{16,22},{18,... | collective-permute-start | bytes 448520 | tf_op jit(solution)/shard_map/ppermute | solution.py:492
  147.7 5.5 %collective-permute-start.14 = (f32[152,128]{1,0:T(8,128)S(1)}, f32[152,128]{1,0:T(8,128)S(1)}, u32[]{:S(2)}, u32[]{:S(2)}) collective-permute-start(f32[152,128]{1,0:T(8,128)S(1)} %get-tuple-element.70), channel_id=1, source_target_pairs={{0,192},{2,194},{4,196},{6,198},{8,200},{10,202},{12,204},{14,206}... | collective-permute-start | bytes 233480 | tf_op jit(solution)/shard_map/ppermute | solution.py:492
  149.3 4.7 %collective-permute-start.12 = (f32[152,128]{1,0:T(8,128)S(1)}, f32[152,128]{1,0:T(8,128)S(1)}, u32[]{:S(2)}, u32[]{:S(2)}) collective-permute-start(f32[152,128]{1,0:T(8,128)S(1)} %get-tuple-element.71), channel_id=1, source_target_pairs={{0,64},{2,66},{4,68},{6,70},{8,72},{10,74},{12,76},{14,78},{16,80}... | collective-permute-start | bytes 233480 | tf_op jit(solution)/shard_map/ppermute | solution.py:492
  149.3 8.0 %collective-permute-start.13 = (f32[152,128]{1,0:T(8,128)S(1)}, f32[152,128]{1,0:T(8,128)S(1)}, u32[]{:S(2)}, u32[]{:S(2)}) collective-permute-start(f32[152,128]{1,0:T(8,128)S(1)} %get-tuple-element.72), channel_id=1, source_target_pairs={{0,128},{2,130},{4,132},{6,134},{8,136},{10,138},{12,140},{14,142}... | collective-permute-start | bytes 233480 | tf_op jit(solution)/shard_map/ppermute | solution.py:492
  157.3 2.7 %collective-permute-start.15 = (f32[152,128]{1,0:T(8,128)S(1)}, f32[152,128]{1,0:T(8,128)}, u32[]{:S(2)}, u32[]{:S(2)}) collective-permute-start(f32[152,128]{1,0:T(8,128)S(1)} %fusion.3), channel_id=1, source_target_pairs={{0,1},{1,0},{2,3},{3,2},{4,5},{5,4},{6,7},{7,6},{8,9},{9,8},{10,11... | collective-permute-start | bytes 233480 | tf_op jit(solution)/shard_map/ppermute | solution.py:633
  167.1 17.8 %all-to-all-start.4 = ((f32[8,80,128]{2,1,0:T(8,128)}), f32[8,80,128]{2,1,0:T(8,128)}, u32[]{:S(2)}, u32[]{:S(2)}) async-start(f32[8,80,128]{2,1,0:T(8,128)} %pad_maximum_fusion), calls=%async_computation.4 | async-start | bytes 655360 | tf_op jit(solution)/shard_map/all_to_all | solution.py:479
  177.0 3.4 %collective-permute-start.8 = (f32[1024,128]{1,0:T(8,128)S(1)}, f32[1024,128]{1,0:T(8,128)S(1)}, u32[]{:S(2)}, u32[]{:S(2)}) collective-permute-start(f32[1024,128]{1,0:T(8,128)S(1)} %returned_sum.1), channel_id=1, source_target_pairs={{0,1},{1,0},{2,3},{3,2},{4,5},{5,4},{6,7},{7,6},{8,9},{9,8},{10,11... | collective-permute-start | bytes 1572872 | tf_op jit(solution)/shard_map/ppermute | solution.py:652
  (17 other events, 72.7 us)

commit v5 on v4

--- a/solution.py
+++ b/solution.py
@@ -31,6 +31,20 @@
     return pl.BlockSpec(memory_space=VMEM)
 
 
+def hbm_spec():
+    return pl.BlockSpec(memory_space=pltpu.HBM)
+
+
+def copy_now(source, target, sem):
+    copy = pltpu.make_async_copy(source, target, sem)
+    copy.start()
+    copy.wait()
+
+
+def whole(value):
+    return pl.BlockSpec(value.shape, lambda i: (0,) * len(value.shape))
+
+
 def sspec():
     return pl.BlockSpec(memory_space=SMEM)
 
@@ -53,6 +67,10 @@
 def onehot_of_rows(row, height):
     sub = lax.broadcasted_iota(jnp.int32, (height, row.shape[1]), 0).astype(I16)
     return jnp.where(sub == row.astype(I16), jnp.ones((), BF16), jnp.zeros((), BF16))
+
+
+def in_hbm(value):
+    return pltpu.with_memory_space_constraint(value, pltpu.HBM)
 
 
 def dot(a, b):
@@ -226,7 +244,7 @@
 
 
 def near_forward_kernel(
-    window, meta_ref, every_ref, keys_ref, table_ref, sum_ref, deg_ref, values_ref
+    window, meta_ref, every_ref, keys_ref, table_ref, sum_hbm, deg_hbm, sum_ref, deg_ref, values_ref, sem
 ):
     nodes = 2 * sum_ref.shape[0]
     deg_ref[...] = jnp.zeros_like(deg_ref)
@@ -250,28 +268,31 @@
             c, end, 0, window, NEAR_LOW, meta_ref, keys_ref, table_ref, sum_ref, values_ref
         ),
     )
+    copy_now(sum_ref, sum_hbm, sem)
+    copy_now(deg_ref, deg_hbm, sem)
 
 
 def near_forward(meta, every, keys, table, nodes, window=768):
     width = table.shape[1]
+    shapes = [(nodes // 2, 2 * width), (16, 128)]
     return pl.pallas_call(
         functools.partial(near_forward_kernel, min(window, table.shape[0])),
         in_specs=[sspec(), vspec(), vspec(), vspec()],
-        out_specs=[vspec(), vspec()],
-        out_shape=[
-            jax.ShapeDtypeStruct((nodes // 2, 2 * width), F32),
-            jax.ShapeDtypeStruct((16, 128), F32),
-        ],
-        scratch_shapes=[VMEM((UNROLL * CHUNK, width), F32)],
+        out_specs=[hbm_spec(), hbm_spec()],
+        out_shape=[pltpu.HBM(shape, F32) for shape in shapes],
+        scratch_shapes=[VMEM(shape, F32) for shape in shapes]
+        + [VMEM((UNROLL * CHUNK, width), F32), pltpu.SemaphoreType.DMA],
         compiler_params=params(),
         name="near_forward",
     )(meta, every, keys, table)
 
 
 def far_forward_kernel(
-    offset, window, meta_ref, keys_ref, table_ref, base_ref, sum_ref, values_ref
+    offset, window, meta_ref, keys_ref, table_ref, base_hbm, sum_ref, values_ref, base_ref, sem
 ):
-    sum_ref[...] = base_ref[...]
+    base_copy = pltpu.make_async_copy(base_hbm, base_ref, sem)
+    base_copy.start()
+    sum_ref[...] = jnp.zeros_like(sum_ref)
     end = pl.cdiv(meta_ref[COUNTS, 1], CHUNK)
     over_chunks(
         meta_ref[COUNTS, 0] // CHUNK,
@@ -280,18 +301,24 @@
             c, end, offset, window, FAR_LOW, meta_ref, keys_ref, table_ref, sum_ref, values_ref
         ),
     )
+    base_copy.wait()
+    sum_ref[...] += base_ref[...]
 
 
 def far_forward(meta, keys, table, base, offset, window=1280):
     return pl.pallas_call(
         functools.partial(far_forward_kernel, offset, min(window, table.shape[0])),
-        in_specs=[sspec(), vspec(), vspec(), vspec()],
+        in_specs=[sspec(), vspec(), vspec(), hbm_spec()],
         out_specs=vspec(),
         out_shape=jax.ShapeDtypeStruct(base.shape, F32),
-        scratch_shapes=[VMEM((UNROLL * CHUNK, table.shape[1]), F32)],
+        scratch_shapes=[
+            VMEM((UNROLL * CHUNK, table.shape[1]), F32),
+            VMEM(base.shape, F32),
+            pltpu.SemaphoreType.DMA,
+        ],
         compiler_params=params(),
         name="far_forward",
-    )(meta, keys, table, base)
+    )(meta, keys, table, in_hbm(base))
 
 
 def dense_kernel(
@@ -338,20 +365,22 @@
 
 def dense(half, mine, other, deg, feats, cot, w_self, w_neigh, bias):
     nodes, width = feats.shape
+    outs = [
+        jax.ShapeDtypeStruct((nodes, width), BF16),
+        jax.ShapeDtypeStruct((nodes // 2, 2 * width), BF16),
+        jax.ShapeDtypeStruct((nodes, width), BF16),
+        jax.ShapeDtypeStruct((192, width), F32),
+    ]
     return pl.pallas_call(
         dense_kernel,
-        in_specs=[sspec()] + [vspec()] * 8,
-        out_specs=[vspec()] * 4,
-        out_shape=[
-            jax.ShapeDtypeStruct((nodes, width), BF16),
-            jax.ShapeDtypeStruct((nodes // 2, 2 * width), BF16),
-            jax.ShapeDtypeStruct((nodes, width), BF16),
-            jax.ShapeDtypeStruct((192, width), F32),
-        ],
+        grid=(1,),
+        in_specs=[sspec()] + [whole(x) for x in (mine, other, deg, feats, cot, w_self, w_neigh, bias)],
+        out_specs=[whole(x) for x in outs],
+        out_shape=outs,
         scratch_shapes=[VMEM((nodes, width), BF16)],
         compiler_params=params(),
         name="dense_part",
-    )(half, mine, other, deg, feats, cot, w_self, w_neigh, bias)
+    )(half, mine, other, in_hbm(deg), in_hbm(feats), in_hbm(cot), in_hbm(w_self), in_hbm(w_neigh), in_hbm(bias))
 
 
 def far_backward_kernel(offset, window, meta_ref, keys_ref, grad_ref, out_ref, acc_ref, values_ref):
@@ -381,7 +410,7 @@
 
 def far_backward(meta, keys, grad_sum, offset, rows, window=1280):
     width = grad_sum.shape[1] // 2
-    block = min(1024, rows)
+    block = min(2048, rows)
     return pl.pallas_call(
         functools.partial(far_backward_kernel, offset, min(window, rows)),
         grid=(rows // block,),
@@ -428,7 +457,9 @@
     )(half, meta, keys, grad_sum, grad_pre, w_self)
 
 
-def returned_kernel(peers_step, half_ref, idx_ref, back_ref, near_ref, part_ref, acc_ref):
+def returned_kernel(
+    peers_step, half_ref, idx_ref, back_ref, near_ref, part_hbm, part_ref, acc_ref, sem
+):
     nodes = part_ref.shape[0]
     own_rows = nodes // 2
     peers, slots, width = back_ref.shape
@@ -446,6 +477,7 @@
     part_ref[own_rows:, :] = acc_ref[:, width:]
     own_span = pl.ds(pl.multiple_of(half_ref[0] * own_rows, own_rows), own_rows)
     part_ref[own_span, :] += near_ref[:own_rows, :]
+    copy_now(part_ref, part_hbm, sem)
 
 
 def returned_sum(half, idx, back, near, nodes):
@@ -453,12 +485,49 @@
     return pl.pallas_call(
         functools.partial(returned_kernel, min(32, back.shape[0])),
         in_specs=[sspec(), vspec(), vspec(), vspec()],
-        out_specs=vspec(),
-        out_shape=jax.ShapeDtypeStruct((nodes, width), F32),
-        scratch_shapes=[VMEM((nodes // 2, 2 * width), F32)],
+        out_specs=hbm_spec(),
+        out_shape=pltpu.HBM((nodes, width), F32),
+        scratch_shapes=[
+            VMEM((nodes, width), F32),
+            VMEM((nodes // 2, 2 * width), F32),
+            pltpu.SemaphoreType.DMA,
+        ],
         compiler_params=params(),
         name="returned_sum",
     )(half, idx, back, near)
+
+
+def finish_kernel(
+    hubs, mine_ref, other_ref, both_ref, feats_ref, hubs_ref, self_ref, neigh_ref, bias_ref
+):
+    width = mine_ref.shape[1]
+    places = both_ref.shape[0]
+    share = (both_ref.shape[1] - hubs) // 2
+    feats_ref[...] = mine_ref[...] + other_ref[...]
+    hubs_ref[...] = pair_sum([both_ref[j, :hubs, :] for j in range(places)])
+    for row in range(0, width, 8):
+        j, at = row // share, hubs + row % share
+        self_ref[row : row + 8, :] = both_ref[j, at : at + 8, :]
+        neigh_ref[row : row + 8, :] = both_ref[j, at + share : at + share + 8, :]
+    at = hubs + width % share
+    bias_ref[...] = both_ref[width // share, at : at + 8, :]
+
+
+def finish(mine, other, both, hubs):
+    nodes, width = mine.shape
+    outs = [
+        jax.ShapeDtypeStruct(shape, F32)
+        for shape in ((nodes, width), (hubs, width), (width, width), (width, width), (8, width))
+    ]
+    return pl.pallas_call(
+        functools.partial(finish_kernel, hubs),
+        grid=(1,),
+        in_specs=[whole(x) for x in (mine, other, both)],
+        out_specs=[whole(x) for x in outs],
+        out_shape=outs,
+        compiler_params=params(),
+        name="finish",
+    )(in_hbm(mine), in_hbm(other), in_hbm(both))
 
 
 def torus_of(size):
@@ -482,8 +551,8 @@
 
 
 def partners(size, axis):
-    step, count = ((torus_of(size)[2] * torus_of(size)[1], torus_of(size)[0]) if axis == X_AXIS
-                   else (1, torus_of(size)[2]))
+    sizes = torus_of(size)
+    step, count = {X_AXIS: sizes[1] * sizes[2], Z_AXIS: sizes[2], Y_AXIS: 1}[axis], sizes[axis]
     return [[(i, i ^ (step * j)) for i in range(size)] for j in range(1, count)]
 
 
@@ -643,15 +712,10 @@
         axis=1,
     )
     both = exchange(after(both, back), Z_AXIS, num_dom)
-    grad_hubs = jnp.sum(both[:, :hubs], axis=0)
-    first = both[:, hubs : hubs + share].reshape(zs * share, width)
-    second = both[:, hubs + share :].reshape(zs * share, width)
-    grad_self, grad_neigh, grad_bias = first[:width], second[:width], first[width]
-
     part = returned_sum(half_scalar, idx, back, near_grads, nodes)
     part_other = lax.ppermute(part, "edge", SWAP)
-    grad_feats = part + part_other
-    return (layer_out, grad_feats, grad_hubs, grad_self, grad_neigh, grad_bias)
+    grad_feats, grad_hubs, grad_self, grad_neigh, grad_bias = finish(part, part_other, both, hubs)
+    return (layer_out, grad_feats, grad_hubs, grad_self, grad_neigh, grad_bias[0])
 
 
 def solution(mesh):

time: 191 us -> 187 us (0.979)
  local copies, waits for them, and re-layouts: 18.8 us -> 12.6 us
  Pallas kernels: 32.9 us -> 36.7 us
  other arithmetic: 16.3 us -> 13.9 us
    unnamed x47 -> x39, local copies, waits for them, and re-layouts: 13.5 us -> 9.54 us
    pallas_call x1 -> x2, Pallas kernels: 1.4 us -> 4.64 us  [the longest x1 2.47 us: dense(): pl.pallas_call(dense_kernel, grid=(1,), in_specs=[sspec()] + [whole(x) fo...]
    ppermute x12, waiting for transfers between devices: 23.3 us -> 20.4 us  [swap_blocks(): lax.ppermute(block, 'dom', pairs)]
    slice x3 -> x0, local copies, waits for them, and re-layouts: 2.22 us -> none  [the longest x1 0.96 us: body(): second = both[:, hubs + share:].reshape(zs * share, width)]
  transfers between devices with their start and end apart: 21 -> 21, of which waited for: 17 -> 16; matrix products, arithmetic and copies ran while one was open for 11% -> 10% of each run, Pallas kernels for 15% -> 15%
where the time goes in v5:
time: 187 us; the launch traced here: 185 us
  starting transfers between devices  71.4 us (38%)
  waiting for transfers between devices  49.2 us (26%)
  Pallas kernels  36.7 us (20%)
  other arithmetic  13.9 us (7%)
  local copies, waits for them, and re-layouts  12.6 us (7%)
    ppermute x12, waiting for transfers between devices, swap_blocks(): lax.ppermute(block, 'dom', pairs)  20.4 us
    all_to_all x3, starting transfers between devices, exchange(): lax.all_to_all(blocks, 'dom', 0, 0, axis_index_groups=groups_of(size, axi...  19.3 us
    ppermute x12, starting transfers between devices, swap_blocks(): lax.ppermute(block, 'dom', pairs)  16.6 us
    all_to_all x1, starting transfers between devices, body(): lax.all_to_all(out_rows, 'dom', split_axis=0, concat_axis=0, tiled=True)  13.8 us
    all_to_all x1, waiting for transfers between devices, body(): lax.all_to_all(out_rows, 'dom', split_axis=0, concat_axis=0, tiled=True)  12.3 us
    all_to_all x1, starting transfers between devices, body(): lax.all_to_all(row_grads.reshape(num_dom, slots, width), 'dom', split_axi...  10.6 us
    unnamed x39, local copies, waits for them, and re-layouts  9.54 us
    pallas_call x1, Pallas kernels, near_forward(): pl.pallas_call(functools.partial(near_forward_kernel, min(window, table.s...  9.32 us
  transfers between devices with their start and end apart: 21, of which 16 were waited for; matrix products, arithmetic and copies ran while one was open for 10% of the time, Pallas kernels for 15%

profile of v5, /device:TPU:1, one launch (start us, length us, event | category | flops | bytes accessed | tf_op | source)
XLA Modules:
  0.0 185.4 jit_solution(13945020076172146602)
XLA Ops:
  2.0 9.0 %all-to-all-start = ((bf16[8,16,128]{2,1,0:T(8,128)(2,1)}), bf16[8,16,128]{2,1,0:T(8,128)(2,1)S(1)}, u32[]{:S(2)}, u32[]{:S(2)}) async-start(bf16[8,16,128]{2,1,0:T(8,128)(2,1)} %broadcast_in_dim.38), calls=%async_computation | async-start | bytes 65536 | tf_op jit(solution)/shard_map/all_to_all | solution.py:548
  13.4 4.1 %outgoing_rows.1 = (bf16[128,64,128]{2,1,0:T(8,128)(2,1)}, s32[64,128]{1,0:T(8,128)S(1)}) custom-call(s32[1]{0:T(128)} %bitcast.4.flip_ref, s32[1,128]{1,0:T(1,128)S(1)} %copy-done.11, s32[128,128]{1,0:T(8,128)S(1)} %bitcast.24, bf16[1024,128]{1,0:T(8,128)(2,1)S(1)} %copy-done.1), custom_call_target="tpu_custom_call" | custom-call | tf_op jit(solution)/shard_map/outgoing_rows/pallas_call | solution.py:134
  17.9 13.8 %all-to-all-start.1 = ((bf16[128,64,128]{2,1,0:T(8,128)(2,1)}), bf16[128,64,128]{2,1,0:T(8,128)(2,1)S(1)}, u32[]{:S(2)}, u32[]{:S(2)}) async-start(bf16[128,64,128]{2,1,0:T(8,128)(2,1)} %get-tuple-element.30), calls=%async_computation.1 | async-start | bytes 4194304 | tf_op jit(solution)/shard_map/all_to_all | solution.py:613
  34.2 2.6 %collective-permute-start.3 = (bf16[128,128]{1,0:T(8,128)(2,1)S(1)}, bf16[128,128]{1,0:T(8,128)(2,1)S(1)}, u32[]{:S(2)}, u32[]{:S(2)}) collective-permute-start(bf16[128,128]{1,0:T(8,128)(2,1)S(1)} %bitcast.28), channel_id=1, source_target_pairs={{0,192},{2,194},{4,196},{6,198},{8,200},{10,202},{12,204},{14,206}... | collective-permute-start | bytes 98312 | tf_op jit(solution)/shard_map/ppermute | solution.py:561
  38.1 2.5 %collective-permute-done.1 = bf16[128,128]{1,0:T(8,128)(2,1)S(1)} collective-permute-done((bf16[128,128]{1,0:T(8,128)(2,1)S(1)}, bf16[128,128]{1,0:T(8,128)(2,1)S(1)}, u32[]{:S(2)}, u32[]{:S(2)}) %collective-permute-start.1) | collective-permute-done | bytes 32800 | tf_op jit(solution)/shard_map/ppermute | solution.py:561
  42.7 2.5 %collective-permute-start.6 = (bf16[512,128]{1,0:T(8,128)(2,1)}, bf16[512,128]{1,0:T(8,128)(2,1)S(1)}, u32[]{:S(2)}, u32[]{:S(2)}) collective-permute-start(bf16[512,128]{1,0:T(8,128)(2,1)} %get-tuple-element.66), channel_id=1, source_target_pairs={{0,6},{2,4},{4,2},{6,0},{8,14},{10,12},{12,10},{14,8},{16,22},{18,... | collective-permute-start | bytes 393224 | tf_op jit(solution)/shard_map/ppermute | solution.py:561
  45.9 7.7 %sort.14 = (s32[16384]{0:T(1024)S(1)}, s32[16384]{0:T(1024)}) sort(s32[16384]{0:T(1024)S(1)} %and_select_fusion, s32[16384]{0:T(1024)S(1)} %iota.11), dimensions={0}, to_apply=%region_0.1 | sort | flops 229376 | bytes 262144 | tf_op jit(solution)/shard_map/sort | solution.py:646
  59.0 9.3 %near_forward.1 = (f32[512,256]{1,0:T(8,128)}, f32[16,128]{1,0:T(8,128)}) custom-call(s32[5,64]{1,0:T(8,128)S(1)} %stack.2.meta_ref, s32[64,256]{1,0:T(8,128)S(1)} %pad_add_fusion.every_ref, s32[64,256]{1,0:T(8,128)S(1)} %reshape.135.keys_ref, bf16[2560,128]{1,0:T(8,128)(2,1)S(1)} %copy-done.6), custom_call_target="tpu_custom_call" | custom-call | tf_op jit(solution)/shard_map/near_forward/pallas_call | solution.py:278
  68.3 12.3 %all-to-all-done.1 = bf16[128,64,128]{2,1,0:T(8,128)(2,1)S(1)} async-done(((bf16[128,64,128]{2,1,0:T(8,128)(2,1)}), bf16[128,64,128]{2,1,0:T(8,128)(2,1)S(1)}, u32[]{:S(2)}, u32[]{:S(2)}) %all-to-all-start.1) | async-done | bytes 2097184 | tf_op jit(solution)/shard_map/all_to_all | solution.py:613
  80.6 3.4 %far_forward.1.mine_ref = f32[512,256]{1,0:T(8,128)S(1)} custom-call(s32[5,64]{1,0:T(8,128)S(1)} %stack.2.meta_ref, s32[64,256]{1,0:T(8,128)S(1)} %reshape.135.keys_ref, bf16[8192,128]{1,0:T(8,128)(2,1)S(1)} %bitcast.23, f32[512,256]{1,0:T(8,128)} %get-tuple-element.35.base_hbm), custom_call_target="tpu_custom_call" | custom-call | tf_op jit(solution)/shard_map/far_forward/pallas_call | solution.py:309
  84.0 5.2 %collective-permute-start.7 = (f32[512,256]{1,0:T(8,128)S(1)}, f32[512,256]{1,0:T(8,128)S(1)}, u32[]{:S(2)}, u32[]{:S(2)}) collective-permute-start(f32[512,256]{1,0:T(8,128)S(1)} %far_forward.1.mine_ref), channel_id=1, source_target_pairs={{0,1},{1,0},{2,3},{3,2},{4,5},{5,4},{6,7},{7,6},{8,9},{9,8},{10,11... | collective-permute-start | bytes 1572872 | tf_op jit(solution)/shard_map/ppermute | solution.py:664
  90.7 2.5 %dense_part.1 = (bf16[1024,128]{1,0:T(8,128)(2,1)}, bf16[512,256]{1,0:T(8,128)(2,1)S(1)}, bf16[1024,128]{1,0:T(8,128)(2,1)S(1)}, f32[192,128]{1,0:T(8,128)}) custom-call(s32[1]{0:T(128)} %bitcast.half_ref, f32[512,256]{1,0:T(8,128)S(1)} %far_forward.1.mine_ref, f32[512,256]{1,0:T(8,128)S(1)} %collective-permute-done.7.other_ref, ...), custom_call_target="tpu_custom_call" | custom-call | tf_op jit(solution)/shard_map/dense_part/pallas_call | solution.py:374
  93.2 3.8 %all-to-all-start.2 = ((f32[8,24,128]{2,1,0:T(8,128)}), f32[8,24,128]{2,1,0:T(8,128)S(1)}, u32[]{:S(2)}, u32[]{:S(2)}) async-start(f32[8,24,128]{2,1,0:T(8,128)} %bitcast.12), calls=%async_computation.2 | async-start | bytes 196608 | tf_op jit(solution)/shard_map/all_to_all | solution.py:548
  97.0 5.9 %far_backward.1 = bf16[8192,128]{1,0:T(8,128)(2,1)} custom-call(s32[5,64]{1,0:T(8,128)S(1)} %stack.2.meta_ref, s32[64,256]{1,0:T(8,128)S(1)} %reshape.135.keys_ref, bf16[512,256]{1,0:T(8,128)(2,1)S(1)} %get-tuple-element.39.grad_ref), custom_call_target="tpu_custom_call" | custom-call | tf_op jit(solution)/shard_map/far_backward/pallas_call | solution.py:414
  105.1 10.6 %all-to-all-start.3 = ((bf16[128,64,128]{2,1,0:T(8,128)(2,1)}), bf16[128,64,128]{2,1,0:T(8,128)(2,1)S(1)}, u32[]{:S(2)}, u32[]{:S(2)}) async-start(bf16[128,64,128]{2,1,0:T(8,128)(2,1)} %bitcast.25), calls=%async_computation.3 | async-start | bytes 4194304 | tf_op jit(solution)/shard_map/all_to_all | solution.py:680
  117.5 5.1 %near_backward.1.near_ref = f32[2560,128]{1,0:T(8,128)S(1)} custom-call(s32[1]{0:T(128)} %bitcast.half_ref, s32[5,64]{1,0:T(8,128)S(1)} %stack.2.meta_ref, s32[64,256]{1,0:T(8,128)S(1)} %reshape.135.keys_ref, bf16[512,256]{1,0:T(8,128)(2,1)S(1)} %copy-done.4, bf16[1024,128]{1,0:T(8,128)(2,1)S(1)} %copy-done.8, bf16[128,128]{1,0:T(8,128)(2,1)S(1)} %copy-done.9), custom_call_target="tpu_custom_call" | custom-call | tf_op jit(solution)/shard_map/near_backward/pallas_call | solution.py:449
  127.4 3.5 %collective-permute-start.10 = (bf16[584,128]{1,0:T(8,128)(2,1)S(1)}, bf16[584,128]{1,0:T(8,128)(2,1)S(1)}, u32[]{:S(2)}, u32[]{:S(2)}) collective-permute-start(bf16[584,128]{1,0:T(8,128)(2,1)S(1)} %get-tuple-element.76), channel_id=1, source_target_pairs={{0,4},{2,6},{4,0},{6,2},{8,12},{10,14},{12,8},{14,10},{16,20},{18,... | collective-permute-start | bytes 448520 | tf_op jit(solution)/shard_map/ppermute | solution.py:561
  132.6 10.2 %collective-permute-done.10 = bf16[584,128]{1,0:T(8,128)(2,1)S(1)} collective-permute-done((bf16[584,128]{1,0:T(8,128)(2,1)S(1)}, bf16[584,128]{1,0:T(8,128)(2,1)S(1)}, u32[]{:S(2)}, u32[]{:S(2)}) %collective-permute-start.10) | collective-permute-done | bytes 149536 | tf_op jit(solution)/shard_map/ppermute | solution.py:561
  143.1 3.4 %collective-permute-start.14 = (f32[152,128]{1,0:T(8,128)S(1)}, f32[152,128]{1,0:T(8,128)S(1)}, u32[]{:S(2)}, u32[]{:S(2)}) collective-permute-start(f32[152,128]{1,0:T(8,128)S(1)} %get-tuple-element.78), channel_id=1, source_target_pairs={{0,192},{2,194},{4,196},{6,198},{8,200},{10,202},{12,204},{14,206}... | collective-permute-start | bytes 233480 | tf_op jit(solution)/shard_map/ppermute | solution.py:561
  152.9 2.6 %collective-permute-start.15 = (f32[152,128]{1,0:T(8,128)S(1)}, f32[152,128]{1,0:T(8,128)}, u32[]{:S(2)}, u32[]{:S(2)}) collective-permute-start(f32[152,128]{1,0:T(8,128)S(1)} %fusion.3), channel_id=1, source_target_pairs={{0,1},{1,0},{2,3},{3,2},{4,5},{5,4},{6,7},{7,6},{8,9},{9,8},{10,11... | collective-permute-start | bytes 233480 | tf_op jit(solution)/shard_map/ppermute | solution.py:702
  158.3 6.6 %all-to-all-done.3.back_ref = bf16[128,64,128]{2,1,0:T(8,128)(2,1)S(1)} async-done(((bf16[128,64,128]{2,1,0:T(8,128)(2,1)}), bf16[128,64,128]{2,1,0:T(8,128)(2,1)S(1)}, u32[]{:S(2)}, u32[]{:S(2)}) %all-to-all-start.3) | async-done | bytes 2097184 | tf_op jit(solution)/shard_map/all_to_all | solution.py:680
  164.9 6.5 %all-to-all-start.4 = ((f32[8,80,128]{2,1,0:T(8,128)}), f32[8,80,128]{2,1,0:T(8,128)}, u32[]{:S(2)}, u32[]{:S(2)}) async-start(f32[8,80,128]{2,1,0:T(8,128)} %pad_maximum_fusion), calls=%async_computation.4 | async-start | bytes 655360 | tf_op jit(solution)/shard_map/all_to_all | solution.py:548
  171.4 4.2 %returned_sum.1.mine_ref = f32[1024,128]{1,0:T(8,128)} custom-call(s32[1]{0:T(128)} %bitcast.half_ref, s32[64,128]{1,0:T(8,128)S(1)} %get-tuple-element.38.idx_ref, bf16[128,64,128]{2,1,0:T(8,128)(2,1)S(1)} %all-to-all-done.3.back_ref, f32[2560,128]{1,0:T(8,128)S(1)} %near_backward.1.near_ref), custom_call_target="tpu_custom_call" | custom-call | tf_op jit(solution)/shard_map/returned_sum/pallas_call | solution.py:485
  179.0 3.6 %all-to-all-done.4.both_ref = f32[8,80,128]{2,1,0:T(8,128)} async-done(((f32[8,80,128]{2,1,0:T(8,128)}), f32[8,80,128]{2,1,0:T(8,128)}, u32[]{:S(2)}, u32[]{:S(2)}) %all-to-all-start.4) | async-done | bytes 327712 | tf_op jit(solution)/shard_map/all_to_all | solution.py:548
  (107 shorter events, 42.8 us)
Async XLA Ops:
  2.0 15.9 %all-to-all-start = ((bf16[8,16,128]{2,1,0:T(8,128)(2,1)}), bf16[8,16,128]{2,1,0:T(8,128)(2,1)S(1)}, u32[]{:S(2)}, u32[]{:S(2)}) async-start(bf16[8,16,128]{2,1,0:T(8,128)(2,1)} %broadcast_in_dim.38), calls=%async_computation | async-start | bytes 65536 | tf_op jit(solution)/shard_map/all_to_all | solution.py:548
  17.9 14.5 %copy-start.2 = (bf16[1024,128]{1,0:T(8,128)(2,1)S(1)}, bf16[1024,128]{1,0:T(8,128)(2,1)}, u32[]{:S(2)}) copy-start(bf16[1024,128]{1,0:T(8,128)(2,1)} %feat_ref.3) | copy-start | bytes 786436
  17.9 14.5 %copy-start.14 = (s32[1,1,8192]{2,1,0:T(1,128)S(1)}, s32[1,1,8192]{2,1,0:T(1,128)}, u32[]{:S(2)}) copy-start(s32[1,1,8192]{2,1,0:T(1,128)} %param.20) | copy-start | bytes 98308
  17.9 14.5 %copy-start.15 = (s32[1,1,8192]{2,1,0:T(1,128)S(1)}, s32[1,1,8192]{2,1,0:T(1,128)}, u32[]{:S(2)}) copy-start(s32[1,1,8192]{2,1,0:T(1,128)} %param.19) | copy-start | bytes 98308
  17.9 62.8 %all-to-all-start.1 = ((bf16[128,64,128]{2,1,0:T(8,128)(2,1)}), bf16[128,64,128]{2,1,0:T(8,128)(2,1)S(1)}, u32[]{:S(2)}, u32[]{:S(2)}) async-start(bf16[128,64,128]{2,1,0:T(8,128)(2,1)} %get-tuple-element.30), calls=%async_computation.1 | async-start | bytes 4194304 | tf_op jit(solution)/shard_map/all_to_all | solution.py:613
  32.6 13.3 %collective-permute-start = (s32[8192]{0:T(1024)S(1)}, s32[8192]{0:T(1024)S(1)}, u32[]{:S(2)}, u32[]{:S(2)}) collective-permute-start(s32[8192]{0:T(1024)S(1)} %fusion.11), channel_id=1, source_target_pairs={{0,1},{1,0},{2,3},{3,2},{4,5},{5,4},{6,7},{7,6},{8,9},{9,8},{10,11... | collective-permute-start | bytes 98312 | tf_op jit(solution)/shard_map/ppermute | solution.py:643
  34.2 7.8 %collective-permute-start.3 = (bf16[128,128]{1,0:T(8,128)(2,1)S(1)}, bf16[128,128]{1,0:T(8,128)(2,1)S(1)}, u32[]{:S(2)}, u32[]{:S(2)}) collective-permute-start(bf16[128,128]{1,0:T(8,128)(2,1)S(1)} %bitcast.28), channel_id=1, source_target_pairs={{0,192},{2,194},{4,196},{6,198},{8,200},{10,202},{12,204},{14,206}... | collective-permute-start | bytes 98312 | tf_op jit(solution)/shard_map/ppermute | solution.py:561
  36.8 4.6 %collective-permute-start.2 = (bf16[128,128]{1,0:T(8,128)(2,1)S(1)}, bf16[128,128]{1,0:T(8,128)(2,1)S(1)}, u32[]{:S(2)}, u32[]{:S(2)}) collective-permute-start(bf16[128,128]{1,0:T(8,128)(2,1)S(1)} %bitcast.29), channel_id=1, source_target_pairs={{0,128},{2,130},{4,132},{6,134},{8,136},{10,138},{12,140},{14,142}... | collective-permute-start | bytes 98312 | tf_op jit(solution)/shard_map/ppermute | solution.py:561
  37.0 3.6 %collective-permute-start.1 = (bf16[128,128]{1,0:T(8,128)(2,1)S(1)}, bf16[128,128]{1,0:T(8,128)(2,1)S(1)}, u32[]{:S(2)}, u32[]{:S(2)}) collective-permute-start(bf16[128,128]{1,0:T(8,128)(2,1)S(1)} %bitcast.30), channel_id=1, source_target_pairs={{0,64},{2,66},{4,68},{6,70},{8,72},{10,74},{12,76},{14,78},{16,80}... | collective-permute-start | bytes 98312 | tf_op jit(solution)/shard_map/ppermute | solution.py:561
  42.7 14.3 %collective-permute-start.6 = (bf16[512,128]{1,0:T(8,128)(2,1)}, bf16[512,128]{1,0:T(8,128)(2,1)S(1)}, u32[]{:S(2)}, u32[]{:S(2)}) collective-permute-start(bf16[512,128]{1,0:T(8,128)(2,1)} %get-tuple-element.66), channel_id=1, source_target_pairs={{0,6},{2,4},{4,2},{6,0},{8,14},{10,12},{12,10},{14,8},{16,22},{18,... | collective-permute-start | bytes 393224 | tf_op jit(solution)/shard_map/ppermute | solution.py:561
  45.1 11.9 %collective-permute-start.5 = (bf16[512,128]{1,0:T(8,128)(2,1)}, bf16[512,128]{1,0:T(8,128)(2,1)S(1)}, u32[]{:S(2)}, u32[]{:S(2)}) collective-permute-start(bf16[512,128]{1,0:T(8,128)(2,1)} %get-tuple-element.66), channel_id=1, source_target_pairs={{0,4},{2,6},{4,0},{6,2},{8,12},{10,14},{12,8},{14,10},{16,20},{18,... | collective-permute-start | bytes 393224 | tf_op jit(solution)/shard_map/ppermute | solution.py:561
  45.8 11.1 %collective-permute-start.4 = (bf16[512,128]{1,0:T(8,128)(2,1)}, bf16[512,128]{1,0:T(8,128)(2,1)S(1)}, u32[]{:S(2)}, u32[]{:S(2)}) collective-permute-start(bf16[512,128]{1,0:T(8,128)(2,1)} %get-tuple-element.66), channel_id=1, source_target_pairs={{0,2},{2,0},{4,6},{6,4},{8,10},{10,8},{12,14},{14,12},{16,18},{18,... | collective-permute-start | bytes 393224 | tf_op jit(solution)/shard_map/ppermute | solution.py:561
  84.0 6.7 %collective-permute-start.7 = (f32[512,256]{1,0:T(8,128)S(1)}, f32[512,256]{1,0:T(8,128)S(1)}, u32[]{:S(2)}, u32[]{:S(2)}) collective-permute-start(f32[512,256]{1,0:T(8,128)S(1)} %far_forward.1.mine_ref), channel_id=1, source_target_pairs={{0,1},{1,0},{2,3},{3,2},{4,5},{5,4},{6,7},{7,6},{8,9},{9,8},{10,11... | collective-permute-start | bytes 1572872 | tf_op jit(solution)/shard_map/ppermute | solution.py:664
  93.2 11.2 %all-to-all-start.2 = ((f32[8,24,128]{2,1,0:T(8,128)}), f32[8,24,128]{2,1,0:T(8,128)S(1)}, u32[]{:S(2)}, u32[]{:S(2)}) async-start(f32[8,24,128]{2,1,0:T(8,128)} %bitcast.12), calls=%async_computation.2 | async-start | bytes 196608 | tf_op jit(solution)/shard_map/all_to_all | solution.py:548
  105.1 59.8 %all-to-all-start.3 = ((bf16[128,64,128]{2,1,0:T(8,128)(2,1)}), bf16[128,64,128]{2,1,0:T(8,128)(2,1)S(1)}, u32[]{:S(2)}, u32[]{:S(2)}) async-start(bf16[128,64,128]{2,1,0:T(8,128)(2,1)} %bitcast.25), calls=%async_computation.3 | async-start | bytes 4194304 | tf_op jit(solution)/shard_map/all_to_all | solution.py:680
  125.7 6.9 %collective-permute-start.9 = (bf16[584,128]{1,0:T(8,128)(2,1)S(1)}, bf16[584,128]{1,0:T(8,128)(2,1)S(1)}, u32[]{:S(2)}, u32[]{:S(2)}) collective-permute-start(bf16[584,128]{1,0:T(8,128)(2,1)S(1)} %get-tuple-element.75), channel_id=1, source_target_pairs={{0,2},{2,0},{4,6},{6,4},{8,10},{10,8},{12,14},{14,12},{16,18},{18,... | collective-permute-start | bytes 448520 | tf_op jit(solution)/shard_map/ppermute | solution.py:561
  127.4 15.4 %collective-permute-start.10 = (bf16[584,128]{1,0:T(8,128)(2,1)S(1)}, bf16[584,128]{1,0:T(8,128)(2,1)S(1)}, u32[]{:S(2)}, u32[]{:S(2)}) collective-permute-start(bf16[584,128]{1,0:T(8,128)(2,1)S(1)} %get-tuple-element.76), channel_id=1, source_target_pairs={{0,4},{2,6},{4,0},{6,2},{8,12},{10,14},{12,8},{14,10},{16,20},{18,... | collective-permute-start | bytes 448520 | tf_op jit(solution)/shard_map/ppermute | solution.py:561
  130.9 12.0 %collective-permute-start.11 = (bf16[584,128]{1,0:T(8,128)(2,1)S(1)}, bf16[584,128]{1,0:T(8,128)(2,1)S(1)}, u32[]{:S(2)}, u32[]{:S(2)}) collective-permute-start(bf16[584,128]{1,0:T(8,128)(2,1)S(1)} %get-tuple-element.77), channel_id=1, source_target_pairs={{0,6},{2,4},{4,2},{6,0},{8,14},{10,12},{12,10},{14,8},{16,22},{18,... | collective-permute-start | bytes 448520 | tf_op jit(solution)/shard_map/ppermute | solution.py:561
  143.1 6.1 %collective-permute-start.14 = (f32[152,128]{1,0:T(8,128)S(1)}, f32[152,128]{1,0:T(8,128)S(1)}, u32[]{:S(2)}, u32[]{:S(2)}) collective-permute-start(f32[152,128]{1,0:T(8,128)S(1)} %get-tuple-element.78), channel_id=1, source_target_pairs={{0,192},{2,194},{4,196},{6,198},{8,200},{10,202},{12,204},{14,206}... | collective-permute-start | bytes 233480 | tf_op jit(solution)/shard_map/ppermute | solution.py:561
  146.5 4.7 %collective-permute-start.12 = (f32[152,128]{1,0:T(8,128)S(1)}, f32[152,128]{1,0:T(8,128)S(1)}, u32[]{:S(2)}, u32[]{:S(2)}) collective-permute-start(f32[152,128]{1,0:T(8,128)S(1)} %get-tuple-element.79), channel_id=1, source_target_pairs={{0,64},{2,66},{4,68},{6,70},{8,72},{10,74},{12,76},{14,78},{16,80}... | collective-permute-start | bytes 233480 | tf_op jit(solution)/shard_map/ppermute | solution.py:561
  146.5 6.4 %collective-permute-start.13 = (f32[152,128]{1,0:T(8,128)S(1)}, f32[152,128]{1,0:T(8,128)S(1)}, u32[]{:S(2)}, u32[]{:S(2)}) collective-permute-start(f32[152,128]{1,0:T(8,128)S(1)} %get-tuple-element.80), channel_id=1, source_target_pairs={{0,128},{2,130},{4,132},{6,134},{8,136},{10,138},{12,140},{14,142}... | collective-permute-start | bytes 233480 | tf_op jit(solution)/shard_map/ppermute | solution.py:561
  152.9 3.7 %collective-permute-start.15 = (f32[152,128]{1,0:T(8,128)S(1)}, f32[152,128]{1,0:T(8,128)}, u32[]{:S(2)}, u32[]{:S(2)}) collective-permute-start(f32[152,128]{1,0:T(8,128)S(1)} %fusion.3), channel_id=1, source_target_pairs={{0,1},{1,0},{2,3},{3,2},{4,5},{5,4},{6,7},{7,6},{8,9},{9,8},{10,11... | collective-permute-start | bytes 233480 | tf_op jit(solution)/shard_map/ppermute | solution.py:702
  164.9 17.8 %all-to-all-start.4 = ((f32[8,80,128]{2,1,0:T(8,128)}), f32[8,80,128]{2,1,0:T(8,128)}, u32[]{:S(2)}, u32[]{:S(2)}) async-start(f32[8,80,128]{2,1,0:T(8,128)} %pad_maximum_fusion), calls=%async_computation.4 | async-start | bytes 655360 | tf_op jit(solution)/shard_map/all_to_all | solution.py:548
  175.7 3.4 %collective-permute-start.8 = (f32[1024,128]{1,0:T(8,128)}, f32[1024,128]{1,0:T(8,128)S(1)}, u32[]{:S(2)}, u32[]{:S(2)}) collective-permute-start(f32[1024,128]{1,0:T(8,128)} %returned_sum.1.mine_ref), channel_id=1, source_target_pairs={{0,1},{1,0},{2,3},{3,2},{4,5},{5,4},{6,7},{7,6},{8,9},{9,8},{10,11... | collective-permute-start | bytes 1572872 | tf_op jit(solution)/shard_map/ppermute | solution.py:716
  (13 other events, 45.0 us)

commit v6 on v5

--- a/solution.py
+++ b/solution.py
@@ -15,7 +15,8 @@
 SMEM = pltpu.SMEM
 SWAP = [(0, 1), (1, 0)]
 CHUNK = 256
-UNROLL = 4
+UNROLL = 6
+DEGREE_LINES = 8
 DST_BITS = 10
 PAD = 1 << 30
 DEAD = 1 << 26
@@ -151,7 +152,7 @@
         scratch_shapes=[VMEM((nodes // 2, 2 * width), BF16), VMEM(rows.shape, jnp.int32)],
         compiler_params=params(),
         name="outgoing_rows",
-    )(flip, count, rows, feats)
+    )(flip, in_hbm(count), in_hbm(rows), in_hbm(feats))
 
 
 def relative(row, base, start, window):
@@ -251,7 +252,7 @@
     sum_ref[...] = jnp.zeros_like(sum_ref)
 
     def degrees(c, _):
-        key = join([every_ref[pl.ds(c * UNROLL + u, 1), :] for u in range(UNROLL)])
+        key = join([every_ref[pl.ds(c * DEGREE_LINES + u, 1), :] for u in range(DEGREE_LINES)])
         dst = key & (nodes - 1)
         high = jnp.where(key < DEAD, dst >> 7, deg_ref.shape[0])
         deg_ref[...] += dot_nt(
@@ -259,7 +260,7 @@
         )
         return 0
 
-    lax.fori_loop(0, every_ref.shape[0] // UNROLL, degrees, 0)
+    lax.fori_loop(0, every_ref.shape[0] // DEGREE_LINES, degrees, 0)
     end = pl.cdiv(meta_ref[COUNTS, 0], CHUNK)
     over_chunks(
         0,
@@ -497,37 +498,33 @@
     )(half, idx, back, near)
 
 
-def finish_kernel(
-    hubs, mine_ref, other_ref, both_ref, feats_ref, hubs_ref, self_ref, neigh_ref, bias_ref
-):
-    width = mine_ref.shape[1]
+def finish_kernel(hubs, both_ref, hubs_ref, self_ref, neigh_ref, bias_ref):
+    width = both_ref.shape[2]
     places = both_ref.shape[0]
     share = (both_ref.shape[1] - hubs) // 2
-    feats_ref[...] = mine_ref[...] + other_ref[...]
     hubs_ref[...] = pair_sum([both_ref[j, :hubs, :] for j in range(places)])
     for row in range(0, width, 8):
         j, at = row // share, hubs + row % share
         self_ref[row : row + 8, :] = both_ref[j, at : at + 8, :]
         neigh_ref[row : row + 8, :] = both_ref[j, at + share : at + share + 8, :]
     at = hubs + width % share
-    bias_ref[...] = both_ref[width // share, at : at + 8, :]
-
-
-def finish(mine, other, both, hubs):
-    nodes, width = mine.shape
+    bias_ref[...] = both_ref[width // share, at : at + 1, :]
+
+
+def finish(both, hubs):
+    width = both.shape[2]
     outs = [
         jax.ShapeDtypeStruct(shape, F32)
-        for shape in ((nodes, width), (hubs, width), (width, width), (width, width), (8, width))
+        for shape in ((hubs, width), (width, width), (width, width), (1, width))
     ]
     return pl.pallas_call(
         functools.partial(finish_kernel, hubs),
-        grid=(1,),
-        in_specs=[whole(x) for x in (mine, other, both)],
-        out_specs=[whole(x) for x in outs],
+        in_specs=[vspec()],
+        out_specs=[vspec()] * 4,
         out_shape=outs,
         compiler_params=params(),
         name="finish",
-    )(in_hbm(mine), in_hbm(other), in_hbm(both))
+    )(both)
 
 
 def torus_of(size):
@@ -602,8 +599,7 @@
     hub_rows = num_dom * half_hubs
     near_rows, far_rows = own_rows + hub_rows, num_dom * slots
 
-    hub_half = lax.dynamic_slice_in_dim(hub_feats, half * half_hubs, half_hubs, 0)
-    hub_z = exchange(jnp.broadcast_to(hub_half[None], (zs,) + hub_half.shape), Z_AXIS, num_dom)
+    hub_z = exchange(jnp.broadcast_to(hub_feats[None], (zs,) + hub_feats.shape), Z_AXIS, num_dom)
 
     me = lax.axis_index("dom")
     counts_row = jnp.pad(send_count, ((0, 0), (0, -num_dom % 128)))
@@ -611,7 +607,8 @@
     out_rows, idx = outgoing(flip, counts_row, send_rows[0], node_feats)
     out_rows, hub_z = lax.optimization_barrier((out_rows, hub_z))
     table = lax.all_to_all(out_rows, "dom", split_axis=0, concat_axis=0, tiled=True)
-    hub_z = after(hub_z.reshape(zs * half_hubs, width), out_rows)
+    hub_z = lax.dynamic_slice_in_dim(hub_z, half * half_hubs, half_hubs, 1)
+    hub_z = hub_z.reshape(zs * half_hubs, width)
     hub_x = jnp.concatenate(swap_blocks([hub_z] * xs, X_AXIS, num_dom))
     hub_y = jnp.concatenate(swap_blocks([hub_x] * ys, Y_AXIS, num_dom))
     own_half = lax.dynamic_slice_in_dim(node_feats, half * own_rows, own_rows, 0)
@@ -714,8 +711,9 @@
     both = exchange(after(both, back), Z_AXIS, num_dom)
     part = returned_sum(half_scalar, idx, back, near_grads, nodes)
     part_other = lax.ppermute(part, "edge", SWAP)
-    grad_feats, grad_hubs, grad_self, grad_neigh, grad_bias = finish(part, part_other, both, hubs)
-    return (layer_out, grad_feats, grad_hubs, grad_self, grad_neigh, grad_bias[0])
+    grad_hubs, grad_self, grad_neigh, grad_bias = finish(both, hubs)
+    grad_feats = part + after(part_other, grad_hubs)
+    return (layer_out, grad_feats, grad_hubs, grad_self, grad_neigh, grad_bias.reshape(width))
 
 
 def solution(mesh):

time: 187 us -> 185 us (0.989)
  waiting for transfers between devices: 49.2 us -> 54.8 us
  local copies, waits for them, and re-layouts: 12.6 us -> 7.69 us
  starting transfers between devices: 71.4 us -> 67 us
  other arithmetic: 13.9 us -> 15.8 us
    unnamed x39 -> x30, local copies, waits for them, and re-layouts: 9.54 us -> 5.06 us
    all_to_all x1, waiting for transfers between devices: 12.3 us -> 16.5 us  [body(): lax.all_to_all(out_rows, 'dom', split_axis=0, concat_axis=0, tiled=True)]
    all_to_all x3, waiting for transfers between devices: 5.52 us -> 8.49 us  [exchange(): lax.all_to_all(blocks, 'dom', 0, 0, axis_index_groups=groups_of(size, axi...]
    ppermute x12, starting transfers between devices: 16.6 us -> 14.7 us  [swap_blocks(): lax.ppermute(block, 'dom', pairs)]
    add x0 -> x1, other arithmetic: none -> 1.89 us  [body(): grad_feats = part + after(part_other, grad_hubs)]
  transfers between devices with their start and end apart: 21 -> 21, of which waited for: 16 -> 13; matrix products, arithmetic and copies ran while one was open for 10% -> 10% of each run, Pallas kernels for 15% -> 17%
where the time goes in v6:
time: 185 us; the launch traced here: 184 us
  starting transfers between devices  67 us (36%)
  waiting for transfers between devices  54.8 us (30%)
  Pallas kernels  37.1 us (20%)
  other arithmetic  15.8 us (9%)
  local copies, waits for them, and re-layouts  7.69 us (4%)
    ppermute x12, waiting for transfers between devices, swap_blocks(): lax.ppermute(block, 'dom', pairs)  21 us
    all_to_all x3, starting transfers between devices, exchange(): lax.all_to_all(blocks, 'dom', 0, 0, axis_index_groups=groups_of(size, axi...  19.7 us
    all_to_all x1, waiting for transfers between devices, body(): lax.all_to_all(out_rows, 'dom', split_axis=0, concat_axis=0, tiled=True)  16.5 us
    ppermute x12, starting transfers between devices, swap_blocks(): lax.ppermute(block, 'dom', pairs)  14.7 us
    all_to_all x1, starting transfers between devices, body(): lax.all_to_all(out_rows, 'dom', split_axis=0, concat_axis=0, tiled=True)  12 us
    all_to_all x1, starting transfers between devices, body(): lax.all_to_all(row_grads.reshape(num_dom, slots, width), 'dom', split_axi...  9.78 us
    all_to_all x3, waiting for transfers between devices, exchange(): lax.all_to_all(blocks, 'dom', 0, 0, axis_index_groups=groups_of(size, axi...  8.49 us
    pallas_call x1, Pallas kernels, near_forward(): pl.pallas_call(functools.partial(near_forward_kernel, min(window, table.s...  8.32 us
  transfers between devices with their start and end apart: 21, of which 13 were waited for; matrix products, arithmetic and copies ran while one was open for 10% of the time, Pallas kernels for 17%

profile of v6, /device:TPU:1, one launch (start us, length us, event | category | flops | bytes accessed | tf_op | source)
XLA Modules:
  0.0 184.1 jit_solution(11296098979583139071)
XLA Ops:
  2.0 9.0 %all-to-all-start = ((bf16[8,32,128]{2,1,0:T(8,128)(2,1)}), bf16[8,32,128]{2,1,0:T(8,128)(2,1)S(1)}, u32[]{:S(2)}, u32[]{:S(2)}) async-start(bf16[8,32,128]{2,1,0:T(8,128)(2,1)} %broadcast_in_dim.38), calls=%async_computation | async-start | bytes 131072 | tf_op jit(solution)/shard_map/all_to_all | solution.py:545
  11.0 5.1 %outgoing_rows.1 = (bf16[128,64,128]{2,1,0:T(8,128)(2,1)}, s32[64,128]{1,0:T(8,128)S(1)}) custom-call(s32[1]{0:T(128)} %bitcast.4.flip_ref, s32[1,128]{1,0:T(1,128)} %count_ref.1, s32[128,128]{1,0:T(8,128)} %bitcast.31, bf16[1024,128]{1,0:T(8,128)(2,1)} %feat_ref.3), custom_call_target="tpu_custom_call" | custom-call | tf_op jit(solution)/shard_map/outgoing_rows/pallas_call | solution.py:135
  18.2 12.0 %all-to-all-start.1 = ((bf16[128,64,128]{2,1,0:T(8,128)(2,1)}), bf16[128,64,128]{2,1,0:T(8,128)(2,1)S(1)}, u32[]{:S(2)}, u32[]{:S(2)}) async-start(bf16[128,64,128]{2,1,0:T(8,128)(2,1)} %get-tuple-element.29), calls=%async_computation.1 | async-start | bytes 4194304 | tf_op jit(solution)/shard_map/all_to_all | solution.py:609
  31.2 2.4 %collective-permute-start.3 = (bf16[128,128]{1,0:T(8,128)(2,1)S(1)}, bf16[128,128]{1,0:T(8,128)(2,1)S(1)}, u32[]{:S(2)}, u32[]{:S(2)}) collective-permute-start(bf16[128,128]{1,0:T(8,128)(2,1)S(1)} %bitcast.24), channel_id=1, source_target_pairs={{0,192},{2,194},{4,196},{6,198},{8,200},{10,202},{12,204},{14,206}... | collective-permute-start | bytes 98312 | tf_op jit(solution)/shard_map/ppermute | solution.py:558
  38.2 2.8 %collective-permute-start.6 = (bf16[512,128]{1,0:T(8,128)(2,1)S(1)}, bf16[512,128]{1,0:T(8,128)(2,1)S(1)}, u32[]{:S(2)}, u32[]{:S(2)}) collective-permute-start(bf16[512,128]{1,0:T(8,128)(2,1)S(1)} %pad_maximum_fusion.17), channel_id=1, source_target_pairs={{0,6},{2,4},{4,2},{6,0},{8,14},{10,12},{12,10},{14,8},{16,22},{18,... | collective-permute-start | bytes 393224 | tf_op jit(solution)/shard_map/ppermute | solution.py:558
  41.8 7.7 %sort.14 = (s32[16384]{0:T(1024)S(1)}, s32[16384]{0:T(1024)}) sort(s32[16384]{0:T(1024)S(1)} %and_select_fusion, s32[16384]{0:T(1024)S(1)} %iota.11), dimensions={0}, to_apply=%region_0.1 | sort | flops 229376 | bytes 262144 | tf_op jit(solution)/shard_map/sort | solution.py:643
  54.4 8.3 %near_forward.1 = (f32[512,256]{1,0:T(8,128)}, f32[16,128]{1,0:T(8,128)}) custom-call(s32[5,64]{1,0:T(8,128)S(1)} %stack.2.meta_ref, s32[64,256]{1,0:T(8,128)S(1)} %pad_add_fusion.every_ref, s32[64,256]{1,0:T(8,128)S(1)} %reshape.138.keys_ref, bf16[2560,128]{1,0:T(8,128)(2,1)S(1)} %constant_dynamic-update-slice_fusion.1.table_ref), custom_call_target="tpu_custom_call" | custom-call | tf_op jit(solution)/shard_map/near_forward/pallas_call | solution.py:279
  62.7 16.5 %all-to-all-done.1 = bf16[128,64,128]{2,1,0:T(8,128)(2,1)S(1)} async-done(((bf16[128,64,128]{2,1,0:T(8,128)(2,1)}), bf16[128,64,128]{2,1,0:T(8,128)(2,1)S(1)}, u32[]{:S(2)}, u32[]{:S(2)}) %all-to-all-start.1) | async-done | bytes 2097184 | tf_op jit(solution)/shard_map/all_to_all | solution.py:609
  79.2 3.8 %far_forward.1.mine_ref = f32[512,256]{1,0:T(8,128)S(1)} custom-call(s32[5,64]{1,0:T(8,128)S(1)} %stack.2.meta_ref, s32[64,256]{1,0:T(8,128)S(1)} %reshape.138.keys_ref, bf16[8192,128]{1,0:T(8,128)(2,1)S(1)} %bitcast.22, f32[512,256]{1,0:T(8,128)} %get-tuple-element.33.base_hbm), custom_call_target="tpu_custom_call" | custom-call | tf_op jit(solution)/shard_map/far_forward/pallas_call | solution.py:310
  83.1 4.5 %collective-permute-start.7 = (f32[512,256]{1,0:T(8,128)S(1)}, f32[512,256]{1,0:T(8,128)S(1)}, u32[]{:S(2)}, u32[]{:S(2)}) collective-permute-start(f32[512,256]{1,0:T(8,128)S(1)} %far_forward.1.mine_ref), channel_id=1, source_target_pairs={{0,1},{1,0},{2,3},{3,2},{4,5},{5,4},{6,7},{7,6},{8,9},{9,8},{10,11... | collective-permute-start | bytes 1572872 | tf_op jit(solution)/shard_map/ppermute | solution.py:661
  89.1 2.5 %dense_part.1 = (bf16[1024,128]{1,0:T(8,128)(2,1)}, bf16[512,256]{1,0:T(8,128)(2,1)S(1)}, bf16[1024,128]{1,0:T(8,128)(2,1)S(1)}, f32[192,128]{1,0:T(8,128)}) custom-call(s32[1]{0:T(128)} %bitcast.half_ref, f32[512,256]{1,0:T(8,128)S(1)} %far_forward.1.mine_ref, f32[512,256]{1,0:T(8,128)S(1)} %collective-permute-done.7.other_ref, ...), custom_call_target="tpu_custom_call" | custom-call | tf_op jit(solution)/shard_map/dense_part/pallas_call | solution.py:375
  91.6 4.0 %all-to-all-start.2 = ((f32[8,24,128]{2,1,0:T(8,128)}), f32[8,24,128]{2,1,0:T(8,128)S(1)}, u32[]{:S(2)}, u32[]{:S(2)}) async-start(f32[8,24,128]{2,1,0:T(8,128)} %bitcast.12), calls=%async_computation.2 | async-start | bytes 196608 | tf_op jit(solution)/shard_map/all_to_all | solution.py:545
  95.6 6.4 %far_backward.1 = bf16[8192,128]{1,0:T(8,128)(2,1)} custom-call(s32[5,64]{1,0:T(8,128)S(1)} %stack.2.meta_ref, s32[64,256]{1,0:T(8,128)S(1)} %reshape.138.keys_ref, bf16[512,256]{1,0:T(8,128)(2,1)S(1)} %get-tuple-element.37.grad_ref), custom_call_target="tpu_custom_call" | custom-call | tf_op jit(solution)/shard_map/far_backward/pallas_call | solution.py:415
  103.7 9.8 %all-to-all-start.3 = ((bf16[128,64,128]{2,1,0:T(8,128)(2,1)}), bf16[128,64,128]{2,1,0:T(8,128)(2,1)S(1)}, u32[]{:S(2)}, u32[]{:S(2)}) async-start(bf16[128,64,128]{2,1,0:T(8,128)(2,1)} %bitcast.23), calls=%async_computation.3 | async-start | bytes 4194304 | tf_op jit(solution)/shard_map/all_to_all | solution.py:677
  115.4 5.1 %near_backward.1.near_ref = f32[2560,128]{1,0:T(8,128)S(1)} custom-call(s32[1]{0:T(128)} %bitcast.half_ref, s32[5,64]{1,0:T(8,128)S(1)} %stack.2.meta_ref, s32[64,256]{1,0:T(8,128)S(1)} %reshape.138.keys_ref, bf16[512,256]{1,0:T(8,128)(2,1)S(1)} %copy-done.1, bf16[1024,128]{1,0:T(8,128)(2,1)S(1)} %copy-done.3, bf16[128,128]{1,0:T(8,128)(2,1)S(1)} %copy-done.4), custom_call_target="tpu_custom_call" | custom-call | tf_op jit(solution)/shard_map/near_backward/pallas_call | solution.py:450
  124.2 3.0 %collective-permute-start.10 = (bf16[584,128]{1,0:T(8,128)(2,1)S(1)}, bf16[584,128]{1,0:T(8,128)(2,1)S(1)}, u32[]{:S(2)}, u32[]{:S(2)}) collective-permute-start(bf16[584,128]{1,0:T(8,128)(2,1)S(1)} %get-tuple-element.66), channel_id=1, source_target_pairs={{0,4},{2,6},{4,0},{6,2},{8,12},{10,14},{12,8},{14,10},{16,20},{18,... | collective-permute-start | bytes 448520 | tf_op jit(solution)/shard_map/ppermute | solution.py:558
  127.5 2.4 %collective-permute-done.9 = bf16[584,128]{1,0:T(8,128)(2,1)S(1)} collective-permute-done((bf16[584,128]{1,0:T(8,128)(2,1)S(1)}, bf16[584,128]{1,0:T(8,128)(2,1)S(1)}, u32[]{:S(2)}, u32[]{:S(2)}) %collective-permute-start.9) | collective-permute-done | bytes 149536 | tf_op jit(solution)/shard_map/ppermute | solution.py:558
  130.0 7.2 %collective-permute-done.10 = bf16[584,128]{1,0:T(8,128)(2,1)S(1)} collective-permute-done((bf16[584,128]{1,0:T(8,128)(2,1)S(1)}, bf16[584,128]{1,0:T(8,128)(2,1)S(1)}, u32[]{:S(2)}, u32[]{:S(2)}) %collective-permute-start.10) | collective-permute-done | bytes 149536 | tf_op jit(solution)/shard_map/ppermute | solution.py:558
  137.2 5.3 %collective-permute-done.11 = bf16[584,128]{1,0:T(8,128)(2,1)S(1)} collective-permute-done((bf16[584,128]{1,0:T(8,128)(2,1)S(1)}, bf16[584,128]{1,0:T(8,128)(2,1)S(1)}, u32[]{:S(2)}, u32[]{:S(2)}) %collective-permute-start.11) | collective-permute-done | bytes 149536 | tf_op jit(solution)/shard_map/ppermute | solution.py:558
  148.4 3.1 %collective-permute-done.13 = f32[152,128]{1,0:T(8,128)S(1)} collective-permute-done((f32[152,128]{1,0:T(8,128)S(1)}, f32[152,128]{1,0:T(8,128)S(1)}, u32[]{:S(2)}, u32[]{:S(2)}) %collective-permute-start.13) | collective-permute-done | bytes 77856 | tf_op jit(solution)/shard_map/ppermute | solution.py:558
  156.5 6.2 %all-to-all-done.3.back_ref = bf16[128,64,128]{2,1,0:T(8,128)(2,1)S(1)} async-done(((bf16[128,64,128]{2,1,0:T(8,128)(2,1)}), bf16[128,64,128]{2,1,0:T(8,128)(2,1)S(1)}, u32[]{:S(2)}, u32[]{:S(2)}) %all-to-all-start.3) | async-done | bytes 2097184 | tf_op jit(solution)/shard_map/all_to_all | solution.py:677
  162.7 6.6 %all-to-all-start.4 = ((f32[8,80,128]{2,1,0:T(8,128)}), f32[8,80,128]{2,1,0:T(8,128)}, u32[]{:S(2)}, u32[]{:S(2)}) async-start(f32[8,80,128]{2,1,0:T(8,128)} %pad_maximum_fusion), calls=%async_computation.4 | async-start | bytes 655360 | tf_op jit(solution)/shard_map/all_to_all | solution.py:545
  169.3 4.2 %returned_sum.1 = f32[1024,128]{1,0:T(8,128)} custom-call(s32[1]{0:T(128)} %bitcast.half_ref, s32[64,128]{1,0:T(8,128)S(1)} %get-tuple-element.36.idx_ref, bf16[128,64,128]{2,1,0:T(8,128)(2,1)S(1)} %all-to-all-done.3.back_ref, f32[2560,128]{1,0:T(8,128)S(1)} %near_backward.1.near_ref), custom_call_target="tpu_custom_call" | custom-call | tf_op jit(solution)/shard_map/returned_sum/pallas_call | solution.py:486
  175.2 5.4 %all-to-all-done.4.both_ref = f32[8,80,128]{2,1,0:T(8,128)} async-done(((f32[8,80,128]{2,1,0:T(8,128)}), f32[8,80,128]{2,1,0:T(8,128)}, u32[]{:S(2)}, u32[]{:S(2)}) %all-to-all-start.4) | async-done | bytes 327712 | tf_op jit(solution)/shard_map/all_to_all | solution.py:545
  (98 shorter events, 38.8 us)
Async XLA Ops:
  2.0 16.3 %all-to-all-start = ((bf16[8,32,128]{2,1,0:T(8,128)(2,1)}), bf16[8,32,128]{2,1,0:T(8,128)(2,1)S(1)}, u32[]{:S(2)}, u32[]{:S(2)}) async-start(bf16[8,32,128]{2,1,0:T(8,128)(2,1)} %broadcast_in_dim.38), calls=%async_computation | async-start | bytes 131072 | tf_op jit(solution)/shard_map/all_to_all | solution.py:545
  18.2 12.7 %copy-start.5 = (bf16[1024,128]{1,0:T(8,128)(2,1)S(1)}, bf16[1024,128]{1,0:T(8,128)(2,1)}, u32[]{:S(2)}) copy-start(bf16[1024,128]{1,0:T(8,128)(2,1)} %feat_ref.3) | copy-start | bytes 786436
  18.2 12.7 %copy-start.9 = (s32[1,1,8192]{2,1,0:T(1,128)S(1)}, s32[1,1,8192]{2,1,0:T(1,128)}, u32[]{:S(2)}) copy-start(s32[1,1,8192]{2,1,0:T(1,128)} %param.20) | copy-start | bytes 98308
  18.2 12.7 %copy-start.10 = (s32[1,1,8192]{2,1,0:T(1,128)S(1)}, s32[1,1,8192]{2,1,0:T(1,128)}, u32[]{:S(2)}) copy-start(s32[1,1,8192]{2,1,0:T(1,128)} %param.19) | copy-start | bytes 98308
  18.2 61.0 %all-to-all-start.1 = ((bf16[128,64,128]{2,1,0:T(8,128)(2,1)}), bf16[128,64,128]{2,1,0:T(8,128)(2,1)S(1)}, u32[]{:S(2)}, u32[]{:S(2)}) async-start(bf16[128,64,128]{2,1,0:T(8,128)(2,1)} %get-tuple-element.29), calls=%async_computation.1 | async-start | bytes 4194304 | tf_op jit(solution)/shard_map/all_to_all | solution.py:609
  31.2 5.7 %collective-permute-start.3 = (bf16[128,128]{1,0:T(8,128)(2,1)S(1)}, bf16[128,128]{1,0:T(8,128)(2,1)S(1)}, u32[]{:S(2)}, u32[]{:S(2)}) collective-permute-start(bf16[128,128]{1,0:T(8,128)(2,1)S(1)} %bitcast.24), channel_id=1, source_target_pairs={{0,192},{2,194},{4,196},{6,198},{8,200},{10,202},{12,204},{14,206}... | collective-permute-start | bytes 98312 | tf_op jit(solution)/shard_map/ppermute | solution.py:558
  33.6 4.6 %collective-permute-start.2 = (bf16[128,128]{1,0:T(8,128)(2,1)S(1)}, bf16[128,128]{1,0:T(8,128)(2,1)S(1)}, u32[]{:S(2)}, u32[]{:S(2)}) collective-permute-start(bf16[128,128]{1,0:T(8,128)(2,1)S(1)} %bitcast.25), channel_id=1, source_target_pairs={{0,128},{2,130},{4,132},{6,134},{8,136},{10,138},{12,140},{14,142}... | collective-permute-start | bytes 98312 | tf_op jit(solution)/shard_map/ppermute | solution.py:558
  33.8 4.4 %collective-permute-start.1 = (bf16[128,128]{1,0:T(8,128)(2,1)S(1)}, bf16[128,128]{1,0:T(8,128)(2,1)S(1)}, u32[]{:S(2)}, u32[]{:S(2)}) collective-permute-start(bf16[128,128]{1,0:T(8,128)(2,1)S(1)} %bitcast.26), channel_id=1, source_target_pairs={{0,64},{2,66},{4,68},{6,70},{8,72},{10,74},{12,76},{14,78},{16,80}... | collective-permute-start | bytes 98312 | tf_op jit(solution)/shard_map/ppermute | solution.py:558
  34.5 7.2 %collective-permute-start = (s32[8192]{0:T(1024)S(1)}, s32[8192]{0:T(1024)S(1)}, u32[]{:S(2)}, u32[]{:S(2)}) collective-permute-start(s32[8192]{0:T(1024)S(1)} %fusion.11), channel_id=1, source_target_pairs={{0,1},{1,0},{2,3},{3,2},{4,5},{5,4},{6,7},{7,6},{8,9},{9,8},{10,11... | collective-permute-start | bytes 98312 | tf_op jit(solution)/shard_map/ppermute | solution.py:640
  38.2 16.2 %collective-permute-start.6 = (bf16[512,128]{1,0:T(8,128)(2,1)S(1)}, bf16[512,128]{1,0:T(8,128)(2,1)S(1)}, u32[]{:S(2)}, u32[]{:S(2)}) collective-permute-start(bf16[512,128]{1,0:T(8,128)(2,1)S(1)} %pad_maximum_fusion.17), channel_id=1, source_target_pairs={{0,6},{2,4},{4,2},{6,0},{8,14},{10,12},{12,10},{14,8},{16,22},{18,... | collective-permute-start | bytes 393224 | tf_op jit(solution)/shard_map/ppermute | solution.py:558
  41.0 13.3 %collective-permute-start.5 = (bf16[512,128]{1,0:T(8,128)(2,1)S(1)}, bf16[512,128]{1,0:T(8,128)(2,1)S(1)}, u32[]{:S(2)}, u32[]{:S(2)}) collective-permute-start(bf16[512,128]{1,0:T(8,128)(2,1)S(1)} %pad_maximum_fusion.17), channel_id=1, source_target_pairs={{0,4},{2,6},{4,0},{6,2},{8,12},{10,14},{12,8},{14,10},{16,20},{18,... | collective-permute-start | bytes 393224 | tf_op jit(solution)/shard_map/ppermute | solution.py:558
  41.6 11.8 %collective-permute-start.4 = (bf16[512,128]{1,0:T(8,128)(2,1)S(1)}, bf16[512,128]{1,0:T(8,128)(2,1)}, u32[]{:S(2)}, u32[]{:S(2)}) collective-permute-start(bf16[512,128]{1,0:T(8,128)(2,1)S(1)} %pad_maximum_fusion.17), channel_id=1, source_target_pairs={{0,2},{2,0},{4,6},{6,4},{8,10},{10,8},{12,14},{14,12},{16,18},{18,... | collective-permute-start | bytes 393224 | tf_op jit(solution)/shard_map/ppermute | solution.py:558
  83.1 6.1 %collective-permute-start.7 = (f32[512,256]{1,0:T(8,128)S(1)}, f32[512,256]{1,0:T(8,128)S(1)}, u32[]{:S(2)}, u32[]{:S(2)}) collective-permute-start(f32[512,256]{1,0:T(8,128)S(1)} %far_forward.1.mine_ref), channel_id=1, source_target_pairs={{0,1},{1,0},{2,3},{3,2},{4,5},{5,4},{6,7},{7,6},{8,9},{9,8},{10,11... | collective-permute-start | bytes 1572872 | tf_op jit(solution)/shard_map/ppermute | solution.py:661
  91.6 11.5 %all-to-all-start.2 = ((f32[8,24,128]{2,1,0:T(8,128)}), f32[8,24,128]{2,1,0:T(8,128)S(1)}, u32[]{:S(2)}, u32[]{:S(2)}) async-start(f32[8,24,128]{2,1,0:T(8,128)} %bitcast.12), calls=%async_computation.2 | async-start | bytes 196608 | tf_op jit(solution)/shard_map/all_to_all | solution.py:545
  103.7 59.0 %all-to-all-start.3 = ((bf16[128,64,128]{2,1,0:T(8,128)(2,1)}), bf16[128,64,128]{2,1,0:T(8,128)(2,1)S(1)}, u32[]{:S(2)}, u32[]{:S(2)}) async-start(bf16[128,64,128]{2,1,0:T(8,128)(2,1)} %bitcast.23), calls=%async_computation.3 | async-start | bytes 4194304 | tf_op jit(solution)/shard_map/all_to_all | solution.py:677
  123.6 6.4 %collective-permute-start.9 = (bf16[584,128]{1,0:T(8,128)(2,1)S(1)}, bf16[584,128]{1,0:T(8,128)(2,1)S(1)}, u32[]{:S(2)}, u32[]{:S(2)}) collective-permute-start(bf16[584,128]{1,0:T(8,128)(2,1)S(1)} %get-tuple-element.65), channel_id=1, source_target_pairs={{0,2},{2,0},{4,6},{6,4},{8,10},{10,8},{12,14},{14,12},{16,18},{18,... | collective-permute-start | bytes 448520 | tf_op jit(solution)/shard_map/ppermute | solution.py:558
  124.2 12.9 %collective-permute-start.10 = (bf16[584,128]{1,0:T(8,128)(2,1)S(1)}, bf16[584,128]{1,0:T(8,128)(2,1)S(1)}, u32[]{:S(2)}, u32[]{:S(2)}) collective-permute-start(bf16[584,128]{1,0:T(8,128)(2,1)S(1)} %get-tuple-element.66), channel_id=1, source_target_pairs={{0,4},{2,6},{4,0},{6,2},{8,12},{10,14},{12,8},{14,10},{16,20},{18,... | collective-permute-start | bytes 448520 | tf_op jit(solution)/shard_map/ppermute | solution.py:558
  127.3 15.3 %collective-permute-start.11 = (bf16[584,128]{1,0:T(8,128)(2,1)S(1)}, bf16[584,128]{1,0:T(8,128)(2,1)S(1)}, u32[]{:S(2)}, u32[]{:S(2)}) collective-permute-start(bf16[584,128]{1,0:T(8,128)(2,1)S(1)} %get-tuple-element.67), channel_id=1, source_target_pairs={{0,6},{2,4},{4,2},{6,0},{8,14},{10,12},{12,10},{14,8},{16,22},{18,... | collective-permute-start | bytes 448520 | tf_op jit(solution)/shard_map/ppermute | solution.py:558
  142.7 5.7 %collective-permute-start.14 = (f32[152,128]{1,0:T(8,128)S(1)}, f32[152,128]{1,0:T(8,128)S(1)}, u32[]{:S(2)}, u32[]{:S(2)}) collective-permute-start(f32[152,128]{1,0:T(8,128)S(1)} %get-tuple-element.68), channel_id=1, source_target_pairs={{0,192},{2,194},{4,196},{6,198},{8,200},{10,202},{12,204},{14,206}... | collective-permute-start | bytes 233480 | tf_op jit(solution)/shard_map/ppermute | solution.py:558
  142.8 5.6 %collective-permute-start.12 = (f32[152,128]{1,0:T(8,128)S(1)}, f32[152,128]{1,0:T(8,128)S(1)}, u32[]{:S(2)}, u32[]{:S(2)}) collective-permute-start(f32[152,128]{1,0:T(8,128)S(1)} %get-tuple-element.69), channel_id=1, source_target_pairs={{0,64},{2,66},{4,68},{6,70},{8,72},{10,74},{12,76},{14,78},{16,80}... | collective-permute-start | bytes 233480 | tf_op jit(solution)/shard_map/ppermute | solution.py:558
  144.3 7.2 %collective-permute-start.13 = (f32[152,128]{1,0:T(8,128)S(1)}, f32[152,128]{1,0:T(8,128)S(1)}, u32[]{:S(2)}, u32[]{:S(2)}) collective-permute-start(f32[152,128]{1,0:T(8,128)S(1)} %get-tuple-element.70), channel_id=1, source_target_pairs={{0,128},{2,130},{4,132},{6,134},{8,136},{10,138},{12,140},{14,142}... | collective-permute-start | bytes 233480 | tf_op jit(solution)/shard_map/ppermute | solution.py:558
  151.5 3.3 %collective-permute-start.15 = (f32[152,128]{1,0:T(8,128)S(1)}, f32[152,128]{1,0:T(8,128)}, u32[]{:S(2)}, u32[]{:S(2)}) collective-permute-start(f32[152,128]{1,0:T(8,128)S(1)} %fusion.3), channel_id=1, source_target_pairs={{0,1},{1,0},{2,3},{3,2},{4,5},{5,4},{6,7},{7,6},{8,9},{9,8},{10,11... | collective-permute-start | bytes 233480 | tf_op jit(solution)/shard_map/ppermute | solution.py:699
  162.7 17.9 %all-to-all-start.4 = ((f32[8,80,128]{2,1,0:T(8,128)}), f32[8,80,128]{2,1,0:T(8,128)}, u32[]{:S(2)}, u32[]{:S(2)}) async-start(f32[8,80,128]{2,1,0:T(8,128)} %pad_maximum_fusion), calls=%async_computation.4 | async-start | bytes 655360 | tf_op jit(solution)/shard_map/all_to_all | solution.py:545
  173.5 8.7 %collective-permute-start.8 = (f32[1024,128]{1,0:T(8,128)}, f32[1024,128]{1,0:T(8,128)S(1)}, u32[]{:S(2)}, u32[]{:S(2)}) collective-permute-start(f32[1024,128]{1,0:T(8,128)} %returned_sum.1), channel_id=1, source_target_pairs={{0,1},{1,0},{2,3},{3,2},{4,5},{5,4},{6,7},{7,6},{8,9},{9,8},{10,11... | collective-permute-start | bytes 1572872 | tf_op jit(solution)/shard_map/ppermute | solution.py:713
  (8 other events, 43.1 us)

commit v7 on v6

--- a/solution.py
+++ b/solution.py
@@ -411,7 +411,7 @@
 
 def far_backward(meta, keys, grad_sum, offset, rows, window=1280):
     width = grad_sum.shape[1] // 2
-    block = min(2048, rows)
+    block = min(4096, rows)
     return pl.pallas_call(
         functools.partial(far_backward_kernel, offset, min(window, rows)),
         grid=(rows // block,),
@@ -458,9 +458,7 @@
     )(half, meta, keys, grad_sum, grad_pre, w_self)
 
 
-def returned_kernel(
-    peers_step, half_ref, idx_ref, back_ref, near_ref, part_hbm, part_ref, acc_ref, sem
-):
+def returned_kernel(peers_step, half_ref, idx_ref, back_ref, near_ref, part_ref, acc_ref):
     nodes = part_ref.shape[0]
     own_rows = nodes // 2
     peers, slots, width = back_ref.shape
@@ -478,7 +476,6 @@
     part_ref[own_rows:, :] = acc_ref[:, width:]
     own_span = pl.ds(pl.multiple_of(half_ref[0] * own_rows, own_rows), own_rows)
     part_ref[own_span, :] += near_ref[:own_rows, :]
-    copy_now(part_ref, part_hbm, sem)
 
 
 def returned_sum(half, idx, back, near, nodes):
@@ -486,13 +483,9 @@
     return pl.pallas_call(
         functools.partial(returned_kernel, min(32, back.shape[0])),
         in_specs=[sspec(), vspec(), vspec(), vspec()],
-        out_specs=hbm_spec(),
-        out_shape=pltpu.HBM((nodes, width), F32),
-        scratch_shapes=[
-            VMEM((nodes, width), F32),
-            VMEM((nodes // 2, 2 * width), F32),
-            pltpu.SemaphoreType.DMA,
-        ],
+        out_specs=vspec(),
+        out_shape=jax.ShapeDtypeStruct((nodes, width), F32),
+        scratch_shapes=[VMEM((nodes // 2, 2 * width), F32)],
         compiler_params=params(),
         name="returned_sum",
     )(half, idx, back, near)
@@ -711,8 +704,8 @@
     both = exchange(after(both, back), Z_AXIS, num_dom)
     part = returned_sum(half_scalar, idx, back, near_grads, nodes)
     part_other = lax.ppermute(part, "edge", SWAP)
-    grad_hubs, grad_self, grad_neigh, grad_bias = finish(both, hubs)
-    grad_feats = part + after(part_other, grad_hubs)
+    grad_feats = part + part_other
+    grad_hubs, grad_self, grad_neigh, grad_bias = finish(after(both, grad_feats), hubs)
     return (layer_out, grad_feats, grad_hubs, grad_self, grad_neigh, grad_bias.reshape(width))
 
 

time: 185 us -> 184 us (level); the launches traced: 184 us -> 180 us
  waiting for transfers between devices: 54.8 us -> 52.6 us
    all_to_all x3, waiting for transfers between devices: 8.49 us -> 5.64 us  [exchange(): lax.all_to_all(blocks, 'dom', 0, 0, axis_index_groups=groups_of(size, axi...]
  transfers between devices with their start and end apart: 21 -> 21, of which waited for: 13 -> 14; matrix products, arithmetic and copies ran while one was open for 10% -> 10% of each run, Pallas kernels for 17% -> 16%
where the time goes in v7:
time: 184 us; the launch traced here: 180 us
  starting transfers between devices  66.3 us (36%)
  waiting for transfers between devices  52.6 us (29%)
  Pallas kernels  37.1 us (20%)
  other arithmetic  14.8 us (8%)
  local copies, waits for them, and re-layouts  7.69 us (4%)
    ppermute x12, waiting for transfers between devices, swap_blocks(): lax.ppermute(block, 'dom', pairs)  20.5 us
    all_to_all x3, starting transfers between devices, exchange(): lax.all_to_all(blocks, 'dom', 0, 0, axis_index_groups=groups_of(size, axi...  18.6 us
    all_to_all x1, waiting for transfers between devices, body(): lax.all_to_all(out_rows, 'dom', split_axis=0, concat_axis=0, tiled=True)  16.5 us
    ppermute x12, starting transfers between devices, swap_blocks(): lax.ppermute(block, 'dom', pairs)  15.4 us
    all_to_all x1, starting transfers between devices, body(): lax.all_to_all(out_rows, 'dom', split_axis=0, concat_axis=0, tiled=True)  12 us
    all_to_all x1, starting transfers between devices, body(): lax.all_to_all(row_grads.reshape(num_dom, slots, width), 'dom', split_axi...  9.25 us
    pallas_call x1, Pallas kernels, near_forward(): pl.pallas_call(functools.partial(near_forward_kernel, min(window, table.s...  8.32 us
    sort x1, other arithmetic, body(): keys = lax.sort(mine).reshape(-1, CHUNK)  7.75 us
  transfers between devices with their start and end apart: 21, of which 14 were waited for; matrix products, arithmetic and copies ran while one was open for 10% of the time, Pallas kernels for 16%

profile of v7, /device:TPU:1, one launch (start us, length us, event | category | flops | bytes accessed | tf_op | source)
XLA Modules:
  0.0 180.2 jit_solution(6395815148150700778)
XLA Ops:
  2.0 9.0 %all-to-all-start = ((bf16[8,32,128]{2,1,0:T(8,128)(2,1)}), bf16[8,32,128]{2,1,0:T(8,128)(2,1)S(1)}, u32[]{:S(2)}, u32[]{:S(2)}) async-start(bf16[8,32,128]{2,1,0:T(8,128)(2,1)} %broadcast_in_dim.38), calls=%async_computation | async-start | bytes 131072 | tf_op jit(solution)/shard_map/all_to_all | solution.py:538
  11.0 5.1 %outgoing_rows.1 = (bf16[128,64,128]{2,1,0:T(8,128)(2,1)}, s32[64,128]{1,0:T(8,128)S(1)}) custom-call(s32[1]{0:T(128)} %bitcast.4.flip_ref, s32[1,128]{1,0:T(1,128)} %count_ref.1, s32[128,128]{1,0:T(8,128)} %bitcast.31, bf16[1024,128]{1,0:T(8,128)(2,1)} %feat_ref.3), custom_call_target="tpu_custom_call" | custom-call | tf_op jit(solution)/shard_map/outgoing_rows/pallas_call | solution.py:135
  18.2 12.0 %all-to-all-start.1 = ((bf16[128,64,128]{2,1,0:T(8,128)(2,1)}), bf16[128,64,128]{2,1,0:T(8,128)(2,1)S(1)}, u32[]{:S(2)}, u32[]{:S(2)}) async-start(bf16[128,64,128]{2,1,0:T(8,128)(2,1)} %get-tuple-element.29), calls=%async_computation.1 | async-start | bytes 4194304 | tf_op jit(solution)/shard_map/all_to_all | solution.py:602
  31.2 2.4 %collective-permute-start.3 = (bf16[128,128]{1,0:T(8,128)(2,1)S(1)}, bf16[128,128]{1,0:T(8,128)(2,1)S(1)}, u32[]{:S(2)}, u32[]{:S(2)}) collective-permute-start(bf16[128,128]{1,0:T(8,128)(2,1)S(1)} %bitcast.24), channel_id=1, source_target_pairs={{0,192},{2,194},{4,196},{6,198},{8,200},{10,202},{12,204},{14,206}... | collective-permute-start | bytes 98312 | tf_op jit(solution)/shard_map/ppermute | solution.py:551
  34.5 2.4 %collective-permute-start = (s32[8192]{0:T(1024)S(1)}, s32[8192]{0:T(1024)S(1)}, u32[]{:S(2)}, u32[]{:S(2)}) collective-permute-start(s32[8192]{0:T(1024)S(1)} %fusion.11), channel_id=1, source_target_pairs={{0,1},{1,0},{2,3},{3,2},{4,5},{5,4},{6,7},{7,6},{8,9},{9,8},{10,11... | collective-permute-start | bytes 98312 | tf_op jit(solution)/shard_map/ppermute | solution.py:633
  38.2 2.8 %collective-permute-start.6 = (bf16[512,128]{1,0:T(8,128)(2,1)S(1)}, bf16[512,128]{1,0:T(8,128)(2,1)S(1)}, u32[]{:S(2)}, u32[]{:S(2)}) collective-permute-start(bf16[512,128]{1,0:T(8,128)(2,1)S(1)} %pad_maximum_fusion.17), channel_id=1, source_target_pairs={{0,6},{2,4},{4,2},{6,0},{8,14},{10,12},{12,10},{14,8},{16,22},{18,... | collective-permute-start | bytes 393224 | tf_op jit(solution)/shard_map/ppermute | solution.py:551
  41.8 7.7 %sort.14 = (s32[16384]{0:T(1024)S(1)}, s32[16384]{0:T(1024)}) sort(s32[16384]{0:T(1024)S(1)} %and_select_fusion, s32[16384]{0:T(1024)S(1)} %iota.11), dimensions={0}, to_apply=%region_0.1 | sort | flops 229376 | bytes 262144 | tf_op jit(solution)/shard_map/sort | solution.py:636
  54.4 8.3 %near_forward.1 = (f32[512,256]{1,0:T(8,128)}, f32[16,128]{1,0:T(8,128)}) custom-call(s32[5,64]{1,0:T(8,128)S(1)} %stack.2.meta_ref, s32[64,256]{1,0:T(8,128)S(1)} %pad_add_fusion.every_ref, s32[64,256]{1,0:T(8,128)S(1)} %reshape.138.keys_ref, bf16[2560,128]{1,0:T(8,128)(2,1)S(1)} %constant_dynamic-update-slice_fusion.1.table_ref), custom_call_target="tpu_custom_call" | custom-call | tf_op jit(solution)/shard_map/near_forward/pallas_call | solution.py:279
  62.7 16.5 %all-to-all-done.1 = bf16[128,64,128]{2,1,0:T(8,128)(2,1)S(1)} async-done(((bf16[128,64,128]{2,1,0:T(8,128)(2,1)}), bf16[128,64,128]{2,1,0:T(8,128)(2,1)S(1)}, u32[]{:S(2)}, u32[]{:S(2)}) %all-to-all-start.1) | async-done | bytes 2097184 | tf_op jit(solution)/shard_map/all_to_all | solution.py:602
  79.2 4.5 %far_forward.1.mine_ref = f32[512,256]{1,0:T(8,128)S(1)} custom-call(s32[5,64]{1,0:T(8,128)S(1)} %stack.2.meta_ref, s32[64,256]{1,0:T(8,128)S(1)} %reshape.138.keys_ref, bf16[8192,128]{1,0:T(8,128)(2,1)S(1)} %bitcast.22, f32[512,256]{1,0:T(8,128)} %get-tuple-element.33.base_hbm), custom_call_target="tpu_custom_call" | custom-call | tf_op jit(solution)/shard_map/far_forward/pallas_call | solution.py:310
  83.7 4.2 %collective-permute-start.7 = (f32[512,256]{1,0:T(8,128)S(1)}, f32[512,256]{1,0:T(8,128)S(1)}, u32[]{:S(2)}, u32[]{:S(2)}) collective-permute-start(f32[512,256]{1,0:T(8,128)S(1)} %far_forward.1.mine_ref), channel_id=1, source_target_pairs={{0,1},{1,0},{2,3},{3,2},{4,5},{5,4},{6,7},{7,6},{8,9},{9,8},{10,11... | collective-permute-start | bytes 1572872 | tf_op jit(solution)/shard_map/ppermute | solution.py:654
  89.4 2.5 %dense_part.1 = (bf16[1024,128]{1,0:T(8,128)(2,1)}, bf16[512,256]{1,0:T(8,128)(2,1)S(1)}, bf16[1024,128]{1,0:T(8,128)(2,1)S(1)}, f32[192,128]{1,0:T(8,128)}) custom-call(s32[1]{0:T(128)} %bitcast.half_ref, f32[512,256]{1,0:T(8,128)S(1)} %far_forward.1.mine_ref, f32[512,256]{1,0:T(8,128)S(1)} %collective-permute-done.7.other_ref, ...), custom_call_target="tpu_custom_call" | custom-call | tf_op jit(solution)/shard_map/dense_part/pallas_call | solution.py:375
  91.9 3.4 %all-to-all-start.2 = ((f32[8,24,128]{2,1,0:T(8,128)}), f32[8,24,128]{2,1,0:T(8,128)S(1)}, u32[]{:S(2)}, u32[]{:S(2)}) async-start(f32[8,24,128]{2,1,0:T(8,128)} %bitcast.12), calls=%async_computation.2 | async-start | bytes 196608 | tf_op jit(solution)/shard_map/all_to_all | solution.py:538
  95.4 6.6 %far_backward.1 = bf16[8192,128]{1,0:T(8,128)(2,1)} custom-call(s32[5,64]{1,0:T(8,128)S(1)} %stack.2.meta_ref, s32[64,256]{1,0:T(8,128)S(1)} %reshape.138.keys_ref, bf16[512,256]{1,0:T(8,128)(2,1)S(1)} %get-tuple-element.37.grad_ref), custom_call_target="tpu_custom_call" | custom-call | tf_op jit(solution)/shard_map/far_backward/pallas_call | solution.py:415
  103.4 9.2 %all-to-all-start.3 = ((bf16[128,64,128]{2,1,0:T(8,128)(2,1)}), bf16[128,64,128]{2,1,0:T(8,128)(2,1)S(1)}, u32[]{:S(2)}, u32[]{:S(2)}) async-start(bf16[128,64,128]{2,1,0:T(8,128)(2,1)} %bitcast.23), calls=%async_computation.3 | async-start | bytes 4194304 | tf_op jit(solution)/shard_map/all_to_all | solution.py:670
  114.6 5.1 %near_backward.1.near_ref = f32[2560,128]{1,0:T(8,128)S(1)} custom-call(s32[1]{0:T(128)} %bitcast.half_ref, s32[5,64]{1,0:T(8,128)S(1)} %stack.2.meta_ref, s32[64,256]{1,0:T(8,128)S(1)} %reshape.138.keys_ref, bf16[512,256]{1,0:T(8,128)(2,1)S(1)} %copy-done.1, bf16[1024,128]{1,0:T(8,128)(2,1)S(1)} %copy-done.3, bf16[128,128]{1,0:T(8,128)(2,1)S(1)} %copy-done.4), custom_call_target="tpu_custom_call" | custom-call | tf_op jit(solution)/shard_map/near_backward/pallas_call | solution.py:450
  129.1 7.2 %collective-permute-done.10 = bf16[584,128]{1,0:T(8,128)(2,1)S(1)} collective-permute-done((bf16[584,128]{1,0:T(8,128)(2,1)S(1)}, bf16[584,128]{1,0:T(8,128)(2,1)S(1)}, u32[]{:S(2)}, u32[]{:S(2)}) %collective-permute-start.10) | collective-permute-done | bytes 149536 | tf_op jit(solution)/shard_map/ppermute | solution.py:551
  136.3 5.0 %collective-permute-done.11 = bf16[584,128]{1,0:T(8,128)(2,1)S(1)} collective-permute-done((bf16[584,128]{1,0:T(8,128)(2,1)S(1)}, bf16[584,128]{1,0:T(8,128)(2,1)S(1)}, u32[]{:S(2)}, u32[]{:S(2)}) %collective-permute-start.11) | collective-permute-done | bytes 149536 | tf_op jit(solution)/shard_map/ppermute | solution.py:551
  147.0 3.7 %collective-permute-done.13 = f32[152,128]{1,0:T(8,128)S(1)} collective-permute-done((f32[152,128]{1,0:T(8,128)S(1)}, f32[152,128]{1,0:T(8,128)S(1)}, u32[]{:S(2)}, u32[]{:S(2)}) %collective-permute-start.13) | collective-permute-done | bytes 77856 | tf_op jit(solution)/shard_map/ppermute | solution.py:551
  150.8 2.3 %collective-permute-start.15 = (f32[152,128]{1,0:T(8,128)S(1)}, f32[152,128]{1,0:T(8,128)}, u32[]{:S(2)}, u32[]{:S(2)}) collective-permute-start(f32[152,128]{1,0:T(8,128)S(1)} %fusion.3), channel_id=1, source_target_pairs={{0,1},{1,0},{2,3},{3,2},{4,5},{5,4},{6,7},{7,6},{8,9},{9,8},{10,11... | collective-permute-start | bytes 233480 | tf_op jit(solution)/shard_map/ppermute | solution.py:692
  155.8 5.9 %all-to-all-done.3.back_ref = bf16[128,64,128]{2,1,0:T(8,128)(2,1)S(1)} async-done(((bf16[128,64,128]{2,1,0:T(8,128)(2,1)}), bf16[128,64,128]{2,1,0:T(8,128)(2,1)S(1)}, u32[]{:S(2)}, u32[]{:S(2)}) %all-to-all-start.3) | async-done | bytes 2097184 | tf_op jit(solution)/shard_map/all_to_all | solution.py:670
  161.7 6.2 %all-to-all-start.4 = ((f32[8,80,128]{2,1,0:T(8,128)}), f32[8,80,128]{2,1,0:T(8,128)}, u32[]{:S(2)}, u32[]{:S(2)}) async-start(f32[8,80,128]{2,1,0:T(8,128)} %pad_maximum_fusion), calls=%async_computation.4 | async-start | bytes 655360 | tf_op jit(solution)/shard_map/all_to_all | solution.py:538
  167.9 3.4 %returned_sum.1 = f32[1024,128]{1,0:T(8,128)S(1)} custom-call(s32[1]{0:T(128)} %bitcast.half_ref, s32[64,128]{1,0:T(8,128)S(1)} %get-tuple-element.36.idx_ref, bf16[128,64,128]{2,1,0:T(8,128)(2,1)S(1)} %all-to-all-done.3.back_ref, f32[2560,128]{1,0:T(8,128)S(1)} %near_backward.1.near_ref), custom_call_target="tpu_custom_call" | custom-call | tf_op jit(solution)/shard_map/returned_sum/pallas_call | solution.py:483
  175.9 2.7 %all-to-all-done.4.both_ref = f32[8,80,128]{2,1,0:T(8,128)} async-done(((f32[8,80,128]{2,1,0:T(8,128)}), f32[8,80,128]{2,1,0:T(8,128)}, u32[]{:S(2)}, u32[]{:S(2)}) %all-to-all-start.4) | async-done | bytes 327712 | tf_op jit(solution)/shard_map/all_to_all | solution.py:538
  (98 shorter events, 40.4 us)
Async XLA Ops:
  2.0 16.3 %all-to-all-start = ((bf16[8,32,128]{2,1,0:T(8,128)(2,1)}), bf16[8,32,128]{2,1,0:T(8,128)(2,1)S(1)}, u32[]{:S(2)}, u32[]{:S(2)}) async-start(bf16[8,32,128]{2,1,0:T(8,128)(2,1)} %broadcast_in_dim.38), calls=%async_computation | async-start | bytes 131072 | tf_op jit(solution)/shard_map/all_to_all | solution.py:538
  18.2 12.7 %copy-start.5 = (bf16[1024,128]{1,0:T(8,128)(2,1)S(1)}, bf16[1024,128]{1,0:T(8,128)(2,1)}, u32[]{:S(2)}) copy-start(bf16[1024,128]{1,0:T(8,128)(2,1)} %feat_ref.3) | copy-start | bytes 786436
  18.2 12.7 %copy-start.9 = (s32[1,1,8192]{2,1,0:T(1,128)S(1)}, s32[1,1,8192]{2,1,0:T(1,128)}, u32[]{:S(2)}) copy-start(s32[1,1,8192]{2,1,0:T(1,128)} %param.20) | copy-start | bytes 98308
  18.2 12.7 %copy-start.10 = (s32[1,1,8192]{2,1,0:T(1,128)S(1)}, s32[1,1,8192]{2,1,0:T(1,128)}, u32[]{:S(2)}) copy-start(s32[1,1,8192]{2,1,0:T(1,128)} %param.19) | copy-start | bytes 98308
  18.2 61.0 %all-to-all-start.1 = ((bf16[128,64,128]{2,1,0:T(8,128)(2,1)}), bf16[128,64,128]{2,1,0:T(8,128)(2,1)S(1)}, u32[]{:S(2)}, u32[]{:S(2)}) async-start(bf16[128,64,128]{2,1,0:T(8,128)(2,1)} %get-tuple-element.29), calls=%async_computation.1 | async-start | bytes 4194304 | tf_op jit(solution)/shard_map/all_to_all | solution.py:602
  31.2 5.7 %collective-permute-start.3 = (bf16[128,128]{1,0:T(8,128)(2,1)S(1)}, bf16[128,128]{1,0:T(8,128)(2,1)S(1)}, u32[]{:S(2)}, u32[]{:S(2)}) collective-permute-start(bf16[128,128]{1,0:T(8,128)(2,1)S(1)} %bitcast.24), channel_id=1, source_target_pairs={{0,192},{2,194},{4,196},{6,198},{8,200},{10,202},{12,204},{14,206}... | collective-permute-start | bytes 98312 | tf_op jit(solution)/shard_map/ppermute | solution.py:551
  33.6 4.6 %collective-permute-start.2 = (bf16[128,128]{1,0:T(8,128)(2,1)S(1)}, bf16[128,128]{1,0:T(8,128)(2,1)S(1)}, u32[]{:S(2)}, u32[]{:S(2)}) collective-permute-start(bf16[128,128]{1,0:T(8,128)(2,1)S(1)} %bitcast.25), channel_id=1, source_target_pairs={{0,128},{2,130},{4,132},{6,134},{8,136},{10,138},{12,140},{14,142}... | collective-permute-start | bytes 98312 | tf_op jit(solution)/shard_map/ppermute | solution.py:551
  33.8 4.4 %collective-permute-start.1 = (bf16[128,128]{1,0:T(8,128)(2,1)S(1)}, bf16[128,128]{1,0:T(8,128)(2,1)S(1)}, u32[]{:S(2)}, u32[]{:S(2)}) collective-permute-start(bf16[128,128]{1,0:T(8,128)(2,1)S(1)} %bitcast.26), channel_id=1, source_target_pairs={{0,64},{2,66},{4,68},{6,70},{8,72},{10,74},{12,76},{14,78},{16,80}... | collective-permute-start | bytes 98312 | tf_op jit(solution)/shard_map/ppermute | solution.py:551
  34.5 7.2 %collective-permute-start = (s32[8192]{0:T(1024)S(1)}, s32[8192]{0:T(1024)S(1)}, u32[]{:S(2)}, u32[]{:S(2)}) collective-permute-start(s32[8192]{0:T(1024)S(1)} %fusion.11), channel_id=1, source_target_pairs={{0,1},{1,0},{2,3},{3,2},{4,5},{5,4},{6,7},{7,6},{8,9},{9,8},{10,11... | collective-permute-start | bytes 98312 | tf_op jit(solution)/shard_map/ppermute | solution.py:633
  38.2 16.2 %collective-permute-start.6 = (bf16[512,128]{1,0:T(8,128)(2,1)S(1)}, bf16[512,128]{1,0:T(8,128)(2,1)S(1)}, u32[]{:S(2)}, u32[]{:S(2)}) collective-permute-start(bf16[512,128]{1,0:T(8,128)(2,1)S(1)} %pad_maximum_fusion.17), channel_id=1, source_target_pairs={{0,6},{2,4},{4,2},{6,0},{8,14},{10,12},{12,10},{14,8},{16,22},{18,... | collective-permute-start | bytes 393224 | tf_op jit(solution)/shard_map/ppermute | solution.py:551
  41.0 13.3 %collective-permute-start.5 = (bf16[512,128]{1,0:T(8,128)(2,1)S(1)}, bf16[512,128]{1,0:T(8,128)(2,1)S(1)}, u32[]{:S(2)}, u32[]{:S(2)}) collective-permute-start(bf16[512,128]{1,0:T(8,128)(2,1)S(1)} %pad_maximum_fusion.17), channel_id=1, source_target_pairs={{0,4},{2,6},{4,0},{6,2},{8,12},{10,14},{12,8},{14,10},{16,20},{18,... | collective-permute-start | bytes 393224 | tf_op jit(solution)/shard_map/ppermute | solution.py:551
  41.6 11.8 %collective-permute-start.4 = (bf16[512,128]{1,0:T(8,128)(2,1)S(1)}, bf16[512,128]{1,0:T(8,128)(2,1)}, u32[]{:S(2)}, u32[]{:S(2)}) collective-permute-start(bf16[512,128]{1,0:T(8,128)(2,1)S(1)} %pad_maximum_fusion.17), channel_id=1, source_target_pairs={{0,2},{2,0},{4,6},{6,4},{8,10},{10,8},{12,14},{14,12},{16,18},{18,... | collective-permute-start | bytes 393224 | tf_op jit(solution)/shard_map/ppermute | solution.py:551
  83.7 5.8 %collective-permute-start.7 = (f32[512,256]{1,0:T(8,128)S(1)}, f32[512,256]{1,0:T(8,128)S(1)}, u32[]{:S(2)}, u32[]{:S(2)}) collective-permute-start(f32[512,256]{1,0:T(8,128)S(1)} %far_forward.1.mine_ref), channel_id=1, source_target_pairs={{0,1},{1,0},{2,3},{3,2},{4,5},{5,4},{6,7},{7,6},{8,9},{9,8},{10,11... | collective-permute-start | bytes 1572872 | tf_op jit(solution)/shard_map/ppermute | solution.py:654
  91.9 10.9 %all-to-all-start.2 = ((f32[8,24,128]{2,1,0:T(8,128)}), f32[8,24,128]{2,1,0:T(8,128)S(1)}, u32[]{:S(2)}, u32[]{:S(2)}) async-start(f32[8,24,128]{2,1,0:T(8,128)} %bitcast.12), calls=%async_computation.2 | async-start | bytes 196608 | tf_op jit(solution)/shard_map/all_to_all | solution.py:538
  103.4 58.3 %all-to-all-start.3 = ((bf16[128,64,128]{2,1,0:T(8,128)(2,1)}), bf16[128,64,128]{2,1,0:T(8,128)(2,1)S(1)}, u32[]{:S(2)}, u32[]{:S(2)}) async-start(bf16[128,64,128]{2,1,0:T(8,128)(2,1)} %bitcast.23), calls=%async_computation.3 | async-start | bytes 4194304 | tf_op jit(solution)/shard_map/all_to_all | solution.py:670
  122.8 6.3 %collective-permute-start.9 = (bf16[584,128]{1,0:T(8,128)(2,1)S(1)}, bf16[584,128]{1,0:T(8,128)(2,1)S(1)}, u32[]{:S(2)}, u32[]{:S(2)}) collective-permute-start(bf16[584,128]{1,0:T(8,128)(2,1)S(1)} %get-tuple-element.65), channel_id=1, source_target_pairs={{0,2},{2,0},{4,6},{6,4},{8,10},{10,8},{12,14},{14,12},{16,18},{18,... | collective-permute-start | bytes 448520 | tf_op jit(solution)/shard_map/ppermute | solution.py:551
  124.8 11.4 %collective-permute-start.10 = (bf16[584,128]{1,0:T(8,128)(2,1)S(1)}, bf16[584,128]{1,0:T(8,128)(2,1)S(1)}, u32[]{:S(2)}, u32[]{:S(2)}) collective-permute-start(bf16[584,128]{1,0:T(8,128)(2,1)S(1)} %get-tuple-element.66), channel_id=1, source_target_pairs={{0,4},{2,6},{4,0},{6,2},{8,12},{10,14},{12,8},{14,10},{16,20},{18,... | collective-permute-start | bytes 448520 | tf_op jit(solution)/shard_map/ppermute | solution.py:551
  126.1 15.2 %collective-permute-start.11 = (bf16[584,128]{1,0:T(8,128)(2,1)S(1)}, bf16[584,128]{1,0:T(8,128)(2,1)S(1)}, u32[]{:S(2)}, u32[]{:S(2)}) collective-permute-start(bf16[584,128]{1,0:T(8,128)(2,1)S(1)} %get-tuple-element.67), channel_id=1, source_target_pairs={{0,6},{2,4},{4,2},{6,0},{8,14},{10,12},{12,10},{14,8},{16,22},{18,... | collective-permute-start | bytes 448520 | tf_op jit(solution)/shard_map/ppermute | solution.py:551
  141.5 5.5 %collective-permute-start.14 = (f32[152,128]{1,0:T(8,128)S(1)}, f32[152,128]{1,0:T(8,128)S(1)}, u32[]{:S(2)}, u32[]{:S(2)}) collective-permute-start(f32[152,128]{1,0:T(8,128)S(1)} %get-tuple-element.68), channel_id=1, source_target_pairs={{0,192},{2,194},{4,196},{6,198},{8,200},{10,202},{12,204},{14,206}... | collective-permute-start | bytes 233480 | tf_op jit(solution)/shard_map/ppermute | solution.py:551
  141.6 5.4 %collective-permute-start.12 = (f32[152,128]{1,0:T(8,128)S(1)}, f32[152,128]{1,0:T(8,128)S(1)}, u32[]{:S(2)}, u32[]{:S(2)}) collective-permute-start(f32[152,128]{1,0:T(8,128)S(1)} %get-tuple-element.69), channel_id=1, source_target_pairs={{0,64},{2,66},{4,68},{6,70},{8,72},{10,74},{12,76},{14,78},{16,80}... | collective-permute-start | bytes 233480 | tf_op jit(solution)/shard_map/ppermute | solution.py:551
  143.5 7.3 %collective-permute-start.13 = (f32[152,128]{1,0:T(8,128)S(1)}, f32[152,128]{1,0:T(8,128)S(1)}, u32[]{:S(2)}, u32[]{:S(2)}) collective-permute-start(f32[152,128]{1,0:T(8,128)S(1)} %get-tuple-element.70), channel_id=1, source_target_pairs={{0,128},{2,130},{4,132},{6,134},{8,136},{10,138},{12,140},{14,142}... | collective-permute-start | bytes 233480 | tf_op jit(solution)/shard_map/ppermute | solution.py:551
  150.8 3.3 %collective-permute-start.15 = (f32[152,128]{1,0:T(8,128)S(1)}, f32[152,128]{1,0:T(8,128)}, u32[]{:S(2)}, u32[]{:S(2)}) collective-permute-start(f32[152,128]{1,0:T(8,128)S(1)} %fusion.3), channel_id=1, source_target_pairs={{0,1},{1,0},{2,3},{3,2},{4,5},{5,4},{6,7},{7,6},{8,9},{9,8},{10,11... | collective-permute-start | bytes 233480 | tf_op jit(solution)/shard_map/ppermute | solution.py:692
  161.7 16.9 %all-to-all-start.4 = ((f32[8,80,128]{2,1,0:T(8,128)}), f32[8,80,128]{2,1,0:T(8,128)}, u32[]{:S(2)}, u32[]{:S(2)}) async-start(f32[8,80,128]{2,1,0:T(8,128)} %pad_maximum_fusion), calls=%async_computation.4 | async-start | bytes 655360 | tf_op jit(solution)/shard_map/all_to_all | solution.py:538
  171.3 3.8 %collective-permute-start.8 = (f32[1024,128]{1,0:T(8,128)S(1)}, f32[1024,128]{1,0:T(8,128)S(1)}, u32[]{:S(2)}, u32[]{:S(2)}) collective-permute-start(f32[1024,128]{1,0:T(8,128)S(1)} %returned_sum.1), channel_id=1, source_target_pairs={{0,1},{1,0},{2,3},{3,2},{4,5},{5,4},{6,7},{7,6},{8,9},{9,8},{10,11... | collective-permute-start | bytes 1572872 | tf_op jit(solution)/shard_map/ppermute | solution.py:706
  (8 other events, 41.4 us)
